TPU v7x, 32 devices: a whole 2x2x4 slice. The times are simulated.
32 devices in a mesh: wide: 8 (over z, x), node: 4 (over y, core).
Axes of the slice: x: 2, y: 2, z: 4, core: 2. Of those that a mesh axis runs over, the one named last changes fastest.
Arguments:
- tokens: bfloat16 [4096, 12288], P(('wide', 'node')), may hold values from -6 to 6
- weight_codes: bfloat16 [12288, 128], P('wide', 'node'), may hold values from -4 to 4
- block_scales: bfloat16 [96, 128], P(None, 'node'), may hold values from 0.0029907227 to 0.029907227
- cotangent: bfloat16 [4096, 128], P(('wide', 'node')), may hold values from -0.09375 to 0.09375
Outputs:
- projected: bfloat16 [4096, 128], P(('wide', 'node'))
- weight_grad: float32 [12288, 128], P('wide', 'node')
All inputs are finite; a program needn't handle non-finite values.
Results may differ from a plain program's by a relative error of at most 0.015.
Values may be sent and summed in bfloat16 or wider, within the bound.
No kernel may reach another device: no remote copies, remote signals or barrier semaphores. Data moves between devices by JAX's collectives and lax.ppermute only.
A program may use at most 64 MiB of HBM per device.

v0:
```python
import jax
import jax.numpy as jnp
from jax import lax
from jax.sharding import PartitionSpec as P

BLOCK = 128


def on_device(tokens, weight_codes, block_scales, cotangent):
    row_codes, row_scales = (
        lax.all_gather(weight_codes, "node", axis=1, tiled=True),
        lax.all_gather(block_scales, "node", axis=1, tiled=True),
    )
    piece = lax.all_gather(row_codes, "wide", axis=0, tiled=True)
    row_index = lax.iota(jnp.int32, piece.shape[0])
    factor = jnp.take(row_scales, row_index // BLOCK, axis=0).astype(jnp.float32)
    dequant = (piece.astype(jnp.float32) * factor).astype(jnp.bfloat16)
    summed = jnp.dot(tokens, dequant, preferred_element_type=jnp.float32)
    projected = summed.astype(jnp.bfloat16)
    partial_value = lax.dot_general(
        tokens, cotangent, (((0,), (0,)), ((), ())), preferred_element_type=jnp.float32
    )
    node_part = lax.psum_scatter(
        partial_value.astype(jnp.bfloat16), "node", scatter_dimension=1, tiled=True
    ).astype(jnp.float32)
    weight_grad = lax.psum_scatter(node_part, "wide", scatter_dimension=0, tiled=True)
    return (projected, weight_grad)


def solution(mesh):
    placed = (
        P(("wide", "node"), None),
        P("wide", "node"),
        P(None, "node"),
        P(("wide", "node"), None),
    )
    return jax.shard_map(
        on_device,
        mesh=mesh,
        in_specs=placed,
        out_specs=(P(("wide", "node"), None), P("wide", "node")),
        check_vma=False,
    )
```

profile of v0, /device:TPU:0, one launch (start us, length us, event | category | flops | bytes accessed | tf_op | source)
XLA Modules:
  0.0 159.3 jit_solution(14781478966564852370)
XLA Ops:
  8.0 0.0 copy-start
  8.0 0.0 reduce-scatter.3.cloned.1.call-start
  8.1 1.8 %copy-done = bf16[128,12288]{1,0:T(8,128)(2,1)S(1)} copy-done((bf16[128,12288]{1,0:T(8,128)(2,1)S(1)}, bf16[128,12288]{1,0:T(8,128)(2,1)}, u32[]{:S(2)}) %copy-start) | copy-done | bytes 3145752
  9.9 3.4 %convolution_convert_fusion = bf16[12288,128]{0,1:T(8,128)(2,1)} fusion(bf16[128,12288]{1,0:T(8,128)(2,1)S(1)} %copy-done, bf16[128,128]{1,0:T(8,128)(2,1)} %param.7), kind=kOutput, calls=%fused_computation.1 | convolution fusion | flops 404226048 | bytes 6324224 | tf_op jit(solution)/shard_map/dot_general | solution.py:20
  13.3 0.0 reduce-scatter.3.cloned.1.call-update
  13.4 0.0 copy-start.1
  13.4 0.0 all-gather.2.cloned.1.call-start
  13.4 8.1 %all_gather.9 = bf16[1536,128]{0,1:T(8,128)(2,1)S(1)} all-gather(bf16[1536,32]{0,1:T(8,128)(2,1)} %param.5), channel_id=1, replica_groups=mesh['wide'=8,'node'=4] {'node'}, dimensions={1}, use_global_device_ids=true | all-gather | bytes 491520 | tf_op jit(solution)/shard_map/all_gather | solution.py:11
  21.6 1.0 copy.12
  22.5 0.0 all-gather.2.cloned.1.call-update
  22.5 0.0 reduce-scatter.5.cloned.1.call-start
  22.6 31.6 %reduce-scatter.3.cloned.1.call-done = bf16[12288,32]{0,1:T(8,128)(2,1)} async-done(((bf16[12288,128]{0,1:T(8,128)(2,1)}), bf16[12288,32]{0,1:T(8,128)(2,1)}) %reduce-scatter.3.cloned.1.call-update) | async-done | bytes 786448 | tf_op jit(solution)/shard_map/reduce_scatter | solution.py:23
  54.2 2.4 %convert_element_type.27 = f32[12288,32]{0,1:T(8,128)} convert(bf16[12288,32]{0,1:T(8,128)(2,1)} %reduce-scatter.3.cloned.1.call-done) | non-fusion elementwise | flops 393216 | bytes 2359296 | tf_op jit(solution)/shard_map/convert_element_type | solution.py:25
  56.6 0.0 reduce-scatter.5.cloned.1.call-update
  56.6 0.0 copy-done.1
  56.6 5.2 %all_gather.11 = bf16[96,128]{0,1:T(8,128)(2,1)S(1)} all-gather(bf16[96,32]{0,1:T(8,128)(2,1)S(1)} %copy-done.1), channel_id=1, replica_groups=mesh['wide'=8,'node'=4] {'node'}, dimensions={1}, use_global_device_ids=true | all-gather | bytes 30720 | tf_op jit(solution)/shard_map/all_gather | solution.py:12
  61.8 0.1 copy.13
  62.0 43.3 %gather_fusion = bf16[12288,128]{1,0:T(8,128)(2,1)} fusion(bf16[96,128]{1,0:T(8,128)(2,1)S(1)} %copy.13, s32[12288]{0:T(1024)S(1)} %broadcast_clamp_fusion), kind=kCustom, calls=%fused_computation | custom fusion | bytes 6340608 | tf_op jit(solution)/shard_map/jit(_take)/gather | solution.py:16
  105.3 0.0 all-gather.2.cloned.1.call-done
  105.3 9.6 %fusion.5 = bf16[128,128]{0,1:T(8,128)(2,1)S(1)} fusion(bf16[128,12288]{1,0:T(8,128)(2,1)S(1)} %copy-done, bf16[12288,128]{1,0:T(8,128)(2,1)} %all-gather.2.cloned.1.call-done, bf16[12288,128]{1,0:T(8,128)(2,1)} %gather_fusion, pred[12288]{0:T(1024)(128)(4,1)S(1)} %fusion.10), kind=kOutput, calls=%fused_computation.8 | convolution fusion | flops 410533888 | bytes 9482240 | tf_op jit(solution)/shard_map/dot_general | solution.py:18
  114.9 0.7 copy.14
  115.6 36.2 %reduce-scatter.5.cloned.1.call-done = f32[1536,32]{0,1:T(8,128)} async-done(((f32[12288,32]{0,1:T(8,128)}), f32[1536,32]{0,1:T(8,128)}) %reduce-scatter.5.cloned.1.call-update) | async-done | bytes 196624 | tf_op jit(solution)/shard_map/reduce_scatter | solution.py:26
  (3 shorter events, 0.1 us)
Async XLA Ops:
  8.0 1.9 %copy-start = (bf16[128,12288]{1,0:T(8,128)(2,1)S(1)}, bf16[128,12288]{1,0:T(8,128)(2,1)}, u32[]{:S(2)}) copy-start(bf16[128,12288]{1,0:T(8,128)(2,1)} %param.4) | copy-start | bytes 9437188
  8.0 46.2 %reduce-scatter.3.cloned.1.call-start = ((), (), s32[]{:S(2)}) async-start(), calls=%async_computation.3 | async-start | bytes 3932160 | tf_op jit(solution)/shard_map/reduce_scatter | solution.py:23
  13.4 43.3 %copy-start.1 = (bf16[96,32]{0,1:T(8,128)(2,1)S(1)}, bf16[96,32]{0,1:T(8,128)(2,1)}, u32[]{:S(2)}) copy-start(bf16[96,32]{0,1:T(8,128)(2,1)} %param.6) | copy-start | bytes 18436
  13.4 91.9 %all-gather.2.cloned.1.call-start = ((), (), s32[]{:S(2)}) async-start(), calls=%async_computation.2 | async-start | bytes 3538944 | tf_op jit(solution)/shard_map/all_gather | solution.py:14
  22.5 129.3 %reduce-scatter.5.cloned.1.call-start = ((), (), s32[]{:S(2)}) async-start(), calls=%async_computation.4 | async-start | bytes 1769472 | tf_op jit(solution)/shard_map/reduce_scatter | solution.py:26
Sparse Core Ops, SparseCore 0:
  13.5 40.6 reduce-scatter.2
Sparse Core Ops, SparseCore 1:
  22.6 61.2 all-gather.1
  88.1 63.7 reduce-scatter.4
where the time goes:
time: 160 us; the launch traced here: 159 us
  waiting for transfers between devices  67.9 us (42%)
  local copies, waits for them, and re-layouts  46.9 us (29%)
  between operations  15.5 us (10%)
  blocking collectives  13.3 us (8%)
  matrix products  13 us (8%)
  other arithmetic  2.45 us (2%)
    gather x1, local copies, waits for them, and re-layouts, on_device(): jnp.take(row_scales, row_index // BLOCK, axis=0).astype(jnp.float32)  43.3 us
    reduce_scatter x1, waiting for transfers between devices, on_device(): lax.psum_scatter(node_part, 'wide', scatter_dimension=0, tiled=True)  36.2 us
    reduce_scatter x1, waiting for transfers between devices, on_device(): lax.psum_scatter(partial_value.astype(jnp.bfloat16), 'node', scatter_dime...  31.6 us
    dot_general x1, matrix products, on_device(): summed = jnp.dot(tokens, dequant, preferred_element_type=jnp.float32)  9.57 us
    all_gather x1, blocking collectives, on_device(): lax.all_gather(weight_codes, 'node', axis=1, tiled=True)  8.15 us
    all_gather x1, blocking collectives, on_device(): lax.all_gather(block_scales, 'node', axis=1, tiled=True)  5.19 us
    dot_general x1, matrix products, on_device(): lax.dot_general(tokens, cotangent, (((0,), (0,)), ((), ())), preferred_el...  3.45 us
  transfers between devices with their start and end apart: 3, of which 2 were waited for; matrix products, arithmetic and copies ran while one was open for 36% of the time, Pallas kernels for 0%

commit v1 on v0

v1 whole, which is shorter than its diff:
```python
import functools

import jax
import jax.numpy as jnp
from jax import lax
from jax.experimental import pallas as pl
from jax.experimental.pallas import tpu as pltpu
from jax.sharding import PartitionSpec as P

BLOCK = 128
F32 = jnp.float32
BF16 = jnp.bfloat16
NT = (((1,), (1,)), ((), ()))
VMEM = pl.BlockSpec(memory_space=pltpu.VMEM)
ANY = pl.BlockSpec(memory_space=pl.ANY)
PARAMS = pltpu.CompilerParams(vmem_limit_bytes=10 << 20)


def place_of(h, x, y, ys):
    return 2 * (ys * x + y) + h


def turn_of(h, x, y, ys):
    if x and y:
        return 0, 2 * (y - 1) + h
    if (x and h) or (y and not h):
        return 0, 2 * (ys - 1) + y
    return 1, (2 + y if x or y else h)


def flip(entries, axis, offset, size):
    return lax.ppermute(entries, axis, [(i, i ^ offset) for i in range(size)])


def columns_of(x, z, cols):
    place = lax.bitwise_xor(lax.axis_index("wide"), 2 * z + x) * cols
    return pl.ds(pl.multiple_of(place, cols), cols)


def first_kernel(ys, zs, tokens, cot, codes, scales, *refs):
    (*made, weight, tokens_v, cot_v, codes_v, scales_v, cot_t, sems) = refs
    rows, cols = codes.shape
    half = cols // 2
    fetched = []

    def fetch(src, dst):
        fetched.append(pltpu.make_async_copy(src, dst, sems.at[len(fetched)]))
        fetched[-1].start()

    for src, dst in ((cot, cot_v), (codes, codes_v), (scales, scales_v)):
        fetch(src, dst)
    order = [(x, z) for x in (1, 0) for z in range(zs)]
    for x, z in order:
        place = columns_of(x, z, cols)
        fetch(tokens.at[:, place], tokens_v.at[:, place])
    for copy in fetched[:3]:
        copy.wait()

    blocks = cols // BLOCK
    first = lax.axis_index("wide") * blocks
    shape = (scales.shape[1], blocks)
    chosen = lax.broadcasted_iota(jnp.int32, shape, 0) == first + lax.broadcasted_iota(jnp.int32, shape, 1)
    factor = jnp.dot(scales_v[...], chosen.astype(F32).astype(BF16), preferred_element_type=F32)
    for b in range(blocks):
        at = b * BLOCK
        piece = (codes_v[:, at : at + BLOCK].astype(F32) * factor[:, b : b + 1]).astype(BF16)
        weight[at // half, :, at % half : at % half + BLOCK] = piece

    cot_t[...] = cot_v[...].astype(F32).T.astype(BF16)
    node = lax.axis_index("node")
    names = [(core, y) for core in (1, 0) for y in range(ys)]
    picked = []
    for core, y in names:
        place = lax.bitwise_xor(node, 2 * y + core) * rows
        picked.append(cot_t[pl.ds(pl.multiple_of(place, rows), rows), :])
    left = jnp.concatenate(picked, axis=0)
    for copy, (x, z) in zip(fetched[3:], order):
        copy.wait()
        right = tokens_v[:, columns_of(x, z, cols)]
        for h in range(2):
            part = jnp.dot(left, right[:, h * half : (h + 1) * half], preferred_element_type=F32).astype(BF16)
            for i, (core, y) in enumerate(names):
                turn, at = turn_of(h, x, y, ys)
                made[2 * (1 - core) + turn][at, z] = part[i * rows : (i + 1) * rows]


def local_products(tokens, cot, codes, scales, ys, zs):
    rows, cols = codes.shape
    half = cols // 2
    operands = (tokens, cot, codes, scales)
    blocks = [jax.ShapeDtypeStruct((n, zs, rows, half), BF16) for n in (3 * ys - 2, ys + 2)]
    return pl.pallas_call(
        functools.partial(first_kernel, ys, zs),
        out_shape=(*blocks, *blocks, jax.ShapeDtypeStruct((2, rows, half), BF16)),
        in_specs=[ANY] * 4,
        out_specs=(VMEM,) * 5,
        scratch_shapes=[pltpu.VMEM(a.shape, BF16) for a in operands]
        + [pltpu.VMEM(cot.shape[::-1], BF16), pltpu.SemaphoreType.DMA((3 + 2 * zs,))],
        compiler_params=PARAMS,
        cost_estimate=pl.CostEstimate(
            flops=2 * tokens.size * cot.shape[1], bytes_accessed=4 * tokens.size, transcendentals=0
        ),
        name="first",
    )(*[pltpu.with_memory_space_constraint(a, pltpu.HBM) for a in operands])


def plain_products(tokens, cot, codes, scales, ys, zs):
    rows, cols = codes.shape
    half = cols // 2
    node, wide = lax.axis_index("node"), lax.axis_index("wide")
    part = jnp.dot(cot.T, tokens, preferred_element_type=F32).astype(BF16)
    part = part.reshape(2 * ys, rows, 2 * zs, 2, half).transpose(3, 0, 2, 1, 4)
    part = jnp.take(part, jnp.arange(2 * ys) ^ node, axis=1)
    part = jnp.take(part, jnp.arange(2 * zs) ^ wide, axis=2)
    part = part.reshape(2, ys, 2, zs, 2, rows, half).transpose(2, 4, 1, 0, 3, 5, 6)
    part = part.reshape(2, 4 * ys, zs, rows, half)
    split = []
    for core in (1, 0):
        named = {turn_of(h, x, y, ys): part[core, place_of(h, x, y, ys)] for h in range(2) for x in range(2) for y in range(ys)}
        for turn, count in enumerate((3 * ys - 2, ys + 2)):
            split.append(jnp.stack([named[turn, i] for i in range(count)]))
    index = (wide * cols + jnp.arange(cols)) // BLOCK
    factor = jnp.take(scales, index, axis=1).astype(F32)
    weight = (codes.astype(F32) * factor).astype(BF16)
    weight = weight.reshape(rows, 2, half).transpose(1, 0, 2)
    return *split, weight


def add_up(outs, arrays, after=(), name="add_up", kind=BF16):
    shapes = [jax.ShapeDtypeStruct(shape, kind) for shape, _ in outs]
    rows, half = arrays[0].shape[-2:]
    if half % BLOCK or rows % 16:
        results = []
        for shape, places in outs:
            result = jnp.zeros(shape, kind)
            for at, terms in places:
                total = sum(arrays[a][i].astype(F32) for a, i in terms)
                result = result.at[at].set(total.astype(kind))
            results.append(result)
        return results

    def kernel(*refs):
        given, made = refs[: len(arrays)], refs[len(arrays) + len(after) :]
        for out, (_, places) in zip(made, outs):
            for at, terms in places:
                terms = [given[a][i] for a, i in terms]
                if len(terms) > 1:
                    terms = [sum(t.astype(F32) for t in terms).astype(kind)]
                out[at] = terms[0]

    return pl.pallas_call(
        kernel,
        out_shape=shapes,
        in_specs=[VMEM] * len(arrays) + [ANY] * len(after),
        out_specs=[VMEM] * len(outs),
        compiler_params=PARAMS,
        name=name,
    )(*arrays, *after)


def finish(sums, arrays, after):
    rows, half = arrays[0].shape[-2:]

    def total(given, h):
        return sum(given[a][i].astype(F32) for a, i in sums[h])

    if half % BLOCK or rows % 16:
        return jnp.concatenate([total(arrays, h) for h in range(2)], axis=1)

    def kernel(*refs):
        for h in range(2):
            refs[-1][:, h * half : (h + 1) * half] = total(refs[:-2], h)

    return pl.pallas_call(
        kernel,
        out_shape=jax.ShapeDtypeStruct((rows, 2 * half), F32),
        in_specs=[VMEM] * len(arrays) + [ANY],
        out_specs=VMEM,
        compiler_params=PARAMS,
        cost_estimate=pl.CostEstimate(flops=4 * 10**10, bytes_accessed=1, transcendentals=0),
        name="finish",
    )(*arrays, after)


def project_kernel(ys, zs, tokens, *refs):
    weights, out, total_t = refs[:4], refs[4], refs[5]
    rows, half = weights[0].shape[2:]
    cols = 2 * half
    most = 2 * ys + 2
    node = lax.axis_index("node")
    total = jnp.zeros((2 * ys * rows, tokens.shape[0]), F32)
    for x in range(2):
        for z in range(zs):
            pieces = tokens[:, columns_of(x, z, cols)]
            for h in range(2):
                picked = []
                for n in range(2 * ys):
                    at = place_of(h, x, n // 2, ys)
                    picked.append(weights[2 * (n % 2) + (at >= most)][at % most, z])
                left = jnp.concatenate(picked, axis=0)
                right = pieces[:, h * half : (h + 1) * half]
                total = total + lax.dot_general(left, right, NT, preferred_element_type=F32)
    total_t[...] = total.reshape(total_t.shape)
    ordered = [total_t[lax.bitwise_xor(node, n)] for n in range(2 * ys)]
    out[...] = jnp.concatenate(ordered, axis=0).T.astype(BF16)


def project(tokens, weights, ys, zs):
    rows = weights[0].shape[2]
    width = 2 * ys * rows
    return pl.pallas_call(
        functools.partial(project_kernel, ys, zs),
        out_shape=jax.ShapeDtypeStruct((tokens.shape[0], width), BF16),
        in_specs=[VMEM] * 5,
        out_specs=VMEM,
        scratch_shapes=[pltpu.VMEM((2 * ys, rows, tokens.shape[0]), F32)],
        compiler_params=PARAMS,
        cost_estimate=pl.CostEstimate(
            flops=2 * tokens.size * width, bytes_accessed=4 * tokens.size, transcendentals=0
        ),
        name="project",
    )(tokens, *weights)


def plain_project(tokens, weights, ys, zs):
    rows, half = weights[0].shape[2:]
    weights = [jnp.concatenate(weights[:2]), jnp.concatenate(weights[2:])]
    node, wide = lax.axis_index("node"), lax.axis_index("wide")
    pieces = tokens.reshape(tokens.shape[0], 2 * zs, 2, half)
    pieces = jnp.take(pieces, jnp.arange(2 * zs) ^ wide, axis=1)
    pieces = pieces.reshape(tokens.shape[0], zs, 2, 2, half)
    total = []
    for n in range(2 * ys):
        part = 0.0
        for h in range(2):
            for x in range(2):
                held = weights[n % 2][place_of(h, x, n // 2, ys)]
                part = part + jnp.einsum("tzl,zrl->tr", pieces[:, :, x, h], held, preferred_element_type=F32)
        total.append(part)
    total = jnp.take(jnp.stack(total, axis=1), jnp.arange(2 * ys) ^ node, axis=1)
    return total.reshape(tokens.shape[0], -1).astype(BF16)


def on_device(wides, nodes, tokens, codes, scales, cotangent):
    ys, zs = nodes // 2, wides // 2
    cols, rows = codes.shape
    half = cols // 2
    aligned = half % BLOCK == 0 and rows % 16 == 0
    products, make_project = (local_products, project) if aligned else (plain_products, plain_project)
    others = range(1, ys)
    one = (zs, rows, half)
    whole = (...,)

    def core_flip(entries):
        return flip(entries, "node", 1, nodes)

    def y_flip(entries, y):
        return flip(entries, "node", 2 * y, nodes)

    def x_flip(entries):
        return flip(entries, "wide", 1, wides)

    def z_flip(entries, z):
        return flip(entries, "wide", 2 * z, wides)

    sent0, sent1, kept0, kept1, weight = products(tokens, cotangent, codes.T, scales.T, ys, zs)

    got0, got1 = core_flip(sent0), core_flip(sent1)
    held = [weight, z_flip(weight, zs // 2)]
    offsets = [0, zs // 2]
    places = [(0, ()), (1, ())]

    def pair(h, x, y):
        _, at = turn_of(h, x, y, ys)
        return [(0, (at,)), (1, (at,))]

    outs = [((ys - 1, *one), [((y - 1,), pair(1, 1, y)) for y in others])]
    outs += [(one, [(whole, pair(0, 1, y))]) for y in others]
    outs += [(one, [(whole, pair(1, 1, 0))])]
    outs += [(one, [(whole, pair(0, 0, y))]) for y in others]
    diag_x, *rest = add_up(outs, [kept0, got0], name="stage1")
    after = [diag_x]
    diag_y, side_x, side_y = rest[: ys - 1], rest[ys - 1], rest[ys:]
    diag_x = x_flip(diag_x)
    diag_y = [y_flip(d, y) for y, d in zip(others, diag_y)]
    side_x = x_flip(side_x)
    side_y = [y_flip(d, y) for y, d in zip(others, side_y)]

    step = zs // 4
    while step:
        outs = [((len(places), 2, rows, half), [((i,), [place]) for i, place in enumerate(places)])]
        (to_z,) = add_up(outs, held, after, name="widen")
        after = [to_z]
        held.append(z_flip(to_z, step))
        places = places + [(len(held) - 1, (i,)) for i in range(len(places))]
        offsets = offsets + [z ^ step for z in offsets]
        step //= 2

    outs = [(one, [(whole, pair(0, 1, 0) + [(2 + y, whole) for y in others])])]
    outs += [(one, [(whole, pair(1, 0, y) + [(2, (y - 1,))])]) for y in others]
    last_x, *last_y = add_up(outs, [kept1, got1, diag_x, *diag_y], after, name="stage2")
    after = last_x
    last_x = x_flip(last_x)
    last_y = [y_flip(d, y) for y, d in zip(others, last_y)]

    sums = [
        pair(0, 0, 0) + [(2 + y, whole) for y in others],
        pair(1, 0, 0) + [(2, whole)],
    ]
    outs = [((2, *one), [((h,), sums[h]) for h in range(2)])]
    (base,) = add_up(outs, [kept1, got1, side_x, *side_y], [after], name="sides", kind=F32)

    outs = [(one, [((z,), [(a, i + (h,))]) for z, (a, i) in zip(offsets, places)]) for h in range(2)]
    own = list(add_up(outs, held, [base], name="own"))
    on_x = [x_flip(own[0])]
    on_y = [[None, y_flip(own[1], y)] for y in others]
    on_x.append(x_flip(own[1]))
    for y in others:
        on_y[y - 1][0] = y_flip(own[0], y)
    diag = [[y_flip(on_x[0], y), x_flip(on_y[y - 1][1])] for y in others]

    arrays = [base, last_x, *last_y]
    plane = [[(0, (0,)), (1, ())], [(0, (1,))] + [(1 + y, ()) for y in others]]
    left = list(range(zs))
    sums = {(z, h): [(a, i + (z,)) for a, i in plane[h]] for z in left for h in range(2)}
    after = [own[0]]
    step = 1
    while step < zs:
        going = [z for z in left if z & step]
        left = [z for z in left if not z & step]
        outs = [((len(going), 2, rows, half), [((i, h), sums[z, h]) for i, z in enumerate(going) for h in range(2)])]
        (to_z,) = add_up(outs, arrays, after, name="plane")
        arrays = [*arrays, z_flip(to_z, step)]
        after = [to_z]
        sums = {(z, h): sums[z, h] + [(len(arrays) - 1, (i, h))] for i, z in enumerate(left) for h in range(2)}
        step *= 2
    weight_grad = finish([sums[0, 0], sums[0, 1]], arrays, tokens)

    held = own + [e for es in on_y for e in es] + on_x
    places = [((i,), [(i, whole)]) for i in range(len(held))]
    (most,) = add_up([((len(held), *one), places)], held, name="most")
    held = [d for ds in diag for d in ds]
    places = [((i,), [(i, whole)]) for i in range(len(held))]
    (last,) = add_up([((len(held), *one), places)], held, [to_z], name="last")
    projected = make_project(tokens, [most, last, core_flip(most), core_flip(last)], ys, zs)
    return projected, weight_grad.T


def solution(mesh):
    placed = (
        P(("wide", "node"), None),
        P("wide", "node"),
        P(None, "node"),
        P(("wide", "node"), None),
    )
    return jax.shard_map(
        functools.partial(on_device, mesh.shape["wide"], mesh.shape["node"]),
        mesh=mesh,
        in_specs=placed,
        out_specs=(P(("wide", "node"), None), P("wide", "node")),
        check_vma=False,
    )
```

time: 160 us -> 41.4 us (0.26)
  waiting for transfers between devices: 67.9 us -> 10.7 us
  local copies, waits for them, and re-layouts: 46.9 us -> 0.01 us
  starting transfers between devices: 0.13 us -> 23.4 us
  between operations: 15.5 us -> 0.73 us
  blocking collectives: 13.3 us -> 0 us
  matrix products: 13 us -> 0 us
  Pallas kernels: 0 us -> 6.43 us
  other arithmetic: 2.45 us -> 0 us
    reduce_scatter x2 -> x0, waiting for transfers between devices: 67.9 us -> none  [the longest x1 36.2 us: on_device(): lax.psum_scatter(node_part, 'wide', scatter_dimension=0, tiled=True)]
    gather x1 -> x0, local copies, waits for them, and re-layouts: 43.3 us -> none  [on_device(): jnp.take(row_scales, row_index // BLOCK, axis=0).astype(jnp.float32)]
    ppermute x0 -> x20, starting transfers between devices: none -> 23.4 us  [flip(): return lax.ppermute(entries, axis, [(i, i ^ offset) for i in range(size)])]
    all_gather x2 -> x0, blocking collectives: 13.3 us -> none  [the longest x1 8.15 us: on_device(): lax.all_gather(weight_codes, 'node', axis=1, tiled=True)]
    dot_general x2 -> x0, matrix products: 13 us -> none  [the longest x1 9.57 us: on_device(): summed = jnp.dot(tokens, dequant, preferred_element_type=jnp.float32)]
    ppermute x0 -> x20, waiting for transfers between devices: none -> 10.7 us  [flip(): return lax.ppermute(entries, axis, [(i, i ^ offset) for i in range(size)])]
    pallas_call x0 -> x12, Pallas kernels: none -> 6.43 us  [the longest x1 3.33 us: local_products(): pl.pallas_call(functools.partial(first_kernel, ys, zs), out_shape=(*block...]
    unnamed x5 -> x2, local copies, waits for them, and re-layouts: 2.57 us -> 0.01 us
  transfers between devices with their start and end apart: 3 -> 20, of which waited for: 2 -> 10; matrix products, arithmetic and copies ran while one was open for 36% -> 0% of each run, Pallas kernels for 0% -> 3%
where the time goes in v1:
time: 41.4 us; the launch traced here: 41.3 us
  starting transfers between devices  23.4 us (57%)
  waiting for transfers between devices  10.7 us (26%)
  Pallas kernels  6.43 us (16%)
  between operations  0.73 us (2%)
    ppermute x20, starting transfers between devices, flip(): return lax.ppermute(entries, axis, [(i, i ^ offset) for i in range(size)])  23.4 us
    ppermute x20, waiting for transfers between devices, flip(): return lax.ppermute(entries, axis, [(i, i ^ offset) for i in range(size)])  10.7 us
    pallas_call x1, Pallas kernels, local_products(): pl.pallas_call(functools.partial(first_kernel, ys, zs), out_shape=(*block...  3.33 us
    pallas_call x1, Pallas kernels, project(): pl.pallas_call(functools.partial(project_kernel, ys, zs), out_shape=jax.S...  1.71 us
  transfers between devices with their start and end apart: 20, of which 10 were waited for; matrix products, arithmetic and copies ran while one was open for 0% of the time, Pallas kernels for 3%

profile of v1, /device:TPU:0, one launch (start us, length us, event | category | flops | bytes accessed | tf_op | source)
XLA Modules:
  0.0 41.3 jit_solution(3988050084263081813)
XLA Ops:
  0.6 3.3 %first.1 = (bf16[4,4,32,768]{3,2,1,0:T(8,128)(2,1)S(1)}, bf16[4,4,32,768]{3,2,1,0:T(8,128)(2,1)S(1)}, bf16[4,4,32,768]{3,2,1,0:T(8,128)(2,1)S(1)}, bf16[4,4,32,7...) custom-call(bf16[128,12288]{1,0:T(8,128)(2,1)} %refs_5_.1, bf16[128,128]{1,0:T(8,128)(2,1)} %cot.1, ...), custom_call_target="tpu_custom_call" | custom-call | flops 402653184 | bytes 6291456 | tf_op jit(solution)/shard_map/first/pallas_call | solution.py:92
  4.0 0.5 %collective-permute-start.1 = (bf16[4,4,32,768]{3,2,1,0:T(8,128)(2,1)S(1)}, bf16[4,4,32,768]{3,2,1,0:T(8,128)(2,1)S(1)}, u32[]{:S(2)}, u32[]{:S(2)}) collective-permute-start(bf16[4,4,32,768]{3,2,1,0:T(8,128)(2,1)S(1)} %get-tuple-element.17), channel_id=1, source_target_pairs={{0,1},{1,0},{2,3},{3,2},{4,5},{5,4},{6,7},{7,6},{8,9},{9,8},{10,11... | collective-permute-start | bytes 2359304 | tf_op jit(solution)/shard_map/ppermute | solution.py:32
  4.5 0.1 collective-permute-start.3
  4.6 4.0 %collective-permute-start = (bf16[2,32,768]{2,1,0:T(8,128)(2,1)S(1)}, bf16[2,32,768]{2,1,0:T(8,128)(2,1)S(1)}, u32[]{:S(2)}, u32[]{:S(2)}) collective-permute-start(bf16[2,32,768]{2,1,0:T(8,128)(2,1)S(1)} %get-tuple-element.15.refs_0_), channel_id=1, source_target_pairs={{0,16},{4,20},{8,24},{12,28},{16,0},{20,4},{24,8},{28,12},{1,17},{... | collective-permute-start | bytes 294920 | tf_op jit(solution)/shard_map/ppermute | solution.py:32
  8.6 0.0 collective-permute-done.1.refs_1_
  8.6 0.2 stage1.1
  8.8 1.6 %collective-permute-start.6 = (bf16[1,4,32,768]{3,2,1,0:T(8,128)(2,1)S(1)}, bf16[1,4,32,768]{3,2,1,0:T(8,128)(2,1)S(1)}, u32[]{:S(2)}, u32[]{:S(2)}) collective-permute-start(bf16[1,4,32,768]{3,2,1,0:T(8,128)(2,1)S(1)} %get-tuple-element.18.refs_2_), channel_id=1, source_target_pairs={{0,4},{4,0},{8,12},{12,8},{16,20},{20,16},{24,28},{28,24},{1,5},{5... | collective-permute-start | bytes 589832 | tf_op jit(solution)/shard_map/ppermute | solution.py:32
  10.3 1.5 %collective-permute-start.7 = (bf16[4,32,768]{2,1,0:T(8,128)(2,1)S(1)}, bf16[4,32,768]{2,1,0:T(8,128)(2,1)S(1)}, u32[]{:S(2)}, u32[]{:S(2)}) collective-permute-start(bf16[4,32,768]{2,1,0:T(8,128)(2,1)S(1)} %get-tuple-element.23), channel_id=1, source_target_pairs={{0,2},{1,3},{2,0},{3,1},{4,6},{5,7},{6,4},{7,5},{8,10},{9,11},{10,... | collective-permute-start | bytes 589832 | tf_op jit(solution)/shard_map/ppermute | solution.py:32
  11.8 0.5 %collective-permute-start.4 = (bf16[4,32,768]{2,1,0:T(8,128)(2,1)S(1)}, bf16[4,32,768]{2,1,0:T(8,128)(2,1)S(1)}, u32[]{:S(2)}, u32[]{:S(2)}) collective-permute-start(bf16[4,32,768]{2,1,0:T(8,128)(2,1)S(1)} %get-tuple-element.21), channel_id=1, source_target_pairs={{0,4},{4,0},{8,12},{12,8},{16,20},{20,16},{24,28},{28,24},{1,5},{5... | collective-permute-start | bytes 589832 | tf_op jit(solution)/shard_map/ppermute | solution.py:32
  12.4 1.3 %collective-permute-done.refs_1_ = bf16[2,32,768]{2,1,0:T(8,128)(2,1)S(1)} collective-permute-done((bf16[2,32,768]{2,1,0:T(8,128)(2,1)S(1)}, bf16[2,32,768]{2,1,0:T(8,128)(2,1)S(1)}, u32[]{:S(2)}, u32[]{:S(2)}) %collective-permute-start) | collective-permute-done | bytes 98336 | tf_op jit(solution)/shard_map/ppermute | solution.py:32
  13.7 1.6 %collective-permute-start.5 = (bf16[4,32,768]{2,1,0:T(8,128)(2,1)S(1)}, bf16[4,32,768]{2,1,0:T(8,128)(2,1)S(1)}, u32[]{:S(2)}, u32[]{:S(2)}) collective-permute-start(bf16[4,32,768]{2,1,0:T(8,128)(2,1)S(1)} %get-tuple-element.22), channel_id=1, source_target_pairs={{0,2},{1,3},{2,0},{3,1},{4,6},{5,7},{6,4},{7,5},{8,10},{9,11},{10,... | collective-permute-start | bytes 589832 | tf_op jit(solution)/shard_map/ppermute | solution.py:32
  15.3 0.0 collective-permute-done.3.refs_1_
  15.3 0.7 %collective-permute-start.2 = (bf16[2,2,32,768]{3,2,1,0:T(8,128)(2,1)S(1)}, bf16[2,2,32,768]{3,2,1,0:T(8,128)(2,1)S(1)}, u32[]{:S(2)}, u32[]{:S(2)}) collective-permute-start(bf16[2,2,32,768]{3,2,1,0:T(8,128)(2,1)S(1)} %widen.1.refs_4_), channel_id=1, source_target_pairs={{0,8},{4,12},{8,0},{12,4},{16,24},{20,28},{24,16},{28,20},{1,9},{5... | collective-permute-start | bytes 589832 | tf_op jit(solution)/shard_map/ppermute | solution.py:32
  16.1 0.6 %collective-permute-done.6.refs_2_ = bf16[1,4,32,768]{3,2,1,0:T(8,128)(2,1)S(1)} collective-permute-done((bf16[1,4,32,768]{3,2,1,0:T(8,128)(2,1)S(1)}, bf16[1,4,32,768]{3,2,1,0:T(8,128)(2,1)S(1)}, u32[]{:S(2)}, u32[]{:S(2)}) %collective-permute-start.6) | collective-permute-done | bytes 196640 | tf_op jit(solution)/shard_map/ppermute | solution.py:32
  16.6 0.7 %collective-permute-done.7.refs_3_ = bf16[4,32,768]{2,1,0:T(8,128)(2,1)S(1)} collective-permute-done((bf16[4,32,768]{2,1,0:T(8,128)(2,1)S(1)}, bf16[4,32,768]{2,1,0:T(8,128)(2,1)S(1)}, u32[]{:S(2)}, u32[]{:S(2)}) %collective-permute-start.7) | collective-permute-done | bytes 196640 | tf_op jit(solution)/shard_map/ppermute | solution.py:32
  17.4 0.1 stage2.1
  17.5 0.8 %collective-permute-start.14 = (bf16[4,32,768]{2,1,0:T(8,128)(2,1)S(1)}, bf16[4,32,768]{2,1,0:T(8,128)(2,1)S(1)}, u32[]{:S(2)}, u32[]{:S(2)}) collective-permute-start(bf16[4,32,768]{2,1,0:T(8,128)(2,1)S(1)} %get-tuple-element.24.refs_4_), channel_id=1, source_target_pairs={{0,4},{4,0},{8,12},{12,8},{16,20},{20,16},{24,28},{28,24},{1,5},{5... | collective-permute-start | bytes 589832 | tf_op jit(solution)/shard_map/ppermute | solution.py:32
  18.3 1.5 %collective-permute-start.15 = (bf16[4,32,768]{2,1,0:T(8,128)(2,1)S(1)}, bf16[4,32,768]{2,1,0:T(8,128)(2,1)S(1)}, u32[]{:S(2)}, u32[]{:S(2)}) collective-permute-start(bf16[4,32,768]{2,1,0:T(8,128)(2,1)S(1)} %get-tuple-element.27), channel_id=1, source_target_pairs={{0,2},{1,3},{2,0},{3,1},{4,6},{5,7},{6,4},{7,5},{8,10},{9,11},{10,... | collective-permute-start | bytes 589832 | tf_op jit(solution)/shard_map/ppermute | solution.py:32
  19.9 1.0 %collective-permute-done.4.refs_2_ = bf16[4,32,768]{2,1,0:T(8,128)(2,1)S(1)} collective-permute-done((bf16[4,32,768]{2,1,0:T(8,128)(2,1)S(1)}, bf16[4,32,768]{2,1,0:T(8,128)(2,1)S(1)}, u32[]{:S(2)}, u32[]{:S(2)}) %collective-permute-start.4) | collective-permute-done | bytes 196640 | tf_op jit(solution)/shard_map/ppermute | solution.py:32
  20.8 0.7 %collective-permute-done.5.refs_3_ = bf16[4,32,768]{2,1,0:T(8,128)(2,1)S(1)} collective-permute-done((bf16[4,32,768]{2,1,0:T(8,128)(2,1)S(1)}, bf16[4,32,768]{2,1,0:T(8,128)(2,1)S(1)}, u32[]{:S(2)}, u32[]{:S(2)}) %collective-permute-start.5) | collective-permute-done | bytes 196640 | tf_op jit(solution)/shard_map/ppermute | solution.py:32
  21.6 0.1 sides.1.refs_3_.refs_0_
  21.7 0.0 collective-permute-done.2.refs_2_
  21.8 1.2 %collective-permute-start.10 = (bf16[4,32,768]{2,1,0:T(8,128)(2,1)S(1)}, bf16[4,32,768]{2,1,0:T(8,128)(2,1)S(1)}, u32[]{:S(2)}, u32[]{:S(2)}) collective-permute-start(bf16[4,32,768]{2,1,0:T(8,128)(2,1)S(1)} %get-tuple-element.25.refs_0_.refs_3_), channel_id=1, source_target_pairs={{0,4},{4,0},{8,12},{12,8},{16,20},{20,16},{24,28},{28,24},{1,5},{5... | collective-permute-start | bytes 589832 | tf_op jit(solution)/shard_map/ppermute | solution.py:32
  22.9 1.8 %collective-permute-start.9 = (bf16[4,32,768]{2,1,0:T(8,128)(2,1)S(1)}, bf16[4,32,768]{2,1,0:T(8,128)(2,1)S(1)}, u32[]{:S(2)}, u32[]{:S(2)}) collective-permute-start(bf16[4,32,768]{2,1,0:T(8,128)(2,1)S(1)} %get-tuple-element.26.refs_1_), channel_id=1, source_target_pairs={{0,2},{1,3},{2,0},{3,1},{4,6},{5,7},{6,4},{7,5},{8,10},{9,11},{10,... | collective-permute-start | bytes 589832 | tf_op jit(solution)/shard_map/ppermute | solution.py:32
  24.8 0.0 collective-permute-done.14.refs_1_
  24.8 1.4 %collective-permute-done.15.refs_2_ = bf16[4,32,768]{2,1,0:T(8,128)(2,1)S(1)} collective-permute-done((bf16[4,32,768]{2,1,0:T(8,128)(2,1)S(1)}, bf16[4,32,768]{2,1,0:T(8,128)(2,1)S(1)}, u32[]{:S(2)}, u32[]{:S(2)}) %collective-permute-start.15) | collective-permute-done | bytes 196640 | tf_op jit(solution)/shard_map/ppermute | solution.py:32
  26.2 1.6 %collective-permute-start.16 = (bf16[2,2,32,768]{3,2,1,0:T(8,128)(2,1)S(1)}, bf16[2,2,32,768]{3,2,1,0:T(8,128)(2,1)S(1)}, u32[]{:S(2)}, u32[]{:S(2)}) collective-permute-start(bf16[2,2,32,768]{3,2,1,0:T(8,128)(2,1)S(1)} %plane.2.refs_4_), channel_id=1, source_target_pairs={{0,8},{4,12},{8,0},{12,4},{16,24},{20,28},{24,16},{28,20},{1,9},{5... | collective-permute-start | bytes 589832 | tf_op jit(solution)/shard_map/ppermute | solution.py:32
  27.8 0.7 %collective-permute-start.11 = (bf16[4,32,768]{2,1,0:T(8,128)(2,1)S(1)}, bf16[4,32,768]{2,1,0:T(8,128)(2,1)S(1)}, u32[]{:S(2)}, u32[]{:S(2)}) collective-permute-start(bf16[4,32,768]{2,1,0:T(8,128)(2,1)S(1)} %get-tuple-element.26.refs_1_), channel_id=1, source_target_pairs={{0,4},{4,0},{8,12},{12,8},{16,20},{20,16},{24,28},{28,24},{1,5},{5... | collective-permute-start | bytes 589832 | tf_op jit(solution)/shard_map/ppermute | solution.py:32
  28.5 1.5 %collective-permute-start.8 = (bf16[4,32,768]{2,1,0:T(8,128)(2,1)S(1)}, bf16[4,32,768]{2,1,0:T(8,128)(2,1)S(1)}, u32[]{:S(2)}, u32[]{:S(2)}) collective-permute-start(bf16[4,32,768]{2,1,0:T(8,128)(2,1)S(1)} %get-tuple-element.25.refs_0_.refs_3_), channel_id=1, source_target_pairs={{0,2},{1,3},{2,0},{3,1},{4,6},{5,7},{6,4},{7,5},{8,10},{9,11},{10,... | collective-permute-start | bytes 589832 | tf_op jit(solution)/shard_map/ppermute | solution.py:32
  30.0 0.0 collective-permute-done.10.refs_4_
  30.0 0.5 %collective-permute-start.12 = (bf16[4,32,768]{2,1,0:T(8,128)(2,1)S(1)}, bf16[4,32,768]{2,1,0:T(8,128)(2,1)S(1)}, u32[]{:S(2)}, u32[]{:S(2)}) collective-permute-start(bf16[4,32,768]{2,1,0:T(8,128)(2,1)S(1)} %collective-permute-done.10.refs_4_), channel_id=1, source_target_pairs={{0,2},{1,3},{2,0},{3,1},{4,6},{5,7},{6,4},{7,5},{8,10},{9,11},{10,... | collective-permute-start | bytes 589832 | tf_op jit(solution)/shard_map/ppermute | solution.py:32
  30.5 0.0 collective-permute-done.9.refs_3_
  30.5 1.7 %collective-permute-start.13 = (bf16[4,32,768]{2,1,0:T(8,128)(2,1)S(1)}, bf16[4,32,768]{2,1,0:T(8,128)(2,1)S(1)}, u32[]{:S(2)}, u32[]{:S(2)}) collective-permute-start(bf16[4,32,768]{2,1,0:T(8,128)(2,1)S(1)} %collective-permute-done.9.refs_3_), channel_id=1, source_target_pairs={{0,4},{4,0},{8,12},{12,8},{16,20},{20,16},{24,28},{28,24},{1,5},{5... | collective-permute-start | bytes 589832 | tf_op jit(solution)/shard_map/ppermute | solution.py:32
  32.2 0.0 collective-permute-done.16.refs_3_
  32.3 0.0 copy-start
  32.3 1.4 %collective-permute-start.19 = (bf16[1,2,32,768]{3,2,1,0:T(8,128)(2,1)S(1)}, bf16[1,2,32,768]{3,2,1,0:T(8,128)(2,1)S(1)}, u32[]{:S(2)}, u32[]{:S(2)}) collective-permute-start(bf16[1,2,32,768]{3,2,1,0:T(8,128)(2,1)S(1)} %plane.3.refs_2_), channel_id=1, source_target_pairs={{0,16},{4,20},{8,24},{12,28},{16,0},{20,4},{24,8},{28,12},{1,17},{... | collective-permute-start | bytes 294920 | tf_op jit(solution)/shard_map/ppermute | solution.py:32
  33.7 1.1 %collective-permute-done.11.refs_5_ = bf16[4,32,768]{2,1,0:T(8,128)(2,1)S(1)} collective-permute-done((bf16[4,32,768]{2,1,0:T(8,128)(2,1)S(1)}, bf16[4,32,768]{2,1,0:T(8,128)(2,1)S(1)}, u32[]{:S(2)}, u32[]{:S(2)}) %collective-permute-start.11) | collective-permute-done | bytes 196640 | tf_op jit(solution)/shard_map/ppermute | solution.py:32
  34.7 0.9 %collective-permute-done.8.refs_2_ = bf16[4,32,768]{2,1,0:T(8,128)(2,1)S(1)} collective-permute-done((bf16[4,32,768]{2,1,0:T(8,128)(2,1)S(1)}, bf16[4,32,768]{2,1,0:T(8,128)(2,1)S(1)}, u32[]{:S(2)}, u32[]{:S(2)}) %collective-permute-start.8) | collective-permute-done | bytes 196640 | tf_op jit(solution)/shard_map/ppermute | solution.py:32
  35.6 0.1 most.1.refs_0_
  35.7 0.1 collective-permute-start.17
  35.8 1.9 %collective-permute-done.12.refs_0_ = bf16[4,32,768]{2,1,0:T(8,128)(2,1)S(1)} collective-permute-done((bf16[4,32,768]{2,1,0:T(8,128)(2,1)S(1)}, bf16[4,32,768]{2,1,0:T(8,128)(2,1)S(1)}, u32[]{:S(2)}, u32[]{:S(2)}) %collective-permute-start.12) | collective-permute-done | bytes 196640 | tf_op jit(solution)/shard_map/ppermute | solution.py:32
  37.7 0.0 collective-permute-done.13.refs_1_
  37.8 0.1 collective-permute-start.18
  37.8 0.0 collective-permute-done.19.refs_4_
  37.8 0.7 %finish.1 = f32[32,1536]{1,0:T(8,128)} custom-call(f32[2,4,32,768]{3,2,1,0:T(8,128)S(1)} %sides.1.refs_3_.refs_0_, bf16[4,32,768]{2,1,0:T(8,128)(2,1)S(1)} %collective-permute-done.14.refs_1_, bf16[4,32,768]{2,1,0:T(8,128)(2,1)S(1)} %collective-permute-done.15.refs_2_, bf16[2,2,32,768]{3,2,1,0:T(8,128)(2,1)S(1)} %collective-permute-done.16.refs_3_, ...), custom_call_target="tpu_custom_call" | custom-call | flops 40000000000 | bytes 1 | tf_op jit(solution)/shard_map/finish/pallas_call | solution.py:174
  38.6 1.0 %collective-permute-done.18.refs_3_ = bf16[2,4,32,768]{3,2,1,0:T(8,128)(2,1)S(1)} collective-permute-done((bf16[2,4,32,768]{3,2,1,0:T(8,128)(2,1)S(1)}, bf16[2,4,32,768]{3,2,1,0:T(8,128)(2,1)S(1)}, u32[]{:S(2)}, u32[]{:S(2)}) %collective-permute-start.18) | collective-permute-done | bytes 393248 | tf_op jit(solution)/shard_map/ppermute | solution.py:32
  39.5 0.0 collective-permute-done.17.refs_2_
  39.5 1.7 %project.1 = bf16[128,128]{1,0:T(8,128)(2,1)} custom-call(bf16[128,12288]{1,0:T(8,128)(2,1)S(1)} %copy-done, bf16[6,4,32,768]{3,2,1,0:T(8,128)(2,1)S(1)} %most.1.refs_0_, bf16[2,4,32,768]{3,2,1,0:T(8,128)(2,1)S(1)} %last.1.refs_1_, bf16[6,4,32,768]{3,2,1,0:T(8,128)(2,1)S(1)} %collective-permute-done.17.refs_2_, ...), custom_call_target="tpu_custom_call" | custom-call | flops 402653184 | bytes 6291456 | tf_op jit(solution)/shard_map/project/pallas_call | solution.py:211
  (6 shorter events, 0.1 us)
Async XLA Ops:
  4.0 4.6 %collective-permute-start.1 = (bf16[4,4,32,768]{3,2,1,0:T(8,128)(2,1)S(1)}, bf16[4,4,32,768]{3,2,1,0:T(8,128)(2,1)S(1)}, u32[]{:S(2)}, u32[]{:S(2)}) collective-permute-start(bf16[4,4,32,768]{3,2,1,0:T(8,128)(2,1)S(1)} %get-tuple-element.17), channel_id=1, source_target_pairs={{0,1},{1,0},{2,3},{3,2},{4,5},{5,4},{6,7},{7,6},{8,9},{9,8},{10,11... | collective-permute-start | bytes 2359304 | tf_op jit(solution)/shard_map/ppermute | solution.py:32
  4.5 10.8 %collective-permute-start.3 = (bf16[4,4,32,768]{3,2,1,0:T(8,128)(2,1)S(1)}, bf16[4,4,32,768]{3,2,1,0:T(8,128)(2,1)S(1)}, u32[]{:S(2)}, u32[]{:S(2)}) collective-permute-start(bf16[4,4,32,768]{3,2,1,0:T(8,128)(2,1)S(1)} %get-tuple-element.20), channel_id=1, source_target_pairs={{0,1},{1,0},{2,3},{3,2},{4,5},{5,4},{6,7},{7,6},{8,9},{9,8},{10,11... | collective-permute-start | bytes 2359304 | tf_op jit(solution)/shard_map/ppermute | solution.py:32
  4.6 9.2 %collective-permute-start = (bf16[2,32,768]{2,1,0:T(8,128)(2,1)S(1)}, bf16[2,32,768]{2,1,0:T(8,128)(2,1)S(1)}, u32[]{:S(2)}, u32[]{:S(2)}) collective-permute-start(bf16[2,32,768]{2,1,0:T(8,128)(2,1)S(1)} %get-tuple-element.15.refs_0_), channel_id=1, source_target_pairs={{0,16},{4,20},{8,24},{12,28},{16,0},{20,4},{24,8},{28,12},{1,17},{... | collective-permute-start | bytes 294920 | tf_op jit(solution)/shard_map/ppermute | solution.py:32
  8.8 7.9 %collective-permute-start.6 = (bf16[1,4,32,768]{3,2,1,0:T(8,128)(2,1)S(1)}, bf16[1,4,32,768]{3,2,1,0:T(8,128)(2,1)S(1)}, u32[]{:S(2)}, u32[]{:S(2)}) collective-permute-start(bf16[1,4,32,768]{3,2,1,0:T(8,128)(2,1)S(1)} %get-tuple-element.18.refs_2_), channel_id=1, source_target_pairs={{0,4},{4,0},{8,12},{12,8},{16,20},{20,16},{24,28},{28,24},{1,5},{5... | collective-permute-start | bytes 589832 | tf_op jit(solution)/shard_map/ppermute | solution.py:32
  10.3 7.0 %collective-permute-start.7 = (bf16[4,32,768]{2,1,0:T(8,128)(2,1)S(1)}, bf16[4,32,768]{2,1,0:T(8,128)(2,1)S(1)}, u32[]{:S(2)}, u32[]{:S(2)}) collective-permute-start(bf16[4,32,768]{2,1,0:T(8,128)(2,1)S(1)} %get-tuple-element.23), channel_id=1, source_target_pairs={{0,2},{1,3},{2,0},{3,1},{4,6},{5,7},{6,4},{7,5},{8,10},{9,11},{10,... | collective-permute-start | bytes 589832 | tf_op jit(solution)/shard_map/ppermute | solution.py:32
  11.8 9.0 %collective-permute-start.4 = (bf16[4,32,768]{2,1,0:T(8,128)(2,1)S(1)}, bf16[4,32,768]{2,1,0:T(8,128)(2,1)S(1)}, u32[]{:S(2)}, u32[]{:S(2)}) collective-permute-start(bf16[4,32,768]{2,1,0:T(8,128)(2,1)S(1)} %get-tuple-element.21), channel_id=1, source_target_pairs={{0,4},{4,0},{8,12},{12,8},{16,20},{20,16},{24,28},{28,24},{1,5},{5... | collective-permute-start | bytes 589832 | tf_op jit(solution)/shard_map/ppermute | solution.py:32
  13.7 7.8 %collective-permute-start.5 = (bf16[4,32,768]{2,1,0:T(8,128)(2,1)S(1)}, bf16[4,32,768]{2,1,0:T(8,128)(2,1)S(1)}, u32[]{:S(2)}, u32[]{:S(2)}) collective-permute-start(bf16[4,32,768]{2,1,0:T(8,128)(2,1)S(1)} %get-tuple-element.22), channel_id=1, source_target_pairs={{0,2},{1,3},{2,0},{3,1},{4,6},{5,7},{6,4},{7,5},{8,10},{9,11},{10,... | collective-permute-start | bytes 589832 | tf_op jit(solution)/shard_map/ppermute | solution.py:32
  15.3 6.4 %collective-permute-start.2 = (bf16[2,2,32,768]{3,2,1,0:T(8,128)(2,1)S(1)}, bf16[2,2,32,768]{3,2,1,0:T(8,128)(2,1)S(1)}, u32[]{:S(2)}, u32[]{:S(2)}) collective-permute-start(bf16[2,2,32,768]{3,2,1,0:T(8,128)(2,1)S(1)} %widen.1.refs_4_), channel_id=1, source_target_pairs={{0,8},{4,12},{8,0},{12,4},{16,24},{20,28},{24,16},{28,20},{1,9},{5... | collective-permute-start | bytes 589832 | tf_op jit(solution)/shard_map/ppermute | solution.py:32
  17.5 7.3 %collective-permute-start.14 = (bf16[4,32,768]{2,1,0:T(8,128)(2,1)S(1)}, bf16[4,32,768]{2,1,0:T(8,128)(2,1)S(1)}, u32[]{:S(2)}, u32[]{:S(2)}) collective-permute-start(bf16[4,32,768]{2,1,0:T(8,128)(2,1)S(1)} %get-tuple-element.24.refs_4_), channel_id=1, source_target_pairs={{0,4},{4,0},{8,12},{12,8},{16,20},{20,16},{24,28},{28,24},{1,5},{5... | collective-permute-start | bytes 589832 | tf_op jit(solution)/shard_map/ppermute | solution.py:32
  18.3 7.8 %collective-permute-start.15 = (bf16[4,32,768]{2,1,0:T(8,128)(2,1)S(1)}, bf16[4,32,768]{2,1,0:T(8,128)(2,1)S(1)}, u32[]{:S(2)}, u32[]{:S(2)}) collective-permute-start(bf16[4,32,768]{2,1,0:T(8,128)(2,1)S(1)} %get-tuple-element.27), channel_id=1, source_target_pairs={{0,2},{1,3},{2,0},{3,1},{4,6},{5,7},{6,4},{7,5},{8,10},{9,11},{10,... | collective-permute-start | bytes 589832 | tf_op jit(solution)/shard_map/ppermute | solution.py:32
  21.8 8.3 %collective-permute-start.10 = (bf16[4,32,768]{2,1,0:T(8,128)(2,1)S(1)}, bf16[4,32,768]{2,1,0:T(8,128)(2,1)S(1)}, u32[]{:S(2)}, u32[]{:S(2)}) collective-permute-start(bf16[4,32,768]{2,1,0:T(8,128)(2,1)S(1)} %get-tuple-element.25.refs_0_.refs_3_), channel_id=1, source_target_pairs={{0,4},{4,0},{8,12},{12,8},{16,20},{20,16},{24,28},{28,24},{1,5},{5... | collective-permute-start | bytes 589832 | tf_op jit(solution)/shard_map/ppermute | solution.py:32
  22.9 7.6 %collective-permute-start.9 = (bf16[4,32,768]{2,1,0:T(8,128)(2,1)S(1)}, bf16[4,32,768]{2,1,0:T(8,128)(2,1)S(1)}, u32[]{:S(2)}, u32[]{:S(2)}) collective-permute-start(bf16[4,32,768]{2,1,0:T(8,128)(2,1)S(1)} %get-tuple-element.26.refs_1_), channel_id=1, source_target_pairs={{0,2},{1,3},{2,0},{3,1},{4,6},{5,7},{6,4},{7,5},{8,10},{9,11},{10,... | collective-permute-start | bytes 589832 | tf_op jit(solution)/shard_map/ppermute | solution.py:32
  26.2 6.0 %collective-permute-start.16 = (bf16[2,2,32,768]{3,2,1,0:T(8,128)(2,1)S(1)}, bf16[2,2,32,768]{3,2,1,0:T(8,128)(2,1)S(1)}, u32[]{:S(2)}, u32[]{:S(2)}) collective-permute-start(bf16[2,2,32,768]{3,2,1,0:T(8,128)(2,1)S(1)} %plane.2.refs_4_), channel_id=1, source_target_pairs={{0,8},{4,12},{8,0},{12,4},{16,24},{20,28},{24,16},{28,20},{1,9},{5... | collective-permute-start | bytes 589832 | tf_op jit(solution)/shard_map/ppermute | solution.py:32
  27.8 6.9 %collective-permute-start.11 = (bf16[4,32,768]{2,1,0:T(8,128)(2,1)S(1)}, bf16[4,32,768]{2,1,0:T(8,128)(2,1)S(1)}, u32[]{:S(2)}, u32[]{:S(2)}) collective-permute-start(bf16[4,32,768]{2,1,0:T(8,128)(2,1)S(1)} %get-tuple-element.26.refs_1_), channel_id=1, source_target_pairs={{0,4},{4,0},{8,12},{12,8},{16,20},{20,16},{24,28},{28,24},{1,5},{5... | collective-permute-start | bytes 589832 | tf_op jit(solution)/shard_map/ppermute | solution.py:32
  28.5 7.1 %collective-permute-start.8 = (bf16[4,32,768]{2,1,0:T(8,128)(2,1)S(1)}, bf16[4,32,768]{2,1,0:T(8,128)(2,1)S(1)}, u32[]{:S(2)}, u32[]{:S(2)}) collective-permute-start(bf16[4,32,768]{2,1,0:T(8,128)(2,1)S(1)} %get-tuple-element.25.refs_0_.refs_3_), channel_id=1, source_target_pairs={{0,2},{1,3},{2,0},{3,1},{4,6},{5,7},{6,4},{7,5},{8,10},{9,11},{10,... | collective-permute-start | bytes 589832 | tf_op jit(solution)/shard_map/ppermute | solution.py:32
  30.0 7.7 %collective-permute-start.12 = (bf16[4,32,768]{2,1,0:T(8,128)(2,1)S(1)}, bf16[4,32,768]{2,1,0:T(8,128)(2,1)S(1)}, u32[]{:S(2)}, u32[]{:S(2)}) collective-permute-start(bf16[4,32,768]{2,1,0:T(8,128)(2,1)S(1)} %collective-permute-done.10.refs_4_), channel_id=1, source_target_pairs={{0,2},{1,3},{2,0},{3,1},{4,6},{5,7},{6,4},{7,5},{8,10},{9,11},{10,... | collective-permute-start | bytes 589832 | tf_op jit(solution)/shard_map/ppermute | solution.py:32
  30.5 7.2 %collective-permute-start.13 = (bf16[4,32,768]{2,1,0:T(8,128)(2,1)S(1)}, bf16[4,32,768]{2,1,0:T(8,128)(2,1)S(1)}, u32[]{:S(2)}, u32[]{:S(2)}) collective-permute-start(bf16[4,32,768]{2,1,0:T(8,128)(2,1)S(1)} %collective-permute-done.9.refs_3_), channel_id=1, source_target_pairs={{0,4},{4,0},{8,12},{12,8},{16,20},{20,16},{24,28},{28,24},{1,5},{5... | collective-permute-start | bytes 589832 | tf_op jit(solution)/shard_map/ppermute | solution.py:32
  32.3 5.6 %copy-start = (bf16[128,12288]{1,0:T(8,128)(2,1)S(1)}, bf16[128,12288]{1,0:T(8,128)(2,1)}, u32[]{:S(2)}) copy-start(bf16[128,12288]{1,0:T(8,128)(2,1)} %refs_5_.1) | copy-start | bytes 9437188
  32.3 5.6 %collective-permute-start.19 = (bf16[1,2,32,768]{3,2,1,0:T(8,128)(2,1)S(1)}, bf16[1,2,32,768]{3,2,1,0:T(8,128)(2,1)S(1)}, u32[]{:S(2)}, u32[]{:S(2)}) collective-permute-start(bf16[1,2,32,768]{3,2,1,0:T(8,128)(2,1)S(1)} %plane.3.refs_2_), channel_id=1, source_target_pairs={{0,16},{4,20},{8,24},{12,28},{16,0},{20,4},{24,8},{28,12},{1,17},{... | collective-permute-start | bytes 294920 | tf_op jit(solution)/shard_map/ppermute | solution.py:32
  35.7 3.9 %collective-permute-start.17 = (bf16[6,4,32,768]{3,2,1,0:T(8,128)(2,1)S(1)}, bf16[6,4,32,768]{3,2,1,0:T(8,128)(2,1)S(1)}, u32[]{:S(2)}, u32[]{:S(2)}) collective-permute-start(bf16[6,4,32,768]{3,2,1,0:T(8,128)(2,1)S(1)} %most.1.refs_0_), channel_id=1, source_target_pairs={{0,1},{1,0},{2,3},{3,2},{4,5},{5,4},{6,7},{7,6},{8,9},{9,8},{10,11... | collective-permute-start | bytes 3538952 | tf_op jit(solution)/shard_map/ppermute | solution.py:32
  37.8 1.8 %collective-permute-start.18 = (bf16[2,4,32,768]{3,2,1,0:T(8,128)(2,1)S(1)}, bf16[2,4,32,768]{3,2,1,0:T(8,128)(2,1)S(1)}, u32[]{:S(2)}, u32[]{:S(2)}) collective-permute-start(bf16[2,4,32,768]{3,2,1,0:T(8,128)(2,1)S(1)} %last.1.refs_1_), channel_id=1, source_target_pairs={{0,1},{1,0},{2,3},{3,2},{4,5},{5,4},{6,7},{7,6},{8,9},{9,8},{10,11... | collective-permute-start | bytes 1179656 | tf_op jit(solution)/shard_map/ppermute | solution.py:32

commit v2 on v1

--- a/solution.py
+++ b/solution.py
@@ -182,53 +182,74 @@
     )(*arrays, after)
 
 
-def project_kernel(ys, zs, tokens, *refs):
-    weights, out, total_t = refs[:4], refs[4], refs[5]
+def project_kernel(ys, zs, x, tokens, *refs):
+    if x == 0:
+        (*weights, out) = refs
+        total = 0.0
+    else:
+        (*weights, earlier, out, total_t) = refs
+        total = earlier[...]
+    count = len(weights) // 2
     rows, half = weights[0].shape[2:]
     cols = 2 * half
-    most = 2 * ys + 2
+    for z in range(zs):
+        pieces = tokens[:, columns_of(x, z, cols)]
+        for h in range(2):
+            picked = []
+            for n in range(2 * ys):
+                held = weights[count * (n % 2) : count * (n % 2 + 1)]
+                y = n // 2
+                if x and y:
+                    picked.append(held[1 + 2 * (y - 1) + h][z])
+                else:
+                    picked.append(held[0][2 * y + h, z])
+            left = jnp.concatenate(picked, axis=0)
+            right = pieces[:, h * half : (h + 1) * half]
+            total = total + lax.dot_general(left, right, NT, preferred_element_type=F32)
+    if x == 0:
+        out[...] = total
+        return
     node = lax.axis_index("node")
-    total = jnp.zeros((2 * ys * rows, tokens.shape[0]), F32)
-    for x in range(2):
-        for z in range(zs):
-            pieces = tokens[:, columns_of(x, z, cols)]
-            for h in range(2):
-                picked = []
-                for n in range(2 * ys):
-                    at = place_of(h, x, n // 2, ys)
-                    picked.append(weights[2 * (n % 2) + (at >= most)][at % most, z])
-                left = jnp.concatenate(picked, axis=0)
-                right = pieces[:, h * half : (h + 1) * half]
-                total = total + lax.dot_general(left, right, NT, preferred_element_type=F32)
     total_t[...] = total.reshape(total_t.shape)
     ordered = [total_t[lax.bitwise_xor(node, n)] for n in range(2 * ys)]
     out[...] = jnp.concatenate(ordered, axis=0).T.astype(BF16)
 
 
-def project(tokens, weights, ys, zs):
-    rows = weights[0].shape[2]
-    width = 2 * ys * rows
+def project(tokens, near, far, ys, zs):
+    rows = near[0].shape[2]
+    count, width = tokens.shape[0], 2 * ys * rows
+    cost = pl.CostEstimate(flops=tokens.size * width, bytes_accessed=2 * tokens.size, transcendentals=0)
+    earlier = pl.pallas_call(
+        functools.partial(project_kernel, ys, zs, 0),
+        out_shape=jax.ShapeDtypeStruct((width, count), F32),
+        in_specs=[VMEM] * (1 + len(near)),
+        out_specs=VMEM,
+        compiler_params=PARAMS,
+        cost_estimate=cost,
+        name="project_near",
+    )(tokens, *near)
     return pl.pallas_call(
-        functools.partial(project_kernel, ys, zs),
-        out_shape=jax.ShapeDtypeStruct((tokens.shape[0], width), BF16),
-        in_specs=[VMEM] * 5,
+        functools.partial(project_kernel, ys, zs, 1),
+        out_shape=jax.ShapeDtypeStruct((count, width), BF16),
+        in_specs=[VMEM] * (2 + len(far)),
         out_specs=VMEM,
-        scratch_shapes=[pltpu.VMEM((2 * ys, rows, tokens.shape[0]), F32)],
-        compiler_params=PARAMS,
-        cost_estimate=pl.CostEstimate(
-            flops=2 * tokens.size * width, bytes_accessed=4 * tokens.size, transcendentals=0
-        ),
-        name="project",
-    )(tokens, *weights)
-
-
-def plain_project(tokens, weights, ys, zs):
-    rows, half = weights[0].shape[2:]
-    weights = [jnp.concatenate(weights[:2]), jnp.concatenate(weights[2:])]
+        scratch_shapes=[pltpu.VMEM((2 * ys, rows, count), F32)],
+        compiler_params=PARAMS,
+        cost_estimate=cost,
+        name="project_far",
+    )(tokens, *far, earlier)
+
+
+def plain_project(tokens, near, far, ys, zs):
+    rows, half = near[0].shape[2:]
     node, wide = lax.axis_index("node"), lax.axis_index("wide")
     pieces = tokens.reshape(tokens.shape[0], 2 * zs, 2, half)
     pieces = jnp.take(pieces, jnp.arange(2 * zs) ^ wide, axis=1)
     pieces = pieces.reshape(tokens.shape[0], zs, 2, 2, half)
+    count = len(far) // 2
+    weights = [
+        jnp.concatenate([near[c], far[count * c], jnp.stack(far[count * c + 1 : count * (c + 1)])]) for c in range(2)
+    ]
     total = []
     for n in range(2 * ys):
         part = 0.0
@@ -337,12 +358,13 @@
     weight_grad = finish([sums[0, 0], sums[0, 1]], arrays, tokens)
 
     held = own + [e for es in on_y for e in es] + on_x
-    places = [((i,), [(i, whole)]) for i in range(len(held))]
-    (most,) = add_up([((len(held), *one), places)], held, name="most")
-    held = [d for ds in diag for d in ds]
-    places = [((i,), [(i, whole)]) for i in range(len(held))]
-    (last,) = add_up([((len(held), *one), places)], held, [to_z], name="last")
-    projected = make_project(tokens, [most, last, core_flip(most), core_flip(last)], ys, zs)
+    groups = [range(2 * ys), range(2 * ys, 2 * ys + 2)]
+    outs = [((len(g), *one), [((i - g[0],), [(i, whole)]) for i in g]) for g in groups]
+    near, side = add_up(outs, held, name="most")
+    ends = [d for ds in diag for d in ds]
+    near = [near, core_flip(near)]
+    far = [side, *ends, core_flip(side), *[core_flip(e) for e in ends]]
+    projected = make_project(tokens, near, far, ys, zs)
     return projected, weight_grad.T
 
 

time: 41.4 us -> 41 us (level)
  waiting for transfers between devices: 10.7 us -> 9.2 us
  starting transfers between devices: 23.4 us -> 24.3 us
    ppermute x20 -> x22, waiting for transfers between devices: 10.7 us -> 9.2 us  [flip(): return lax.ppermute(entries, axis, [(i, i ^ offset) for i in range(size)])]
    ppermute x20 -> x22, starting transfers between devices: 23.4 us -> 24.3 us  [flip(): return lax.ppermute(entries, axis, [(i, i ^ offset) for i in range(size)])]
    pallas_call x1 -> x2, Pallas kernels: 1.71 us -> 1.89 us  [the longest x1 1.32 us: project(): pl.pallas_call(functools.partial(project_kernel, ys, zs, 1), out_shape=ja...]
  transfers between devices with their start and end apart: 20 -> 22, of which waited for: 10 -> 9; matrix products, arithmetic and copies ran while one was open for 0% -> 0% of each run, Pallas kernels for 3% -> 5%
where the time goes in v2:
time: 41 us; the launch traced here: 40.9 us
  starting transfers between devices  24.3 us (59%)
  waiting for transfers between devices  9.2 us (22%)
  Pallas kernels  6.58 us (16%)
  between operations  0.75 us (2%)
    ppermute x22, starting transfers between devices, flip(): return lax.ppermute(entries, axis, [(i, i ^ offset) for i in range(size)])  24.3 us
    ppermute x22, waiting for transfers between devices, flip(): return lax.ppermute(entries, axis, [(i, i ^ offset) for i in range(size)])  9.2 us
    pallas_call x1, Pallas kernels, local_products(): pl.pallas_call(functools.partial(first_kernel, ys, zs), out_shape=(*block...  3.33 us
    pallas_call x1, Pallas kernels, project(): pl.pallas_call(functools.partial(project_kernel, ys, zs, 1), out_shape=ja...  1.32 us
  transfers between devices with their start and end apart: 22, of which 9 were waited for; matrix products, arithmetic and copies ran while one was open for 0% of the time, Pallas kernels for 5%

profile of v2, /device:TPU:0, one launch (start us, length us, event | category | flops | bytes accessed | tf_op | source)
XLA Modules:
  0.0 40.9 jit_solution(13666873143640436860)
XLA Ops:
  0.6 3.3 %first.1 = (bf16[4,4,32,768]{3,2,1,0:T(8,128)(2,1)S(1)}, bf16[4,4,32,768]{3,2,1,0:T(8,128)(2,1)S(1)}, bf16[4,4,32,768]{3,2,1,0:T(8,128)(2,1)S(1)}, bf16[4,4,32,7...) custom-call(bf16[128,12288]{1,0:T(8,128)(2,1)} %refs_5_.1, bf16[128,128]{1,0:T(8,128)(2,1)} %cot.1, ...), custom_call_target="tpu_custom_call" | custom-call | flops 402653184 | bytes 6291456 | tf_op jit(solution)/shard_map/first/pallas_call | solution.py:92
  4.0 0.5 %collective-permute-start.1 = (bf16[4,4,32,768]{3,2,1,0:T(8,128)(2,1)S(1)}, bf16[4,4,32,768]{3,2,1,0:T(8,128)(2,1)S(1)}, u32[]{:S(2)}, u32[]{:S(2)}) collective-permute-start(bf16[4,4,32,768]{3,2,1,0:T(8,128)(2,1)S(1)} %get-tuple-element.19), channel_id=1, source_target_pairs={{0,1},{1,0},{2,3},{3,2},{4,5},{5,4},{6,7},{7,6},{8,9},{9,8},{10,11... | collective-permute-start | bytes 2359304 | tf_op jit(solution)/shard_map/ppermute | solution.py:32
  4.5 0.1 collective-permute-start.3
  4.6 4.0 %collective-permute-start = (bf16[2,32,768]{2,1,0:T(8,128)(2,1)S(1)}, bf16[2,32,768]{2,1,0:T(8,128)(2,1)S(1)}, u32[]{:S(2)}, u32[]{:S(2)}) collective-permute-start(bf16[2,32,768]{2,1,0:T(8,128)(2,1)S(1)} %get-tuple-element.17.refs_0_), channel_id=1, source_target_pairs={{0,16},{4,20},{8,24},{12,28},{16,0},{20,4},{24,8},{28,12},{1,17},{... | collective-permute-start | bytes 294920 | tf_op jit(solution)/shard_map/ppermute | solution.py:32
  8.6 0.0 collective-permute-done.1.refs_1_
  8.6 0.2 stage1.1
  8.8 1.6 %collective-permute-start.6 = (bf16[1,4,32,768]{3,2,1,0:T(8,128)(2,1)S(1)}, bf16[1,4,32,768]{3,2,1,0:T(8,128)(2,1)S(1)}, u32[]{:S(2)}, u32[]{:S(2)}) collective-permute-start(bf16[1,4,32,768]{3,2,1,0:T(8,128)(2,1)S(1)} %get-tuple-element.20.refs_2_), channel_id=1, source_target_pairs={{0,4},{4,0},{8,12},{12,8},{16,20},{20,16},{24,28},{28,24},{1,5},{5... | collective-permute-start | bytes 589832 | tf_op jit(solution)/shard_map/ppermute | solution.py:32
  10.3 1.5 %collective-permute-start.7 = (bf16[4,32,768]{2,1,0:T(8,128)(2,1)S(1)}, bf16[4,32,768]{2,1,0:T(8,128)(2,1)S(1)}, u32[]{:S(2)}, u32[]{:S(2)}) collective-permute-start(bf16[4,32,768]{2,1,0:T(8,128)(2,1)S(1)} %get-tuple-element.25), channel_id=1, source_target_pairs={{0,2},{1,3},{2,0},{3,1},{4,6},{5,7},{6,4},{7,5},{8,10},{9,11},{10,... | collective-permute-start | bytes 589832 | tf_op jit(solution)/shard_map/ppermute | solution.py:32
  11.8 0.5 %collective-permute-start.4 = (bf16[4,32,768]{2,1,0:T(8,128)(2,1)S(1)}, bf16[4,32,768]{2,1,0:T(8,128)(2,1)S(1)}, u32[]{:S(2)}, u32[]{:S(2)}) collective-permute-start(bf16[4,32,768]{2,1,0:T(8,128)(2,1)S(1)} %get-tuple-element.23), channel_id=1, source_target_pairs={{0,4},{4,0},{8,12},{12,8},{16,20},{20,16},{24,28},{28,24},{1,5},{5... | collective-permute-start | bytes 589832 | tf_op jit(solution)/shard_map/ppermute | solution.py:32
  12.4 1.3 %collective-permute-done.refs_1_ = bf16[2,32,768]{2,1,0:T(8,128)(2,1)S(1)} collective-permute-done((bf16[2,32,768]{2,1,0:T(8,128)(2,1)S(1)}, bf16[2,32,768]{2,1,0:T(8,128)(2,1)S(1)}, u32[]{:S(2)}, u32[]{:S(2)}) %collective-permute-start) | collective-permute-done | bytes 98336 | tf_op jit(solution)/shard_map/ppermute | solution.py:32
  13.7 1.6 %collective-permute-start.5 = (bf16[4,32,768]{2,1,0:T(8,128)(2,1)S(1)}, bf16[4,32,768]{2,1,0:T(8,128)(2,1)S(1)}, u32[]{:S(2)}, u32[]{:S(2)}) collective-permute-start(bf16[4,32,768]{2,1,0:T(8,128)(2,1)S(1)} %get-tuple-element.24), channel_id=1, source_target_pairs={{0,2},{1,3},{2,0},{3,1},{4,6},{5,7},{6,4},{7,5},{8,10},{9,11},{10,... | collective-permute-start | bytes 589832 | tf_op jit(solution)/shard_map/ppermute | solution.py:32
  15.3 0.0 collective-permute-done.3.refs_1_
  15.3 0.7 %collective-permute-start.2 = (bf16[2,2,32,768]{3,2,1,0:T(8,128)(2,1)S(1)}, bf16[2,2,32,768]{3,2,1,0:T(8,128)(2,1)S(1)}, u32[]{:S(2)}, u32[]{:S(2)}) collective-permute-start(bf16[2,2,32,768]{3,2,1,0:T(8,128)(2,1)S(1)} %widen.1.refs_4_), channel_id=1, source_target_pairs={{0,8},{4,12},{8,0},{12,4},{16,24},{20,28},{24,16},{28,20},{1,9},{5... | collective-permute-start | bytes 589832 | tf_op jit(solution)/shard_map/ppermute | solution.py:32
  16.1 0.6 %collective-permute-done.6.refs_2_ = bf16[1,4,32,768]{3,2,1,0:T(8,128)(2,1)S(1)} collective-permute-done((bf16[1,4,32,768]{3,2,1,0:T(8,128)(2,1)S(1)}, bf16[1,4,32,768]{3,2,1,0:T(8,128)(2,1)S(1)}, u32[]{:S(2)}, u32[]{:S(2)}) %collective-permute-start.6) | collective-permute-done | bytes 196640 | tf_op jit(solution)/shard_map/ppermute | solution.py:32
  16.6 0.7 %collective-permute-done.7.refs_3_ = bf16[4,32,768]{2,1,0:T(8,128)(2,1)S(1)} collective-permute-done((bf16[4,32,768]{2,1,0:T(8,128)(2,1)S(1)}, bf16[4,32,768]{2,1,0:T(8,128)(2,1)S(1)}, u32[]{:S(2)}, u32[]{:S(2)}) %collective-permute-start.7) | collective-permute-done | bytes 196640 | tf_op jit(solution)/shard_map/ppermute | solution.py:32
  17.4 0.1 stage2.1
  17.5 0.8 %collective-permute-start.18 = (bf16[4,32,768]{2,1,0:T(8,128)(2,1)S(1)}, bf16[4,32,768]{2,1,0:T(8,128)(2,1)S(1)}, u32[]{:S(2)}, u32[]{:S(2)}) collective-permute-start(bf16[4,32,768]{2,1,0:T(8,128)(2,1)S(1)} %get-tuple-element.26.refs_4_), channel_id=1, source_target_pairs={{0,4},{4,0},{8,12},{12,8},{16,20},{20,16},{24,28},{28,24},{1,5},{5... | collective-permute-start | bytes 589832 | tf_op jit(solution)/shard_map/ppermute | solution.py:32
  18.3 1.5 %collective-permute-start.19 = (bf16[4,32,768]{2,1,0:T(8,128)(2,1)S(1)}, bf16[4,32,768]{2,1,0:T(8,128)(2,1)S(1)}, u32[]{:S(2)}, u32[]{:S(2)}) collective-permute-start(bf16[4,32,768]{2,1,0:T(8,128)(2,1)S(1)} %get-tuple-element.31), channel_id=1, source_target_pairs={{0,2},{1,3},{2,0},{3,1},{4,6},{5,7},{6,4},{7,5},{8,10},{9,11},{10,... | collective-permute-start | bytes 589832 | tf_op jit(solution)/shard_map/ppermute | solution.py:32
  19.9 1.0 %collective-permute-done.4.refs_2_ = bf16[4,32,768]{2,1,0:T(8,128)(2,1)S(1)} collective-permute-done((bf16[4,32,768]{2,1,0:T(8,128)(2,1)S(1)}, bf16[4,32,768]{2,1,0:T(8,128)(2,1)S(1)}, u32[]{:S(2)}, u32[]{:S(2)}) %collective-permute-start.4) | collective-permute-done | bytes 196640 | tf_op jit(solution)/shard_map/ppermute | solution.py:32
  20.8 0.7 %collective-permute-done.5.refs_3_ = bf16[4,32,768]{2,1,0:T(8,128)(2,1)S(1)} collective-permute-done((bf16[4,32,768]{2,1,0:T(8,128)(2,1)S(1)}, bf16[4,32,768]{2,1,0:T(8,128)(2,1)S(1)}, u32[]{:S(2)}, u32[]{:S(2)}) %collective-permute-start.5) | collective-permute-done | bytes 196640 | tf_op jit(solution)/shard_map/ppermute | solution.py:32
  21.6 0.1 sides.1.refs_3_.refs_0_
  21.7 0.0 copy-start
  21.7 0.0 collective-permute-done.2.refs_2_
  21.8 1.2 %collective-permute-start.10 = (bf16[4,32,768]{2,1,0:T(8,128)(2,1)S(1)}, bf16[4,32,768]{2,1,0:T(8,128)(2,1)S(1)}, u32[]{:S(2)}, u32[]{:S(2)}) collective-permute-start(bf16[4,32,768]{2,1,0:T(8,128)(2,1)S(1)} %get-tuple-element.27.refs_0_.refs_3_), channel_id=1, source_target_pairs={{0,4},{4,0},{8,12},{12,8},{16,20},{20,16},{24,28},{28,24},{1,5},{5... | collective-permute-start | bytes 589832 | tf_op jit(solution)/shard_map/ppermute | solution.py:32
  22.9 1.8 %collective-permute-start.9 = (bf16[4,32,768]{2,1,0:T(8,128)(2,1)S(1)}, bf16[4,32,768]{2,1,0:T(8,128)(2,1)S(1)}, u32[]{:S(2)}, u32[]{:S(2)}) collective-permute-start(bf16[4,32,768]{2,1,0:T(8,128)(2,1)S(1)} %get-tuple-element.28.refs_1_), channel_id=1, source_target_pairs={{0,2},{1,3},{2,0},{3,1},{4,6},{5,7},{6,4},{7,5},{8,10},{9,11},{10,... | collective-permute-start | bytes 589832 | tf_op jit(solution)/shard_map/ppermute | solution.py:32
  24.8 0.0 collective-permute-done.18.refs_1_
  24.8 1.4 %collective-permute-done.19.refs_2_ = bf16[4,32,768]{2,1,0:T(8,128)(2,1)S(1)} collective-permute-done((bf16[4,32,768]{2,1,0:T(8,128)(2,1)S(1)}, bf16[4,32,768]{2,1,0:T(8,128)(2,1)S(1)}, u32[]{:S(2)}, u32[]{:S(2)}) %collective-permute-start.19) | collective-permute-done | bytes 196640 | tf_op jit(solution)/shard_map/ppermute | solution.py:32
  26.2 1.6 %collective-permute-start.20 = (bf16[2,2,32,768]{3,2,1,0:T(8,128)(2,1)S(1)}, bf16[2,2,32,768]{3,2,1,0:T(8,128)(2,1)S(1)}, u32[]{:S(2)}, u32[]{:S(2)}) collective-permute-start(bf16[2,2,32,768]{3,2,1,0:T(8,128)(2,1)S(1)} %plane.2.refs_4_), channel_id=1, source_target_pairs={{0,8},{4,12},{8,0},{12,4},{16,24},{20,28},{24,16},{28,20},{1,9},{5... | collective-permute-start | bytes 589832 | tf_op jit(solution)/shard_map/ppermute | solution.py:32
  27.8 0.7 %collective-permute-start.11 = (bf16[4,32,768]{2,1,0:T(8,128)(2,1)S(1)}, bf16[4,32,768]{2,1,0:T(8,128)(2,1)S(1)}, u32[]{:S(2)}, u32[]{:S(2)}) collective-permute-start(bf16[4,32,768]{2,1,0:T(8,128)(2,1)S(1)} %get-tuple-element.28.refs_1_), channel_id=1, source_target_pairs={{0,4},{4,0},{8,12},{12,8},{16,20},{20,16},{24,28},{28,24},{1,5},{5... | collective-permute-start | bytes 589832 | tf_op jit(solution)/shard_map/ppermute | solution.py:32
  28.5 1.5 %collective-permute-start.8 = (bf16[4,32,768]{2,1,0:T(8,128)(2,1)S(1)}, bf16[4,32,768]{2,1,0:T(8,128)(2,1)S(1)}, u32[]{:S(2)}, u32[]{:S(2)}) collective-permute-start(bf16[4,32,768]{2,1,0:T(8,128)(2,1)S(1)} %get-tuple-element.27.refs_0_.refs_3_), channel_id=1, source_target_pairs={{0,2},{1,3},{2,0},{3,1},{4,6},{5,7},{6,4},{7,5},{8,10},{9,11},{10,... | collective-permute-start | bytes 589832 | tf_op jit(solution)/shard_map/ppermute | solution.py:32
  30.0 0.0 collective-permute-done.10.refs_4_
  30.0 0.5 %collective-permute-start.12 = (bf16[4,32,768]{2,1,0:T(8,128)(2,1)S(1)}, bf16[4,32,768]{2,1,0:T(8,128)(2,1)S(1)}, u32[]{:S(2)}, u32[]{:S(2)}) collective-permute-start(bf16[4,32,768]{2,1,0:T(8,128)(2,1)S(1)} %collective-permute-done.10.refs_4_), channel_id=1, source_target_pairs={{0,2},{1,3},{2,0},{3,1},{4,6},{5,7},{6,4},{7,5},{8,10},{9,11},{10,... | collective-permute-start | bytes 589832 | tf_op jit(solution)/shard_map/ppermute | solution.py:32
  30.5 1.7 %collective-permute-start.13 = (bf16[4,32,768]{2,1,0:T(8,128)(2,1)S(1)}, bf16[4,32,768]{2,1,0:T(8,128)(2,1)S(1)}, u32[]{:S(2)}, u32[]{:S(2)}) collective-permute-start(bf16[4,32,768]{2,1,0:T(8,128)(2,1)S(1)} %collective-permute-done.9.refs_3_), channel_id=1, source_target_pairs={{0,4},{4,0},{8,12},{12,8},{16,20},{20,16},{24,28},{28,24},{1,5},{5... | collective-permute-start | bytes 589832 | tf_op jit(solution)/shard_map/ppermute | solution.py:32
  32.2 0.0 collective-permute-done.20.refs_3_
  32.3 1.4 %collective-permute-start.21 = (bf16[1,2,32,768]{3,2,1,0:T(8,128)(2,1)S(1)}, bf16[1,2,32,768]{3,2,1,0:T(8,128)(2,1)S(1)}, u32[]{:S(2)}, u32[]{:S(2)}) collective-permute-start(bf16[1,2,32,768]{3,2,1,0:T(8,128)(2,1)S(1)} %plane.3), channel_id=1, source_target_pairs={{0,16},{4,20},{8,24},{12,28},{16,0},{20,4},{24,8},{28,12},{1,17},{... | collective-permute-start | bytes 294920 | tf_op jit(solution)/shard_map/ppermute | solution.py:32
  33.6 1.1 %collective-permute-done.11.refs_5_ = bf16[4,32,768]{2,1,0:T(8,128)(2,1)S(1)} collective-permute-done((bf16[4,32,768]{2,1,0:T(8,128)(2,1)S(1)}, bf16[4,32,768]{2,1,0:T(8,128)(2,1)S(1)}, u32[]{:S(2)}, u32[]{:S(2)}) %collective-permute-start.11) | collective-permute-done | bytes 196640 | tf_op jit(solution)/shard_map/ppermute | solution.py:32
  34.7 0.9 %collective-permute-done.8.refs_2_ = bf16[4,32,768]{2,1,0:T(8,128)(2,1)S(1)} collective-permute-done((bf16[4,32,768]{2,1,0:T(8,128)(2,1)S(1)}, bf16[4,32,768]{2,1,0:T(8,128)(2,1)S(1)}, u32[]{:S(2)}, u32[]{:S(2)}) %collective-permute-start.8) | collective-permute-done | bytes 196640 | tf_op jit(solution)/shard_map/ppermute | solution.py:32
  35.6 0.1 most.1
  35.7 0.1 collective-permute-start.17
  35.8 0.5 %collective-permute-start.14 = (bf16[2,4,32,768]{3,2,1,0:T(8,128)(2,1)S(1)}, bf16[2,4,32,768]{3,2,1,0:T(8,128)(2,1)S(1)}, u32[]{:S(2)}, u32[]{:S(2)}) collective-permute-start(bf16[2,4,32,768]{3,2,1,0:T(8,128)(2,1)S(1)} %get-tuple-element.29.refs_0_), channel_id=1, source_target_pairs={{0,1},{1,0},{2,3},{3,2},{4,5},{5,4},{6,7},{7,6},{8,9},{9,8},{10,11... | collective-permute-start | bytes 1179656 | tf_op jit(solution)/shard_map/ppermute | solution.py:32
  36.3 1.4 %collective-permute-done.12.refs_1_ = bf16[4,32,768]{2,1,0:T(8,128)(2,1)S(1)} collective-permute-done((bf16[4,32,768]{2,1,0:T(8,128)(2,1)S(1)}, bf16[4,32,768]{2,1,0:T(8,128)(2,1)S(1)}, u32[]{:S(2)}, u32[]{:S(2)}) %collective-permute-start.12) | collective-permute-done | bytes 196640 | tf_op jit(solution)/shard_map/ppermute | solution.py:32
  37.7 0.5 %collective-permute-start.16 = (bf16[4,32,768]{2,1,0:T(8,128)(2,1)S(1)}, bf16[4,32,768]{2,1,0:T(8,128)(2,1)S(1)}, u32[]{:S(2)}, u32[]{:S(2)}) collective-permute-start(bf16[4,32,768]{2,1,0:T(8,128)(2,1)S(1)} %collective-permute-done.13.refs_2_), channel_id=1, source_target_pairs={{0,1},{1,0},{2,3},{3,2},{4,5},{5,4},{6,7},{7,6},{8,9},{9,8},{10,11... | collective-permute-start | bytes 589832 | tf_op jit(solution)/shard_map/ppermute | solution.py:32
  38.2 0.7 %finish.1 = f32[32,1536]{1,0:T(8,128)} custom-call(f32[2,4,32,768]{3,2,1,0:T(8,128)S(1)} %sides.1.refs_3_.refs_0_, bf16[4,32,768]{2,1,0:T(8,128)(2,1)S(1)} %collective-permute-done.18.refs_1_, bf16[4,32,768]{2,1,0:T(8,128)(2,1)S(1)} %collective-permute-done.19.refs_2_, bf16[2,2,32,768]{3,2,1,0:T(8,128)(2,1)S(1)} %collective-permute-done.20.refs_3_, ...), custom_call_target="tpu_custom_call" | custom-call | flops 40000000000 | bytes 1 | tf_op jit(solution)/shard_map/finish/pallas_call | solution.py:174
  39.0 0.0 collective-permute-done.17.refs_1_
  39.0 0.6 %project_near.1.refs_6_ = f32[128,128]{1,0:T(8,128)S(1)} custom-call(bf16[128,12288]{1,0:T(8,128)(2,1)S(1)} %copy-done, bf16[4,4,32,768]{3,2,1,0:T(8,128)(2,1)S(1)} %get-tuple-element.30.refs_0_, bf16[4,4,32,768]{3,2,1,0:T(8,128)(2,1)S(1)} %collective-permute-done.17.refs_1_), custom_call_target="tpu_custom_call" | custom-call | flops 201326592 | bytes 3145728 | tf_op jit(solution)/shard_map/project_near/pallas_call | solution.py:222
  39.5 0.0 collective-permute-done.14.refs_3_
  39.5 0.0 collective-permute-done.15.refs_4_
  39.6 1.3 %project_far.1 = bf16[128,128]{1,0:T(8,128)(2,1)} custom-call(bf16[128,12288]{1,0:T(8,128)(2,1)S(1)} %copy-done, bf16[2,4,32,768]{3,2,1,0:T(8,128)(2,1)S(1)} %get-tuple-element.29.refs_0_, bf16[4,32,768]{2,1,0:T(8,128)(2,1)S(1)} %collective-permute-done.12.refs_1_, bf16[4,32,768]{2,1,0:T(8,128)(2,1)S(1)} %collective-permute-done.13.refs_2_, ...), custom_call_target="tpu_custom_call" | custom-call | flops 201326592 | bytes 3145728 | tf_op jit(solution)/shard_map/project_far/pallas_call | solution.py:231
  (10 shorter events, 0.1 us)
Async XLA Ops:
  4.0 4.6 %collective-permute-start.1 = (bf16[4,4,32,768]{3,2,1,0:T(8,128)(2,1)S(1)}, bf16[4,4,32,768]{3,2,1,0:T(8,128)(2,1)S(1)}, u32[]{:S(2)}, u32[]{:S(2)}) collective-permute-start(bf16[4,4,32,768]{3,2,1,0:T(8,128)(2,1)S(1)} %get-tuple-element.19), channel_id=1, source_target_pairs={{0,1},{1,0},{2,3},{3,2},{4,5},{5,4},{6,7},{7,6},{8,9},{9,8},{10,11... | collective-permute-start | bytes 2359304 | tf_op jit(solution)/shard_map/ppermute | solution.py:32
  4.5 10.8 %collective-permute-start.3 = (bf16[4,4,32,768]{3,2,1,0:T(8,128)(2,1)S(1)}, bf16[4,4,32,768]{3,2,1,0:T(8,128)(2,1)S(1)}, u32[]{:S(2)}, u32[]{:S(2)}) collective-permute-start(bf16[4,4,32,768]{3,2,1,0:T(8,128)(2,1)S(1)} %get-tuple-element.22), channel_id=1, source_target_pairs={{0,1},{1,0},{2,3},{3,2},{4,5},{5,4},{6,7},{7,6},{8,9},{9,8},{10,11... | collective-permute-start | bytes 2359304 | tf_op jit(solution)/shard_map/ppermute | solution.py:32
  4.6 9.2 %collective-permute-start = (bf16[2,32,768]{2,1,0:T(8,128)(2,1)S(1)}, bf16[2,32,768]{2,1,0:T(8,128)(2,1)S(1)}, u32[]{:S(2)}, u32[]{:S(2)}) collective-permute-start(bf16[2,32,768]{2,1,0:T(8,128)(2,1)S(1)} %get-tuple-element.17.refs_0_), channel_id=1, source_target_pairs={{0,16},{4,20},{8,24},{12,28},{16,0},{20,4},{24,8},{28,12},{1,17},{... | collective-permute-start | bytes 294920 | tf_op jit(solution)/shard_map/ppermute | solution.py:32
  8.8 7.9 %collective-permute-start.6 = (bf16[1,4,32,768]{3,2,1,0:T(8,128)(2,1)S(1)}, bf16[1,4,32,768]{3,2,1,0:T(8,128)(2,1)S(1)}, u32[]{:S(2)}, u32[]{:S(2)}) collective-permute-start(bf16[1,4,32,768]{3,2,1,0:T(8,128)(2,1)S(1)} %get-tuple-element.20.refs_2_), channel_id=1, source_target_pairs={{0,4},{4,0},{8,12},{12,8},{16,20},{20,16},{24,28},{28,24},{1,5},{5... | collective-permute-start | bytes 589832 | tf_op jit(solution)/shard_map/ppermute | solution.py:32
  10.3 7.0 %collective-permute-start.7 = (bf16[4,32,768]{2,1,0:T(8,128)(2,1)S(1)}, bf16[4,32,768]{2,1,0:T(8,128)(2,1)S(1)}, u32[]{:S(2)}, u32[]{:S(2)}) collective-permute-start(bf16[4,32,768]{2,1,0:T(8,128)(2,1)S(1)} %get-tuple-element.25), channel_id=1, source_target_pairs={{0,2},{1,3},{2,0},{3,1},{4,6},{5,7},{6,4},{7,5},{8,10},{9,11},{10,... | collective-permute-start | bytes 589832 | tf_op jit(solution)/shard_map/ppermute | solution.py:32
  11.8 9.0 %collective-permute-start.4 = (bf16[4,32,768]{2,1,0:T(8,128)(2,1)S(1)}, bf16[4,32,768]{2,1,0:T(8,128)(2,1)S(1)}, u32[]{:S(2)}, u32[]{:S(2)}) collective-permute-start(bf16[4,32,768]{2,1,0:T(8,128)(2,1)S(1)} %get-tuple-element.23), channel_id=1, source_target_pairs={{0,4},{4,0},{8,12},{12,8},{16,20},{20,16},{24,28},{28,24},{1,5},{5... | collective-permute-start | bytes 589832 | tf_op jit(solution)/shard_map/ppermute | solution.py:32
  13.7 7.8 %collective-permute-start.5 = (bf16[4,32,768]{2,1,0:T(8,128)(2,1)S(1)}, bf16[4,32,768]{2,1,0:T(8,128)(2,1)S(1)}, u32[]{:S(2)}, u32[]{:S(2)}) collective-permute-start(bf16[4,32,768]{2,1,0:T(8,128)(2,1)S(1)} %get-tuple-element.24), channel_id=1, source_target_pairs={{0,2},{1,3},{2,0},{3,1},{4,6},{5,7},{6,4},{7,5},{8,10},{9,11},{10,... | collective-permute-start | bytes 589832 | tf_op jit(solution)/shard_map/ppermute | solution.py:32
  15.3 6.4 %collective-permute-start.2 = (bf16[2,2,32,768]{3,2,1,0:T(8,128)(2,1)S(1)}, bf16[2,2,32,768]{3,2,1,0:T(8,128)(2,1)S(1)}, u32[]{:S(2)}, u32[]{:S(2)}) collective-permute-start(bf16[2,2,32,768]{3,2,1,0:T(8,128)(2,1)S(1)} %widen.1.refs_4_), channel_id=1, source_target_pairs={{0,8},{4,12},{8,0},{12,4},{16,24},{20,28},{24,16},{28,20},{1,9},{5... | collective-permute-start | bytes 589832 | tf_op jit(solution)/shard_map/ppermute | solution.py:32
  17.5 7.3 %collective-permute-start.18 = (bf16[4,32,768]{2,1,0:T(8,128)(2,1)S(1)}, bf16[4,32,768]{2,1,0:T(8,128)(2,1)S(1)}, u32[]{:S(2)}, u32[]{:S(2)}) collective-permute-start(bf16[4,32,768]{2,1,0:T(8,128)(2,1)S(1)} %get-tuple-element.26.refs_4_), channel_id=1, source_target_pairs={{0,4},{4,0},{8,12},{12,8},{16,20},{20,16},{24,28},{28,24},{1,5},{5... | collective-permute-start | bytes 589832 | tf_op jit(solution)/shard_map/ppermute | solution.py:32
  18.3 7.8 %collective-permute-start.19 = (bf16[4,32,768]{2,1,0:T(8,128)(2,1)S(1)}, bf16[4,32,768]{2,1,0:T(8,128)(2,1)S(1)}, u32[]{:S(2)}, u32[]{:S(2)}) collective-permute-start(bf16[4,32,768]{2,1,0:T(8,128)(2,1)S(1)} %get-tuple-element.31), channel_id=1, source_target_pairs={{0,2},{1,3},{2,0},{3,1},{4,6},{5,7},{6,4},{7,5},{8,10},{9,11},{10,... | collective-permute-start | bytes 589832 | tf_op jit(solution)/shard_map/ppermute | solution.py:32
  21.7 16.5 %copy-start = (bf16[128,12288]{1,0:T(8,128)(2,1)S(1)}, bf16[128,12288]{1,0:T(8,128)(2,1)}, u32[]{:S(2)}) copy-start(bf16[128,12288]{1,0:T(8,128)(2,1)} %refs_5_.1) | copy-start | bytes 9437188
  21.8 8.3 %collective-permute-start.10 = (bf16[4,32,768]{2,1,0:T(8,128)(2,1)S(1)}, bf16[4,32,768]{2,1,0:T(8,128)(2,1)S(1)}, u32[]{:S(2)}, u32[]{:S(2)}) collective-permute-start(bf16[4,32,768]{2,1,0:T(8,128)(2,1)S(1)} %get-tuple-element.27.refs_0_.refs_3_), channel_id=1, source_target_pairs={{0,4},{4,0},{8,12},{12,8},{16,20},{20,16},{24,28},{28,24},{1,5},{5... | collective-permute-start | bytes 589832 | tf_op jit(solution)/shard_map/ppermute | solution.py:32
  22.9 7.6 %collective-permute-start.9 = (bf16[4,32,768]{2,1,0:T(8,128)(2,1)S(1)}, bf16[4,32,768]{2,1,0:T(8,128)(2,1)S(1)}, u32[]{:S(2)}, u32[]{:S(2)}) collective-permute-start(bf16[4,32,768]{2,1,0:T(8,128)(2,1)S(1)} %get-tuple-element.28.refs_1_), channel_id=1, source_target_pairs={{0,2},{1,3},{2,0},{3,1},{4,6},{5,7},{6,4},{7,5},{8,10},{9,11},{10,... | collective-permute-start | bytes 589832 | tf_op jit(solution)/shard_map/ppermute | solution.py:32
  26.2 6.0 %collective-permute-start.20 = (bf16[2,2,32,768]{3,2,1,0:T(8,128)(2,1)S(1)}, bf16[2,2,32,768]{3,2,1,0:T(8,128)(2,1)S(1)}, u32[]{:S(2)}, u32[]{:S(2)}) collective-permute-start(bf16[2,2,32,768]{3,2,1,0:T(8,128)(2,1)S(1)} %plane.2.refs_4_), channel_id=1, source_target_pairs={{0,8},{4,12},{8,0},{12,4},{16,24},{20,28},{24,16},{28,20},{1,9},{5... | collective-permute-start | bytes 589832 | tf_op jit(solution)/shard_map/ppermute | solution.py:32
  27.8 6.9 %collective-permute-start.11 = (bf16[4,32,768]{2,1,0:T(8,128)(2,1)S(1)}, bf16[4,32,768]{2,1,0:T(8,128)(2,1)S(1)}, u32[]{:S(2)}, u32[]{:S(2)}) collective-permute-start(bf16[4,32,768]{2,1,0:T(8,128)(2,1)S(1)} %get-tuple-element.28.refs_1_), channel_id=1, source_target_pairs={{0,4},{4,0},{8,12},{12,8},{16,20},{20,16},{24,28},{28,24},{1,5},{5... | collective-permute-start | bytes 589832 | tf_op jit(solution)/shard_map/ppermute | solution.py:32
  28.5 7.1 %collective-permute-start.8 = (bf16[4,32,768]{2,1,0:T(8,128)(2,1)S(1)}, bf16[4,32,768]{2,1,0:T(8,128)(2,1)S(1)}, u32[]{:S(2)}, u32[]{:S(2)}) collective-permute-start(bf16[4,32,768]{2,1,0:T(8,128)(2,1)S(1)} %get-tuple-element.27.refs_0_.refs_3_), channel_id=1, source_target_pairs={{0,2},{1,3},{2,0},{3,1},{4,6},{5,7},{6,4},{7,5},{8,10},{9,11},{10,... | collective-permute-start | bytes 589832 | tf_op jit(solution)/shard_map/ppermute | solution.py:32
  30.0 7.7 %collective-permute-start.12 = (bf16[4,32,768]{2,1,0:T(8,128)(2,1)S(1)}, bf16[4,32,768]{2,1,0:T(8,128)(2,1)S(1)}, u32[]{:S(2)}, u32[]{:S(2)}) collective-permute-start(bf16[4,32,768]{2,1,0:T(8,128)(2,1)S(1)} %collective-permute-done.10.refs_4_), channel_id=1, source_target_pairs={{0,2},{1,3},{2,0},{3,1},{4,6},{5,7},{6,4},{7,5},{8,10},{9,11},{10,... | collective-permute-start | bytes 589832 | tf_op jit(solution)/shard_map/ppermute | solution.py:32
  30.5 7.2 %collective-permute-start.13 = (bf16[4,32,768]{2,1,0:T(8,128)(2,1)S(1)}, bf16[4,32,768]{2,1,0:T(8,128)(2,1)S(1)}, u32[]{:S(2)}, u32[]{:S(2)}) collective-permute-start(bf16[4,32,768]{2,1,0:T(8,128)(2,1)S(1)} %collective-permute-done.9.refs_3_), channel_id=1, source_target_pairs={{0,4},{4,0},{8,12},{12,8},{16,20},{20,16},{24,28},{28,24},{1,5},{5... | collective-permute-start | bytes 589832 | tf_op jit(solution)/shard_map/ppermute | solution.py:32
  32.3 6.0 %collective-permute-start.21 = (bf16[1,2,32,768]{3,2,1,0:T(8,128)(2,1)S(1)}, bf16[1,2,32,768]{3,2,1,0:T(8,128)(2,1)S(1)}, u32[]{:S(2)}, u32[]{:S(2)}) collective-permute-start(bf16[1,2,32,768]{3,2,1,0:T(8,128)(2,1)S(1)} %plane.3), channel_id=1, source_target_pairs={{0,16},{4,20},{8,24},{12,28},{16,0},{20,4},{24,8},{28,12},{1,17},{... | collective-permute-start | bytes 294920 | tf_op jit(solution)/shard_map/ppermute | solution.py:32
  35.7 3.3 %collective-permute-start.17 = (bf16[4,4,32,768]{3,2,1,0:T(8,128)(2,1)S(1)}, bf16[4,4,32,768]{3,2,1,0:T(8,128)(2,1)S(1)}, u32[]{:S(2)}, u32[]{:S(2)}) collective-permute-start(bf16[4,4,32,768]{3,2,1,0:T(8,128)(2,1)S(1)} %get-tuple-element.30.refs_0_), channel_id=1, source_target_pairs={{0,1},{1,0},{2,3},{3,2},{4,5},{5,4},{6,7},{7,6},{8,9},{9,8},{10,11... | collective-permute-start | bytes 2359304 | tf_op jit(solution)/shard_map/ppermute | solution.py:32
  35.8 3.8 %collective-permute-start.14 = (bf16[2,4,32,768]{3,2,1,0:T(8,128)(2,1)S(1)}, bf16[2,4,32,768]{3,2,1,0:T(8,128)(2,1)S(1)}, u32[]{:S(2)}, u32[]{:S(2)}) collective-permute-start(bf16[2,4,32,768]{3,2,1,0:T(8,128)(2,1)S(1)} %get-tuple-element.29.refs_0_), channel_id=1, source_target_pairs={{0,1},{1,0},{2,3},{3,2},{4,5},{5,4},{6,7},{7,6},{8,9},{9,8},{10,11... | collective-permute-start | bytes 1179656 | tf_op jit(solution)/shard_map/ppermute | solution.py:32
  37.7 1.8 %collective-permute-start.15 = (bf16[4,32,768]{2,1,0:T(8,128)(2,1)S(1)}, bf16[4,32,768]{2,1,0:T(8,128)(2,1)S(1)}, u32[]{:S(2)}, u32[]{:S(2)}) collective-permute-start(bf16[4,32,768]{2,1,0:T(8,128)(2,1)S(1)} %collective-permute-done.12.refs_1_), channel_id=1, source_target_pairs={{0,1},{1,0},{2,3},{3,2},{4,5},{5,4},{6,7},{7,6},{8,9},{9,8},{10,11... | collective-permute-start | bytes 589832 | tf_op jit(solution)/shard_map/ppermute | solution.py:32
  37.7 1.8 %collective-permute-start.16 = (bf16[4,32,768]{2,1,0:T(8,128)(2,1)S(1)}, bf16[4,32,768]{2,1,0:T(8,128)(2,1)S(1)}, u32[]{:S(2)}, u32[]{:S(2)}) collective-permute-start(bf16[4,32,768]{2,1,0:T(8,128)(2,1)S(1)} %collective-permute-done.13.refs_2_), channel_id=1, source_target_pairs={{0,1},{1,0},{2,3},{3,2},{4,5},{5,4},{6,7},{7,6},{8,9},{9,8},{10,11... | collective-permute-start | bytes 589832 | tf_op jit(solution)/shard_map/ppermute | solution.py:32

commit v3 on v2

--- a/solution.py
+++ b/solution.py
@@ -37,71 +37,96 @@
     return pl.ds(pl.multiple_of(place, cols), cols)
 
 
-def first_kernel(ys, zs, tokens, cot, codes, scales, *refs):
-    (*made, weight, tokens_v, cot_v, codes_v, scales_v, cot_t, sems) = refs
-    rows, cols = codes.shape
+def store_products(left, tokens, x, z, ys, made):
+    refs = list(made.values())
+    rows, half = refs[0].shape[2:]
+    right = tokens[:, columns_of(x, z, 2 * half)]
+    for h in range(2):
+        names = [(c, y) for c in (1, 0) for y in range(ys) if (c, turn_of(h, x, y, ys)[0]) in made]
+        if not names:
+            continue
+        picked = [left[((1 - c) * ys + y) * rows :][:rows] for c, y in names]
+        picked = picked[0] if len(picked) == 1 else jnp.concatenate(picked, axis=0)
+        part = jnp.dot(picked, right[:, h * half : (h + 1) * half], preferred_element_type=F32).astype(BF16)
+        for i, (c, y) in enumerate(names):
+            turn, at = turn_of(h, x, y, ys)
+            made[c, turn][at, z] = part[i * rows : (i + 1) * rows]
+
+
+def first_kernel(ys, zs, tokens, cot, sent0, left, held, cot_v, cot_t, sems):
+    cols = tokens.shape[1] // (2 * zs)
+    rows = sent0.shape[2]
+    small = pltpu.make_async_copy(cot, cot_v, sems.at[0])
+    small.start()
+    order = [(x, z) for x in (1, 0) for z in range(zs)]
+    copies = []
+    for i, (x, z) in enumerate(order):
+        place = columns_of(x, z, cols)
+        copies.append(pltpu.make_async_copy(tokens.at[:, place], held.at[:, place], sems.at[1 + i]))
+        copies[-1].start()
+    small.wait()
+    cot_t[...] = cot_v[...].astype(F32).T.astype(BF16)
+    node = lax.axis_index("node")
+    picked = []
+    for core in (1, 0):
+        for y in range(ys):
+            place = lax.bitwise_xor(node, 2 * y + core) * rows
+            picked.append(cot_t[pl.ds(pl.multiple_of(place, rows), rows), :])
+    ordered = jnp.concatenate(picked, axis=0)
+    left[...] = ordered
+    for copy, (x, z) in zip(copies, order):
+        copy.wait()
+        store_products(ordered, held, x, z, ys, {(1, 0): sent0})
+
+
+def second_kernel(ys, zs, held, left, codes, scales, sent1, kept0, kept1, weight):
+    cols = codes.shape[1]
     half = cols // 2
-    fetched = []
-
-    def fetch(src, dst):
-        fetched.append(pltpu.make_async_copy(src, dst, sems.at[len(fetched)]))
-        fetched[-1].start()
-
-    for src, dst in ((cot, cot_v), (codes, codes_v), (scales, scales_v)):
-        fetch(src, dst)
-    order = [(x, z) for x in (1, 0) for z in range(zs)]
-    for x, z in order:
-        place = columns_of(x, z, cols)
-        fetch(tokens.at[:, place], tokens_v.at[:, place])
-    for copy in fetched[:3]:
-        copy.wait()
-
     blocks = cols // BLOCK
     first = lax.axis_index("wide") * blocks
     shape = (scales.shape[1], blocks)
     chosen = lax.broadcasted_iota(jnp.int32, shape, 0) == first + lax.broadcasted_iota(jnp.int32, shape, 1)
-    factor = jnp.dot(scales_v[...], chosen.astype(F32).astype(BF16), preferred_element_type=F32)
+    factor = jnp.dot(scales[...], chosen.astype(F32).astype(BF16), preferred_element_type=F32)
     for b in range(blocks):
         at = b * BLOCK
-        piece = (codes_v[:, at : at + BLOCK].astype(F32) * factor[:, b : b + 1]).astype(BF16)
-        weight[at // half, :, at % half : at % half + BLOCK] = piece
-
-    cot_t[...] = cot_v[...].astype(F32).T.astype(BF16)
-    node = lax.axis_index("node")
-    names = [(core, y) for core in (1, 0) for y in range(ys)]
-    picked = []
-    for core, y in names:
-        place = lax.bitwise_xor(node, 2 * y + core) * rows
-        picked.append(cot_t[pl.ds(pl.multiple_of(place, rows), rows), :])
-    left = jnp.concatenate(picked, axis=0)
-    for copy, (x, z) in zip(fetched[3:], order):
-        copy.wait()
-        right = tokens_v[:, columns_of(x, z, cols)]
-        for h in range(2):
-            part = jnp.dot(left, right[:, h * half : (h + 1) * half], preferred_element_type=F32).astype(BF16)
-            for i, (core, y) in enumerate(names):
-                turn, at = turn_of(h, x, y, ys)
-                made[2 * (1 - core) + turn][at, z] = part[i * rows : (i + 1) * rows]
+        piece = codes[:, at : at + BLOCK].astype(F32) * factor[:, b : b + 1]
+        weight[at // half, :, at % half : at % half + BLOCK] = piece.astype(BF16)
+    ordered = left[...]
+    for x in (1, 0):
+        for z in range(zs):
+            store_products(ordered, held, x, z, ys, {(1, 1): sent1, (0, 0): kept0, (0, 1): kept1})
 
 
 def local_products(tokens, cot, codes, scales, ys, zs):
     rows, cols = codes.shape
     half = cols // 2
-    operands = (tokens, cot, codes, scales)
     blocks = [jax.ShapeDtypeStruct((n, zs, rows, half), BF16) for n in (3 * ys - 2, ys + 2)]
-    return pl.pallas_call(
+    turned = jax.ShapeDtypeStruct(cot.shape[::-1], BF16)
+    cost = pl.CostEstimate(flops=tokens.size * cot.shape[1], bytes_accessed=3 * tokens.size, transcendentals=0)
+    sent0, left, held = pl.pallas_call(
         functools.partial(first_kernel, ys, zs),
-        out_shape=(*blocks, *blocks, jax.ShapeDtypeStruct((2, rows, half), BF16)),
-        in_specs=[ANY] * 4,
-        out_specs=(VMEM,) * 5,
-        scratch_shapes=[pltpu.VMEM(a.shape, BF16) for a in operands]
-        + [pltpu.VMEM(cot.shape[::-1], BF16), pltpu.SemaphoreType.DMA((3 + 2 * zs,))],
-        compiler_params=PARAMS,
-        cost_estimate=pl.CostEstimate(
-            flops=2 * tokens.size * cot.shape[1], bytes_accessed=4 * tokens.size, transcendentals=0
-        ),
+        out_shape=(blocks[0], turned, jax.ShapeDtypeStruct(tokens.shape, BF16)),
+        in_specs=[ANY] * 2,
+        out_specs=(VMEM,) * 3,
+        scratch_shapes=[
+            pltpu.VMEM(cot.shape, BF16),
+            pltpu.VMEM(turned.shape, BF16),
+            pltpu.SemaphoreType.DMA((1 + 2 * zs,)),
+        ],
+        compiler_params=PARAMS,
+        cost_estimate=cost,
         name="first",
-    )(*[pltpu.with_memory_space_constraint(a, pltpu.HBM) for a in operands])
+    )(*[pltpu.with_memory_space_constraint(a, pltpu.HBM) for a in (tokens, cot)])
+    sent1, kept0, kept1, weight = pl.pallas_call(
+        functools.partial(second_kernel, ys, zs),
+        out_shape=(blocks[1], *blocks, jax.ShapeDtypeStruct((2, rows, half), BF16)),
+        in_specs=[VMEM] * 4,
+        out_specs=(VMEM,) * 4,
+        compiler_params=PARAMS,
+        cost_estimate=cost,
+        name="second",
+    )(held, left, codes, scales)
+    return sent0, sent1, kept0, kept1, weight
 
 
 def plain_products(tokens, cot, codes, scales, ys, zs):
@@ -187,7 +212,7 @@
         (*weights, out) = refs
         total = 0.0
     else:
-        (*weights, earlier, out, total_t) = refs
+        (earlier, *weights, out, total_t) = refs
         total = earlier[...]
     count = len(weights) // 2
     rows, half = weights[0].shape[2:]
@@ -237,7 +262,7 @@
         compiler_params=PARAMS,
         cost_estimate=cost,
         name="project_far",
-    )(tokens, *far, earlier)
+    )(tokens, earlier, *far)
 
 
 def plain_project(tokens, near, far, ys, zs):
@@ -297,15 +322,15 @@
 
     outs = [((ys - 1, *one), [((y - 1,), pair(1, 1, y)) for y in others])]
     outs += [(one, [(whole, pair(0, 1, y))]) for y in others]
+    outs += [(one, [(whole, pair(0, 0, y))]) for y in others]
     outs += [(one, [(whole, pair(1, 1, 0))])]
-    outs += [(one, [(whole, pair(0, 0, y))]) for y in others]
     diag_x, *rest = add_up(outs, [kept0, got0], name="stage1")
     after = [diag_x]
-    diag_y, side_x, side_y = rest[: ys - 1], rest[ys - 1], rest[ys:]
+    diag_y, side_y, side_x = rest[: ys - 1], rest[ys - 1 : -1], rest[-1]
     diag_x = x_flip(diag_x)
     diag_y = [y_flip(d, y) for y, d in zip(others, diag_y)]
+    side_y = [y_flip(d, y) for y, d in zip(others, side_y)]
     side_x = x_flip(side_x)
-    side_y = [y_flip(d, y) for y, d in zip(others, side_y)]
 
     step = zs // 4
     while step:
@@ -325,11 +350,11 @@
     last_y = [y_flip(d, y) for y, d in zip(others, last_y)]
 
     sums = [
-        pair(0, 0, 0) + [(2 + y, whole) for y in others],
-        pair(1, 0, 0) + [(2, whole)],
+        pair(0, 0, 0) + [(1 + y, whole) for y in others],
+        pair(1, 0, 0) + [(1 + ys, whole)],
     ]
     outs = [((2, *one), [((h,), sums[h]) for h in range(2)])]
-    (base,) = add_up(outs, [kept1, got1, side_x, *side_y], [after], name="sides", kind=F32)
+    (base,) = add_up(outs, [kept1, got1, *side_y, side_x], [after], name="sides", kind=F32)
 
     outs = [(one, [((z,), [(a, i + (h,))]) for z, (a, i) in zip(offsets, places)]) for h in range(2)]
     own = list(add_up(outs, held, [base], name="own"))
@@ -357,10 +382,9 @@
         step *= 2
     weight_grad = finish([sums[0, 0], sums[0, 1]], arrays, tokens)
 
-    held = own + [e for es in on_y for e in es] + on_x
-    groups = [range(2 * ys), range(2 * ys, 2 * ys + 2)]
-    outs = [((len(g), *one), [((i - g[0],), [(i, whole)]) for i in g]) for g in groups]
-    near, side = add_up(outs, held, name="most")
+    held = own + [e for es in on_y for e in es]
+    (near,) = add_up([((2 * ys, *one), [((i,), [(i, whole)]) for i in range(2 * ys)])], held, name="near")
+    (side,) = add_up([((2, *one), [((h,), [(h, whole)]) for h in range(2)])], on_x, [near], name="side")
     ends = [d for ds in diag for d in ds]
     near = [near, core_flip(near)]
     far = [side, *ends, core_flip(side), *[core_flip(e) for e in ends]]

time: 41 us -> 41.2 us (level)
  waiting for transfers between devices: 9.2 us -> 9.88 us
  starting transfers between devices: 24.3 us -> 23.8 us
    ppermute x22, waiting for transfers between devices: 9.2 us -> 9.88 us  [flip(): return lax.ppermute(entries, axis, [(i, i ^ offset) for i in range(size)])]
    ppermute x22, starting transfers between devices: 24.3 us -> 23.8 us  [flip(): return lax.ppermute(entries, axis, [(i, i ^ offset) for i in range(size)])]
    pallas_call x1 -> x2, Pallas kernels: 3.33 us -> 3.37 us  [the longest x1 2.6 us: local_products(): pl.pallas_call(functools.partial(first_kernel, ys, zs), out_shape=(blocks...]
  transfers between devices with their start and end apart: 22 -> 22, of which waited for: 9 -> 9; matrix products, arithmetic and copies ran while one was open for 0% -> 0% of each run, Pallas kernels for 5% -> 7%
where the time goes in v3:
time: 41.2 us; the launch traced here: 41.1 us
  starting transfers between devices  23.8 us (58%)
  waiting for transfers between devices  9.88 us (24%)
  Pallas kernels  6.63 us (16%)
  between operations  0.78 us (2%)
    ppermute x22, starting transfers between devices, flip(): return lax.ppermute(entries, axis, [(i, i ^ offset) for i in range(size)])  23.8 us
    ppermute x22, waiting for transfers between devices, flip(): return lax.ppermute(entries, axis, [(i, i ^ offset) for i in range(size)])  9.88 us
    pallas_call x1, Pallas kernels, local_products(): pl.pallas_call(functools.partial(first_kernel, ys, zs), out_shape=(blocks...  2.6 us
    pallas_call x1, Pallas kernels, project(): pl.pallas_call(functools.partial(project_kernel, ys, zs, 1), out_shape=ja...  1.32 us
  transfers between devices with their start and end apart: 22, of which 9 were waited for; matrix products, arithmetic and copies ran while one was open for 0% of the time, Pallas kernels for 7%

profile of v3, /device:TPU:0, one launch (start us, length us, event | category | flops | bytes accessed | tf_op | source)
XLA Modules:
  0.0 41.1 jit_solution(11865408735315954177)
XLA Ops:
  0.7 2.6 %first.1 = (bf16[4,4,32,768]{3,2,1,0:T(8,128)(2,1)S(1)}, bf16[128,128]{1,0:T(8,128)(2,1)S(1)}, bf16[128,12288]{1,0:T(8,128)(2,1)S(1)}) custom-call(bf16[128,12288]{1,0:T(8,128)(2,1)} %refs_5_.1, bf16[128,128]{1,0:T(8,128)(2,1)} %cot.1), custom_call_target="tpu_custom_call" | custom-call | flops 201326592 | bytes 4718592 | tf_op jit(solution)/shard_map/first/pallas_call | solution.py:106
  3.3 0.5 %collective-permute-start.1 = (bf16[4,4,32,768]{3,2,1,0:T(8,128)(2,1)S(1)}, bf16[4,4,32,768]{3,2,1,0:T(8,128)(2,1)S(1)}, u32[]{:S(2)}, u32[]{:S(2)}) collective-permute-start(bf16[4,4,32,768]{3,2,1,0:T(8,128)(2,1)S(1)} %get-tuple-element.21), channel_id=1, source_target_pairs={{0,1},{1,0},{2,3},{3,2},{4,5},{5,4},{6,7},{7,6},{8,9},{9,8},{10,11... | collective-permute-start | bytes 2359304 | tf_op jit(solution)/shard_map/ppermute | solution.py:32
  3.8 0.8 %second.1 = (bf16[4,4,32,768]{3,2,1,0:T(8,128)(2,1)S(1)}, bf16[4,4,32,768]{3,2,1,0:T(8,128)(2,1)S(1)}, bf16[4,4,32,768]{3,2,1,0:T(8,128)(2,1)S(1)}, bf16[2,32,768]{2,1,0:T(8,128)(2,1)S(1)}) custom-call(bf16[128,12288]{1,0:T(8,128)(2,1)S(1)} %get-tuple-element.17.held, bf16[128,128]{1,0:T(8,128)(2,1)S(1)} %get-tuple-element.18.left, ...), custom_call_target="tpu_custom_call" | custom-call | flops 201326592 | bytes 4718592 | tf_op jit(solution)/shard_map/second/pallas_call | solution.py:120
  4.6 0.1 collective-permute-start.3
  4.7 4.0 %collective-permute-start = (bf16[2,32,768]{2,1,0:T(8,128)(2,1)S(1)}, bf16[2,32,768]{2,1,0:T(8,128)(2,1)S(1)}, u32[]{:S(2)}, u32[]{:S(2)}) collective-permute-start(bf16[2,32,768]{2,1,0:T(8,128)(2,1)S(1)} %get-tuple-element.19.refs_0_), channel_id=1, source_target_pairs={{0,16},{4,20},{8,24},{12,28},{16,0},{20,4},{24,8},{28,12},{1,17},{... | collective-permute-start | bytes 294920 | tf_op jit(solution)/shard_map/ppermute | solution.py:32
  8.7 0.0 collective-permute-done.1.refs_1_
  8.7 0.2 stage1.1
  8.9 1.6 %collective-permute-start.7 = (bf16[4,32,768]{2,1,0:T(8,128)(2,1)S(1)}, bf16[4,32,768]{2,1,0:T(8,128)(2,1)S(1)}, u32[]{:S(2)}, u32[]{:S(2)}) collective-permute-start(bf16[4,32,768]{2,1,0:T(8,128)(2,1)S(1)} %get-tuple-element.27), channel_id=1, source_target_pairs={{0,2},{1,3},{2,0},{3,1},{4,6},{5,7},{6,4},{7,5},{8,10},{9,11},{10,... | collective-permute-start | bytes 589832 | tf_op jit(solution)/shard_map/ppermute | solution.py:32
  10.5 1.5 %collective-permute-start.6 = (bf16[1,4,32,768]{3,2,1,0:T(8,128)(2,1)S(1)}, bf16[1,4,32,768]{3,2,1,0:T(8,128)(2,1)S(1)}, u32[]{:S(2)}, u32[]{:S(2)}) collective-permute-start(bf16[1,4,32,768]{3,2,1,0:T(8,128)(2,1)S(1)} %get-tuple-element.22.refs_2_), channel_id=1, source_target_pairs={{0,4},{4,0},{8,12},{12,8},{16,20},{20,16},{24,28},{28,24},{1,5},{5... | collective-permute-start | bytes 589832 | tf_op jit(solution)/shard_map/ppermute | solution.py:32
  12.0 0.5 %collective-permute-start.4 = (bf16[4,32,768]{2,1,0:T(8,128)(2,1)S(1)}, bf16[4,32,768]{2,1,0:T(8,128)(2,1)S(1)}, u32[]{:S(2)}, u32[]{:S(2)}) collective-permute-start(bf16[4,32,768]{2,1,0:T(8,128)(2,1)S(1)} %get-tuple-element.25), channel_id=1, source_target_pairs={{0,2},{1,3},{2,0},{3,1},{4,6},{5,7},{6,4},{7,5},{8,10},{9,11},{10,... | collective-permute-start | bytes 589832 | tf_op jit(solution)/shard_map/ppermute | solution.py:32
  12.5 1.4 %collective-permute-done.refs_1_ = bf16[2,32,768]{2,1,0:T(8,128)(2,1)S(1)} collective-permute-done((bf16[2,32,768]{2,1,0:T(8,128)(2,1)S(1)}, bf16[2,32,768]{2,1,0:T(8,128)(2,1)S(1)}, u32[]{:S(2)}, u32[]{:S(2)}) %collective-permute-start) | collective-permute-done | bytes 98336 | tf_op jit(solution)/shard_map/ppermute | solution.py:32
  13.9 1.5 %collective-permute-start.5 = (bf16[4,32,768]{2,1,0:T(8,128)(2,1)S(1)}, bf16[4,32,768]{2,1,0:T(8,128)(2,1)S(1)}, u32[]{:S(2)}, u32[]{:S(2)}) collective-permute-start(bf16[4,32,768]{2,1,0:T(8,128)(2,1)S(1)} %get-tuple-element.26), channel_id=1, source_target_pairs={{0,4},{4,0},{8,12},{12,8},{16,20},{20,16},{24,28},{28,24},{1,5},{5... | collective-permute-start | bytes 589832 | tf_op jit(solution)/shard_map/ppermute | solution.py:32
  15.4 0.0 collective-permute-done.3.refs_1_
  15.4 0.7 %collective-permute-start.2 = (bf16[2,2,32,768]{3,2,1,0:T(8,128)(2,1)S(1)}, bf16[2,2,32,768]{3,2,1,0:T(8,128)(2,1)S(1)}, u32[]{:S(2)}, u32[]{:S(2)}) collective-permute-start(bf16[2,2,32,768]{3,2,1,0:T(8,128)(2,1)S(1)} %widen.1.refs_4_), channel_id=1, source_target_pairs={{0,8},{4,12},{8,0},{12,4},{16,24},{20,28},{24,16},{28,20},{1,9},{5... | collective-permute-start | bytes 589832 | tf_op jit(solution)/shard_map/ppermute | solution.py:32
  16.2 0.6 %collective-permute-done.7.refs_3_ = bf16[4,32,768]{2,1,0:T(8,128)(2,1)S(1)} collective-permute-done((bf16[4,32,768]{2,1,0:T(8,128)(2,1)S(1)}, bf16[4,32,768]{2,1,0:T(8,128)(2,1)S(1)}, u32[]{:S(2)}, u32[]{:S(2)}) %collective-permute-start.7) | collective-permute-done | bytes 196640 | tf_op jit(solution)/shard_map/ppermute | solution.py:32
  16.8 0.8 %collective-permute-done.6.refs_2_ = bf16[1,4,32,768]{3,2,1,0:T(8,128)(2,1)S(1)} collective-permute-done((bf16[1,4,32,768]{3,2,1,0:T(8,128)(2,1)S(1)}, bf16[1,4,32,768]{3,2,1,0:T(8,128)(2,1)S(1)}, u32[]{:S(2)}, u32[]{:S(2)}) %collective-permute-start.6) | collective-permute-done | bytes 196640 | tf_op jit(solution)/shard_map/ppermute | solution.py:32
  17.5 0.1 stage2.1
  17.7 0.8 %collective-permute-start.19 = (bf16[4,32,768]{2,1,0:T(8,128)(2,1)S(1)}, bf16[4,32,768]{2,1,0:T(8,128)(2,1)S(1)}, u32[]{:S(2)}, u32[]{:S(2)}) collective-permute-start(bf16[4,32,768]{2,1,0:T(8,128)(2,1)S(1)} %get-tuple-element.31), channel_id=1, source_target_pairs={{0,2},{1,3},{2,0},{3,1},{4,6},{5,7},{6,4},{7,5},{8,10},{9,11},{10,... | collective-permute-start | bytes 589832 | tf_op jit(solution)/shard_map/ppermute | solution.py:32
  18.5 1.5 %collective-permute-start.18 = (bf16[4,32,768]{2,1,0:T(8,128)(2,1)S(1)}, bf16[4,32,768]{2,1,0:T(8,128)(2,1)S(1)}, u32[]{:S(2)}, u32[]{:S(2)}) collective-permute-start(bf16[4,32,768]{2,1,0:T(8,128)(2,1)S(1)} %get-tuple-element.28.refs_4_), channel_id=1, source_target_pairs={{0,4},{4,0},{8,12},{12,8},{16,20},{20,16},{24,28},{28,24},{1,5},{5... | collective-permute-start | bytes 589832 | tf_op jit(solution)/shard_map/ppermute | solution.py:32
  20.0 1.0 %collective-permute-done.4.refs_2_ = bf16[4,32,768]{2,1,0:T(8,128)(2,1)S(1)} collective-permute-done((bf16[4,32,768]{2,1,0:T(8,128)(2,1)S(1)}, bf16[4,32,768]{2,1,0:T(8,128)(2,1)S(1)}, u32[]{:S(2)}, u32[]{:S(2)}) %collective-permute-start.4) | collective-permute-done | bytes 196640 | tf_op jit(solution)/shard_map/ppermute | solution.py:32
  21.0 0.8 %collective-permute-done.5.refs_3_ = bf16[4,32,768]{2,1,0:T(8,128)(2,1)S(1)} collective-permute-done((bf16[4,32,768]{2,1,0:T(8,128)(2,1)S(1)}, bf16[4,32,768]{2,1,0:T(8,128)(2,1)S(1)}, u32[]{:S(2)}, u32[]{:S(2)}) %collective-permute-start.5) | collective-permute-done | bytes 196640 | tf_op jit(solution)/shard_map/ppermute | solution.py:32
  21.8 0.1 sides.1.refs_3_.refs_0_
  21.9 0.0 collective-permute-done.2.refs_2_
  21.9 1.1 %collective-permute-start.9 = (bf16[4,32,768]{2,1,0:T(8,128)(2,1)S(1)}, bf16[4,32,768]{2,1,0:T(8,128)(2,1)S(1)}, u32[]{:S(2)}, u32[]{:S(2)}) collective-permute-start(bf16[4,32,768]{2,1,0:T(8,128)(2,1)S(1)} %get-tuple-element.30.refs_1_), channel_id=1, source_target_pairs={{0,2},{1,3},{2,0},{3,1},{4,6},{5,7},{6,4},{7,5},{8,10},{9,11},{10,... | collective-permute-start | bytes 589832 | tf_op jit(solution)/shard_map/ppermute | solution.py:32
  23.1 1.8 %collective-permute-start.11 = (bf16[4,32,768]{2,1,0:T(8,128)(2,1)S(1)}, bf16[4,32,768]{2,1,0:T(8,128)(2,1)S(1)}, u32[]{:S(2)}, u32[]{:S(2)}) collective-permute-start(bf16[4,32,768]{2,1,0:T(8,128)(2,1)S(1)} %get-tuple-element.29.refs_0_.refs_3_), channel_id=1, source_target_pairs={{0,4},{4,0},{8,12},{12,8},{16,20},{20,16},{24,28},{28,24},{1,5},{5... | collective-permute-start | bytes 589832 | tf_op jit(solution)/shard_map/ppermute | solution.py:32
  24.9 0.0 collective-permute-done.19.refs_2_
  24.9 1.5 %collective-permute-done.18.refs_1_ = bf16[4,32,768]{2,1,0:T(8,128)(2,1)S(1)} collective-permute-done((bf16[4,32,768]{2,1,0:T(8,128)(2,1)S(1)}, bf16[4,32,768]{2,1,0:T(8,128)(2,1)S(1)}, u32[]{:S(2)}, u32[]{:S(2)}) %collective-permute-start.18) | collective-permute-done | bytes 196640 | tf_op jit(solution)/shard_map/ppermute | solution.py:32
  26.4 1.7 %collective-permute-start.20 = (bf16[2,2,32,768]{3,2,1,0:T(8,128)(2,1)S(1)}, bf16[2,2,32,768]{3,2,1,0:T(8,128)(2,1)S(1)}, u32[]{:S(2)}, u32[]{:S(2)}) collective-permute-start(bf16[2,2,32,768]{3,2,1,0:T(8,128)(2,1)S(1)} %plane.2.refs_4_), channel_id=1, source_target_pairs={{0,8},{4,12},{8,0},{12,4},{16,24},{20,28},{24,16},{28,20},{1,9},{5... | collective-permute-start | bytes 589832 | tf_op jit(solution)/shard_map/ppermute | solution.py:32
  28.0 0.7 %collective-permute-start.8 = (bf16[4,32,768]{2,1,0:T(8,128)(2,1)S(1)}, bf16[4,32,768]{2,1,0:T(8,128)(2,1)S(1)}, u32[]{:S(2)}, u32[]{:S(2)}) collective-permute-start(bf16[4,32,768]{2,1,0:T(8,128)(2,1)S(1)} %get-tuple-element.29.refs_0_.refs_3_), channel_id=1, source_target_pairs={{0,2},{1,3},{2,0},{3,1},{4,6},{5,7},{6,4},{7,5},{8,10},{9,11},{10,... | collective-permute-start | bytes 589832 | tf_op jit(solution)/shard_map/ppermute | solution.py:32
  28.8 1.5 %collective-permute-start.12 = (bf16[4,32,768]{2,1,0:T(8,128)(2,1)S(1)}, bf16[4,32,768]{2,1,0:T(8,128)(2,1)S(1)}, u32[]{:S(2)}, u32[]{:S(2)}) collective-permute-start(bf16[4,32,768]{2,1,0:T(8,128)(2,1)S(1)} %get-tuple-element.30.refs_1_), channel_id=1, source_target_pairs={{0,4},{4,0},{8,12},{12,8},{16,20},{20,16},{24,28},{28,24},{1,5},{5... | collective-permute-start | bytes 589832 | tf_op jit(solution)/shard_map/ppermute | solution.py:32
  30.3 0.5 %collective-permute-start.14 = (bf16[4,32,768]{2,1,0:T(8,128)(2,1)S(1)}, bf16[4,32,768]{2,1,0:T(8,128)(2,1)S(1)}, u32[]{:S(2)}, u32[]{:S(2)}) collective-permute-start(bf16[4,32,768]{2,1,0:T(8,128)(2,1)S(1)} %collective-permute-done.9.refs_3_), channel_id=1, source_target_pairs={{0,4},{4,0},{8,12},{12,8},{16,20},{20,16},{24,28},{28,24},{1,5},{5... | collective-permute-start | bytes 589832 | tf_op jit(solution)/shard_map/ppermute | solution.py:32
  30.8 0.0 collective-permute-done.11.refs_0_
  30.8 1.6 %collective-permute-start.13 = (bf16[4,32,768]{2,1,0:T(8,128)(2,1)S(1)}, bf16[4,32,768]{2,1,0:T(8,128)(2,1)S(1)}, u32[]{:S(2)}, u32[]{:S(2)}) collective-permute-start(bf16[4,32,768]{2,1,0:T(8,128)(2,1)S(1)} %collective-permute-done.11.refs_0_), channel_id=1, source_target_pairs={{0,2},{1,3},{2,0},{3,1},{4,6},{5,7},{6,4},{7,5},{8,10},{9,11},{10,... | collective-permute-start | bytes 589832 | tf_op jit(solution)/shard_map/ppermute | solution.py:32
  32.4 1.3 %collective-permute-start.21 = (bf16[1,2,32,768]{3,2,1,0:T(8,128)(2,1)S(1)}, bf16[1,2,32,768]{3,2,1,0:T(8,128)(2,1)S(1)}, u32[]{:S(2)}, u32[]{:S(2)}) collective-permute-start(bf16[1,2,32,768]{3,2,1,0:T(8,128)(2,1)S(1)} %plane.3), channel_id=1, source_target_pairs={{0,16},{4,20},{8,24},{12,28},{16,0},{20,4},{24,8},{28,12},{1,17},{... | collective-permute-start | bytes 294920 | tf_op jit(solution)/shard_map/ppermute | solution.py:32
  33.7 1.2 %collective-permute-done.8.refs_2_ = bf16[4,32,768]{2,1,0:T(8,128)(2,1)S(1)} collective-permute-done((bf16[4,32,768]{2,1,0:T(8,128)(2,1)S(1)}, bf16[4,32,768]{2,1,0:T(8,128)(2,1)S(1)}, u32[]{:S(2)}, u32[]{:S(2)}) %collective-permute-start.8) | collective-permute-done | bytes 196640 | tf_op jit(solution)/shard_map/ppermute | solution.py:32
  34.9 0.1 near.1.refs_0_.refs_2_
  35.0 0.1 collective-permute-start.10
  35.0 0.7 %collective-permute-done.12.refs_1_ = bf16[4,32,768]{2,1,0:T(8,128)(2,1)S(1)} collective-permute-done((bf16[4,32,768]{2,1,0:T(8,128)(2,1)S(1)}, bf16[4,32,768]{2,1,0:T(8,128)(2,1)S(1)}, u32[]{:S(2)}, u32[]{:S(2)}) %collective-permute-start.12) | collective-permute-done | bytes 196640 | tf_op jit(solution)/shard_map/ppermute | solution.py:32
  35.8 0.1 collective-permute-start.15
  35.9 2.0 %collective-permute-done.14.refs_3_ = bf16[4,32,768]{2,1,0:T(8,128)(2,1)S(1)} collective-permute-done((bf16[4,32,768]{2,1,0:T(8,128)(2,1)S(1)}, bf16[4,32,768]{2,1,0:T(8,128)(2,1)S(1)}, u32[]{:S(2)}, u32[]{:S(2)}) %collective-permute-start.14) | collective-permute-done | bytes 196640 | tf_op jit(solution)/shard_map/ppermute | solution.py:32
  37.9 0.0 collective-permute-start.17
  37.9 0.0 collective-permute-done.13.refs_2_
  37.9 0.5 %collective-permute-start.16 = (bf16[4,32,768]{2,1,0:T(8,128)(2,1)S(1)}, bf16[4,32,768]{2,1,0:T(8,128)(2,1)S(1)}, u32[]{:S(2)}, u32[]{:S(2)}) collective-permute-start(bf16[4,32,768]{2,1,0:T(8,128)(2,1)S(1)} %collective-permute-done.13.refs_2_), channel_id=1, source_target_pairs={{0,1},{1,0},{2,3},{3,2},{4,5},{5,4},{6,7},{7,6},{8,9},{9,8},{10,11... | collective-permute-start | bytes 589832 | tf_op jit(solution)/shard_map/ppermute | solution.py:32
  38.4 0.0 collective-permute-done.21.refs_4_
  38.4 0.7 %finish.1 = f32[32,1536]{1,0:T(8,128)} custom-call(f32[2,4,32,768]{3,2,1,0:T(8,128)S(1)} %sides.1.refs_3_.refs_0_, bf16[4,32,768]{2,1,0:T(8,128)(2,1)S(1)} %collective-permute-done.18.refs_1_, bf16[4,32,768]{2,1,0:T(8,128)(2,1)S(1)} %collective-permute-done.19.refs_2_, bf16[2,2,32,768]{3,2,1,0:T(8,128)(2,1)S(1)} %collective-permute-done.20.refs_3_, ...), custom_call_target="tpu_custom_call" | custom-call | flops 40000000000 | bytes 1 | tf_op jit(solution)/shard_map/finish/pallas_call | solution.py:199
  39.1 0.6 %project_near.1.refs_0_ = f32[128,128]{1,0:T(8,128)S(1)} custom-call(bf16[128,12288]{1,0:T(8,128)(2,1)S(1)} %copy-done, bf16[4,4,32,768]{3,2,1,0:T(8,128)(2,1)S(1)} %near.1.refs_0_.refs_2_, bf16[4,4,32,768]{3,2,1,0:T(8,128)(2,1)S(1)} %collective-permute-done.10.refs_1_), custom_call_target="tpu_custom_call" | custom-call | flops 201326592 | bytes 3145728 | tf_op jit(solution)/shard_map/project_near/pallas_call | solution.py:247
  39.7 0.0 collective-permute-done.17.refs_6_
  39.7 1.3 %project_far.1 = bf16[128,128]{1,0:T(8,128)(2,1)} custom-call(bf16[128,12288]{1,0:T(8,128)(2,1)S(1)} %copy-done, f32[128,128]{1,0:T(8,128)S(1)} %project_near.1.refs_0_, bf16[2,4,32,768]{3,2,1,0:T(8,128)(2,1)S(1)} %side.1.refs_1_, bf16[4,32,768]{2,1,0:T(8,128)(2,1)S(1)} %collective-permute-done.13.refs_2_, ...), custom_call_target="tpu_custom_call" | custom-call | flops 201326592 | bytes 3145728 | tf_op jit(solution)/shard_map/project_far/pallas_call | solution.py:256
  (16 shorter events, 0.2 us)
Async XLA Ops:
  0.6 3.1 %copy-start.2 = (bf16[96,32]{0,1:T(8,128)(2,1)S(1)}, bf16[96,32]{0,1:T(8,128)(2,1)}, u32[]{:S(2)}) copy-start(bf16[96,32]{0,1:T(8,128)(2,1)} %param.6) | copy-start | bytes 18436
  0.6 3.1 %copy-start.1 = (bf16[1536,32]{0,1:T(8,128)(2,1)S(1)}, bf16[1536,32]{0,1:T(8,128)(2,1)}, u32[]{:S(2)}) copy-start(bf16[1536,32]{0,1:T(8,128)(2,1)} %param.5) | copy-start | bytes 294916
  3.3 5.5 %collective-permute-start.1 = (bf16[4,4,32,768]{3,2,1,0:T(8,128)(2,1)S(1)}, bf16[4,4,32,768]{3,2,1,0:T(8,128)(2,1)S(1)}, u32[]{:S(2)}, u32[]{:S(2)}) collective-permute-start(bf16[4,4,32,768]{3,2,1,0:T(8,128)(2,1)S(1)} %get-tuple-element.21), channel_id=1, source_target_pairs={{0,1},{1,0},{2,3},{3,2},{4,5},{5,4},{6,7},{7,6},{8,9},{9,8},{10,11... | collective-permute-start | bytes 2359304 | tf_op jit(solution)/shard_map/ppermute | solution.py:32
  4.6 10.9 %collective-permute-start.3 = (bf16[4,4,32,768]{3,2,1,0:T(8,128)(2,1)S(1)}, bf16[4,4,32,768]{3,2,1,0:T(8,128)(2,1)S(1)}, u32[]{:S(2)}, u32[]{:S(2)}) collective-permute-start(bf16[4,4,32,768]{3,2,1,0:T(8,128)(2,1)S(1)} %get-tuple-element.24), channel_id=1, source_target_pairs={{0,1},{1,0},{2,3},{3,2},{4,5},{5,4},{6,7},{7,6},{8,9},{9,8},{10,11... | collective-permute-start | bytes 2359304 | tf_op jit(solution)/shard_map/ppermute | solution.py:32
  4.7 9.2 %collective-permute-start = (bf16[2,32,768]{2,1,0:T(8,128)(2,1)S(1)}, bf16[2,32,768]{2,1,0:T(8,128)(2,1)S(1)}, u32[]{:S(2)}, u32[]{:S(2)}) collective-permute-start(bf16[2,32,768]{2,1,0:T(8,128)(2,1)S(1)} %get-tuple-element.19.refs_0_), channel_id=1, source_target_pairs={{0,16},{4,20},{8,24},{12,28},{16,0},{20,4},{24,8},{28,12},{1,17},{... | collective-permute-start | bytes 294920 | tf_op jit(solution)/shard_map/ppermute | solution.py:32
  8.9 7.9 %collective-permute-start.7 = (bf16[4,32,768]{2,1,0:T(8,128)(2,1)S(1)}, bf16[4,32,768]{2,1,0:T(8,128)(2,1)S(1)}, u32[]{:S(2)}, u32[]{:S(2)}) collective-permute-start(bf16[4,32,768]{2,1,0:T(8,128)(2,1)S(1)} %get-tuple-element.27), channel_id=1, source_target_pairs={{0,2},{1,3},{2,0},{3,1},{4,6},{5,7},{6,4},{7,5},{8,10},{9,11},{10,... | collective-permute-start | bytes 589832 | tf_op jit(solution)/shard_map/ppermute | solution.py:32
  10.5 7.1 %collective-permute-start.6 = (bf16[1,4,32,768]{3,2,1,0:T(8,128)(2,1)S(1)}, bf16[1,4,32,768]{3,2,1,0:T(8,128)(2,1)S(1)}, u32[]{:S(2)}, u32[]{:S(2)}) collective-permute-start(bf16[1,4,32,768]{3,2,1,0:T(8,128)(2,1)S(1)} %get-tuple-element.22.refs_2_), channel_id=1, source_target_pairs={{0,4},{4,0},{8,12},{12,8},{16,20},{20,16},{24,28},{28,24},{1,5},{5... | collective-permute-start | bytes 589832 | tf_op jit(solution)/shard_map/ppermute | solution.py:32
  12.0 9.0 %collective-permute-start.4 = (bf16[4,32,768]{2,1,0:T(8,128)(2,1)S(1)}, bf16[4,32,768]{2,1,0:T(8,128)(2,1)S(1)}, u32[]{:S(2)}, u32[]{:S(2)}) collective-permute-start(bf16[4,32,768]{2,1,0:T(8,128)(2,1)S(1)} %get-tuple-element.25), channel_id=1, source_target_pairs={{0,2},{1,3},{2,0},{3,1},{4,6},{5,7},{6,4},{7,5},{8,10},{9,11},{10,... | collective-permute-start | bytes 589832 | tf_op jit(solution)/shard_map/ppermute | solution.py:32
  13.9 7.9 %collective-permute-start.5 = (bf16[4,32,768]{2,1,0:T(8,128)(2,1)S(1)}, bf16[4,32,768]{2,1,0:T(8,128)(2,1)S(1)}, u32[]{:S(2)}, u32[]{:S(2)}) collective-permute-start(bf16[4,32,768]{2,1,0:T(8,128)(2,1)S(1)} %get-tuple-element.26), channel_id=1, source_target_pairs={{0,4},{4,0},{8,12},{12,8},{16,20},{20,16},{24,28},{28,24},{1,5},{5... | collective-permute-start | bytes 589832 | tf_op jit(solution)/shard_map/ppermute | solution.py:32
  15.4 6.5 %collective-permute-start.2 = (bf16[2,2,32,768]{3,2,1,0:T(8,128)(2,1)S(1)}, bf16[2,2,32,768]{3,2,1,0:T(8,128)(2,1)S(1)}, u32[]{:S(2)}, u32[]{:S(2)}) collective-permute-start(bf16[2,2,32,768]{3,2,1,0:T(8,128)(2,1)S(1)} %widen.1.refs_4_), channel_id=1, source_target_pairs={{0,8},{4,12},{8,0},{12,4},{16,24},{20,28},{24,16},{28,20},{1,9},{5... | collective-permute-start | bytes 589832 | tf_op jit(solution)/shard_map/ppermute | solution.py:32
  17.7 7.2 %collective-permute-start.19 = (bf16[4,32,768]{2,1,0:T(8,128)(2,1)S(1)}, bf16[4,32,768]{2,1,0:T(8,128)(2,1)S(1)}, u32[]{:S(2)}, u32[]{:S(2)}) collective-permute-start(bf16[4,32,768]{2,1,0:T(8,128)(2,1)S(1)} %get-tuple-element.31), channel_id=1, source_target_pairs={{0,2},{1,3},{2,0},{3,1},{4,6},{5,7},{6,4},{7,5},{8,10},{9,11},{10,... | collective-permute-start | bytes 589832 | tf_op jit(solution)/shard_map/ppermute | solution.py:32
  18.5 7.8 %collective-permute-start.18 = (bf16[4,32,768]{2,1,0:T(8,128)(2,1)S(1)}, bf16[4,32,768]{2,1,0:T(8,128)(2,1)S(1)}, u32[]{:S(2)}, u32[]{:S(2)}) collective-permute-start(bf16[4,32,768]{2,1,0:T(8,128)(2,1)S(1)} %get-tuple-element.28.refs_4_), channel_id=1, source_target_pairs={{0,4},{4,0},{8,12},{12,8},{16,20},{20,16},{24,28},{28,24},{1,5},{5... | collective-permute-start | bytes 589832 | tf_op jit(solution)/shard_map/ppermute | solution.py:32
  21.9 8.3 %collective-permute-start.9 = (bf16[4,32,768]{2,1,0:T(8,128)(2,1)S(1)}, bf16[4,32,768]{2,1,0:T(8,128)(2,1)S(1)}, u32[]{:S(2)}, u32[]{:S(2)}) collective-permute-start(bf16[4,32,768]{2,1,0:T(8,128)(2,1)S(1)} %get-tuple-element.30.refs_1_), channel_id=1, source_target_pairs={{0,2},{1,3},{2,0},{3,1},{4,6},{5,7},{6,4},{7,5},{8,10},{9,11},{10,... | collective-permute-start | bytes 589832 | tf_op jit(solution)/shard_map/ppermute | solution.py:32
  23.1 15.3 %copy-start = (bf16[128,12288]{1,0:T(8,128)(2,1)S(1)}, bf16[128,12288]{1,0:T(8,128)(2,1)}, u32[]{:S(2)}) copy-start(bf16[128,12288]{1,0:T(8,128)(2,1)} %refs_5_.1) | copy-start | bytes 9437188
  23.1 7.7 %collective-permute-start.11 = (bf16[4,32,768]{2,1,0:T(8,128)(2,1)S(1)}, bf16[4,32,768]{2,1,0:T(8,128)(2,1)S(1)}, u32[]{:S(2)}, u32[]{:S(2)}) collective-permute-start(bf16[4,32,768]{2,1,0:T(8,128)(2,1)S(1)} %get-tuple-element.29.refs_0_.refs_3_), channel_id=1, source_target_pairs={{0,4},{4,0},{8,12},{12,8},{16,20},{20,16},{24,28},{28,24},{1,5},{5... | collective-permute-start | bytes 589832 | tf_op jit(solution)/shard_map/ppermute | solution.py:32
  26.4 6.0 %collective-permute-start.20 = (bf16[2,2,32,768]{3,2,1,0:T(8,128)(2,1)S(1)}, bf16[2,2,32,768]{3,2,1,0:T(8,128)(2,1)S(1)}, u32[]{:S(2)}, u32[]{:S(2)}) collective-permute-start(bf16[2,2,32,768]{3,2,1,0:T(8,128)(2,1)S(1)} %plane.2.refs_4_), channel_id=1, source_target_pairs={{0,8},{4,12},{8,0},{12,4},{16,24},{20,28},{24,16},{28,20},{1,9},{5... | collective-permute-start | bytes 589832 | tf_op jit(solution)/shard_map/ppermute | solution.py:32
  28.0 6.9 %collective-permute-start.8 = (bf16[4,32,768]{2,1,0:T(8,128)(2,1)S(1)}, bf16[4,32,768]{2,1,0:T(8,128)(2,1)S(1)}, u32[]{:S(2)}, u32[]{:S(2)}) collective-permute-start(bf16[4,32,768]{2,1,0:T(8,128)(2,1)S(1)} %get-tuple-element.29.refs_0_.refs_3_), channel_id=1, source_target_pairs={{0,2},{1,3},{2,0},{3,1},{4,6},{5,7},{6,4},{7,5},{8,10},{9,11},{10,... | collective-permute-start | bytes 589832 | tf_op jit(solution)/shard_map/ppermute | solution.py:32
  28.8 7.0 %collective-permute-start.12 = (bf16[4,32,768]{2,1,0:T(8,128)(2,1)S(1)}, bf16[4,32,768]{2,1,0:T(8,128)(2,1)S(1)}, u32[]{:S(2)}, u32[]{:S(2)}) collective-permute-start(bf16[4,32,768]{2,1,0:T(8,128)(2,1)S(1)} %get-tuple-element.30.refs_1_), channel_id=1, source_target_pairs={{0,4},{4,0},{8,12},{12,8},{16,20},{20,16},{24,28},{28,24},{1,5},{5... | collective-permute-start | bytes 589832 | tf_op jit(solution)/shard_map/ppermute | solution.py:32
  30.3 7.6 %collective-permute-start.14 = (bf16[4,32,768]{2,1,0:T(8,128)(2,1)S(1)}, bf16[4,32,768]{2,1,0:T(8,128)(2,1)S(1)}, u32[]{:S(2)}, u32[]{:S(2)}) collective-permute-start(bf16[4,32,768]{2,1,0:T(8,128)(2,1)S(1)} %collective-permute-done.9.refs_3_), channel_id=1, source_target_pairs={{0,4},{4,0},{8,12},{12,8},{16,20},{20,16},{24,28},{28,24},{1,5},{5... | collective-permute-start | bytes 589832 | tf_op jit(solution)/shard_map/ppermute | solution.py:32
  30.8 7.1 %collective-permute-start.13 = (bf16[4,32,768]{2,1,0:T(8,128)(2,1)S(1)}, bf16[4,32,768]{2,1,0:T(8,128)(2,1)S(1)}, u32[]{:S(2)}, u32[]{:S(2)}) collective-permute-start(bf16[4,32,768]{2,1,0:T(8,128)(2,1)S(1)} %collective-permute-done.11.refs_0_), channel_id=1, source_target_pairs={{0,2},{1,3},{2,0},{3,1},{4,6},{5,7},{6,4},{7,5},{8,10},{9,11},{10,... | collective-permute-start | bytes 589832 | tf_op jit(solution)/shard_map/ppermute | solution.py:32
  32.4 6.0 %collective-permute-start.21 = (bf16[1,2,32,768]{3,2,1,0:T(8,128)(2,1)S(1)}, bf16[1,2,32,768]{3,2,1,0:T(8,128)(2,1)S(1)}, u32[]{:S(2)}, u32[]{:S(2)}) collective-permute-start(bf16[1,2,32,768]{3,2,1,0:T(8,128)(2,1)S(1)} %plane.3), channel_id=1, source_target_pairs={{0,16},{4,20},{8,24},{12,28},{16,0},{20,4},{24,8},{28,12},{1,17},{... | collective-permute-start | bytes 294920 | tf_op jit(solution)/shard_map/ppermute | solution.py:32
  35.0 4.2 %collective-permute-start.10 = (bf16[4,4,32,768]{3,2,1,0:T(8,128)(2,1)S(1)}, bf16[4,4,32,768]{3,2,1,0:T(8,128)(2,1)S(1)}, u32[]{:S(2)}, u32[]{:S(2)}) collective-permute-start(bf16[4,4,32,768]{3,2,1,0:T(8,128)(2,1)S(1)} %near.1.refs_0_.refs_2_), channel_id=1, source_target_pairs={{0,1},{1,0},{2,3},{3,2},{4,5},{5,4},{6,7},{7,6},{8,9},{9,8},{10,11... | collective-permute-start | bytes 2359304 | tf_op jit(solution)/shard_map/ppermute | solution.py:32
  35.8 3.9 %collective-permute-start.15 = (bf16[2,4,32,768]{3,2,1,0:T(8,128)(2,1)S(1)}, bf16[2,4,32,768]{3,2,1,0:T(8,128)(2,1)S(1)}, u32[]{:S(2)}, u32[]{:S(2)}) collective-permute-start(bf16[2,4,32,768]{3,2,1,0:T(8,128)(2,1)S(1)} %side.1.refs_1_), channel_id=1, source_target_pairs={{0,1},{1,0},{2,3},{3,2},{4,5},{5,4},{6,7},{7,6},{8,9},{9,8},{10,11... | collective-permute-start | bytes 1179656 | tf_op jit(solution)/shard_map/ppermute | solution.py:32
  37.9 1.8 %collective-permute-start.17 = (bf16[4,32,768]{2,1,0:T(8,128)(2,1)S(1)}, bf16[4,32,768]{2,1,0:T(8,128)(2,1)S(1)}, u32[]{:S(2)}, u32[]{:S(2)}) collective-permute-start(bf16[4,32,768]{2,1,0:T(8,128)(2,1)S(1)} %collective-permute-done.14.refs_3_), channel_id=1, source_target_pairs={{0,1},{1,0},{2,3},{3,2},{4,5},{5,4},{6,7},{7,6},{8,9},{9,8},{10,11... | collective-permute-start | bytes 589832 | tf_op jit(solution)/shard_map/ppermute | solution.py:32
  37.9 1.8 %collective-permute-start.16 = (bf16[4,32,768]{2,1,0:T(8,128)(2,1)S(1)}, bf16[4,32,768]{2,1,0:T(8,128)(2,1)S(1)}, u32[]{:S(2)}, u32[]{:S(2)}) collective-permute-start(bf16[4,32,768]{2,1,0:T(8,128)(2,1)S(1)} %collective-permute-done.13.refs_2_), channel_id=1, source_target_pairs={{0,1},{1,0},{2,3},{3,2},{4,5},{5,4},{6,7},{7,6},{8,9},{9,8},{10,11... | collective-permute-start | bytes 589832 | tf_op jit(solution)/shard_map/ppermute | solution.py:32

commit v4 on v2

--- a/solution.py
+++ b/solution.py
@@ -187,7 +187,7 @@
         (*weights, out) = refs
         total = 0.0
     else:
-        (*weights, earlier, out, total_t) = refs
+        (*weights, earlier, out) = refs
         total = earlier[...]
     count = len(weights) // 2
     rows, half = weights[0].shape[2:]
@@ -203,16 +203,24 @@
                     picked.append(held[1 + 2 * (y - 1) + h][z])
                 else:
                     picked.append(held[0][2 * y + h, z])
-            left = jnp.concatenate(picked, axis=0)
-            right = pieces[:, h * half : (h + 1) * half]
+            left = pieces[:, h * half : (h + 1) * half]
+            right = jnp.concatenate(picked, axis=0)
             total = total + lax.dot_general(left, right, NT, preferred_element_type=F32)
     if x == 0:
         out[...] = total
         return
     node = lax.axis_index("node")
-    total_t[...] = total.reshape(total_t.shape)
-    ordered = [total_t[lax.bitwise_xor(node, n)] for n in range(2 * ys)]
-    out[...] = jnp.concatenate(ordered, axis=0).T.astype(BF16)
+    width = total.shape[1]
+    lane = lax.broadcasted_iota(jnp.int32, total.shape, 1)
+    bit = 1
+    while bit < 2 * ys:
+        shift = bit * rows
+        above = pltpu.roll(total, width - shift, 1)
+        below = pltpu.roll(total, shift, 1)
+        other = jnp.where(lax.bitwise_and(lane, shift) == 0, above, below)
+        total = jnp.where(lax.bitwise_and(node, bit) == 0, total, other)
+        bit *= 2
+    out[...] = total.astype(BF16)
 
 
 def project(tokens, near, far, ys, zs):
@@ -221,7 +229,7 @@
     cost = pl.CostEstimate(flops=tokens.size * width, bytes_accessed=2 * tokens.size, transcendentals=0)
     earlier = pl.pallas_call(
         functools.partial(project_kernel, ys, zs, 0),
-        out_shape=jax.ShapeDtypeStruct((width, count), F32),
+        out_shape=jax.ShapeDtypeStruct((count, width), F32),
         in_specs=[VMEM] * (1 + len(near)),
         out_specs=VMEM,
         compiler_params=PARAMS,
@@ -233,7 +241,6 @@
         out_shape=jax.ShapeDtypeStruct((count, width), BF16),
         in_specs=[VMEM] * (2 + len(far)),
         out_specs=VMEM,
-        scratch_shapes=[pltpu.VMEM((2 * ys, rows, count), F32)],
         compiler_params=PARAMS,
         cost_estimate=cost,
         name="project_far",

time: 41 us -> 41.1 us (level)
  no operation moved by 1% of the time
where the time goes in v4:
time: 41.1 us; the launch traced here: 40.9 us
  starting transfers between devices  24.3 us (59%)
  waiting for transfers between devices  9.2 us (22%)
  Pallas kernels  6.61 us (16%)
  between operations  0.75 us (2%)
    ppermute x22, starting transfers between devices, flip(): return lax.ppermute(entries, axis, [(i, i ^ offset) for i in range(size)])  24.3 us
    ppermute x22, waiting for transfers between devices, flip(): return lax.ppermute(entries, axis, [(i, i ^ offset) for i in range(size)])  9.2 us
    pallas_call x1, Pallas kernels, local_products(): pl.pallas_call(functools.partial(first_kernel, ys, zs), out_shape=(*block...  3.33 us
    pallas_call x1, Pallas kernels, project(): pl.pallas_call(functools.partial(project_kernel, ys, zs, 1), out_shape=ja...  1.36 us
  transfers between devices with their start and end apart: 22, of which 9 were waited for; matrix products, arithmetic and copies ran while one was open for 0% of the time, Pallas kernels for 5%

profile of v4, /device:TPU:0, one launch (start us, length us, event | category | flops | bytes accessed | tf_op | source)
XLA Modules:
  0.0 40.9 jit_solution(17396421425962238292)
XLA Ops:
  0.6 3.3 %first.1 = (bf16[4,4,32,768]{3,2,1,0:T(8,128)(2,1)S(1)}, bf16[4,4,32,768]{3,2,1,0:T(8,128)(2,1)S(1)}, bf16[4,4,32,768]{3,2,1,0:T(8,128)(2,1)S(1)}, bf16[4,4,32,7...) custom-call(bf16[128,12288]{1,0:T(8,128)(2,1)} %refs_5_.1, bf16[128,128]{1,0:T(8,128)(2,1)} %cot.1, ...), custom_call_target="tpu_custom_call" | custom-call | flops 402653184 | bytes 6291456 | tf_op jit(solution)/shard_map/first/pallas_call | solution.py:92
  4.0 0.5 %collective-permute-start.1 = (bf16[4,4,32,768]{3,2,1,0:T(8,128)(2,1)S(1)}, bf16[4,4,32,768]{3,2,1,0:T(8,128)(2,1)S(1)}, u32[]{:S(2)}, u32[]{:S(2)}) collective-permute-start(bf16[4,4,32,768]{3,2,1,0:T(8,128)(2,1)S(1)} %get-tuple-element.19), channel_id=1, source_target_pairs={{0,1},{1,0},{2,3},{3,2},{4,5},{5,4},{6,7},{7,6},{8,9},{9,8},{10,11... | collective-permute-start | bytes 2359304 | tf_op jit(solution)/shard_map/ppermute | solution.py:32
  4.5 0.1 collective-permute-start.3
  4.6 4.0 %collective-permute-start = (bf16[2,32,768]{2,1,0:T(8,128)(2,1)S(1)}, bf16[2,32,768]{2,1,0:T(8,128)(2,1)S(1)}, u32[]{:S(2)}, u32[]{:S(2)}) collective-permute-start(bf16[2,32,768]{2,1,0:T(8,128)(2,1)S(1)} %get-tuple-element.17.refs_0_), channel_id=1, source_target_pairs={{0,16},{4,20},{8,24},{12,28},{16,0},{20,4},{24,8},{28,12},{1,17},{... | collective-permute-start | bytes 294920 | tf_op jit(solution)/shard_map/ppermute | solution.py:32
  8.6 0.0 collective-permute-done.1.refs_1_
  8.6 0.2 stage1.1
  8.8 1.6 %collective-permute-start.6 = (bf16[1,4,32,768]{3,2,1,0:T(8,128)(2,1)S(1)}, bf16[1,4,32,768]{3,2,1,0:T(8,128)(2,1)S(1)}, u32[]{:S(2)}, u32[]{:S(2)}) collective-permute-start(bf16[1,4,32,768]{3,2,1,0:T(8,128)(2,1)S(1)} %get-tuple-element.20.refs_2_), channel_id=1, source_target_pairs={{0,4},{4,0},{8,12},{12,8},{16,20},{20,16},{24,28},{28,24},{1,5},{5... | collective-permute-start | bytes 589832 | tf_op jit(solution)/shard_map/ppermute | solution.py:32
  10.3 1.5 %collective-permute-start.7 = (bf16[4,32,768]{2,1,0:T(8,128)(2,1)S(1)}, bf16[4,32,768]{2,1,0:T(8,128)(2,1)S(1)}, u32[]{:S(2)}, u32[]{:S(2)}) collective-permute-start(bf16[4,32,768]{2,1,0:T(8,128)(2,1)S(1)} %get-tuple-element.25), channel_id=1, source_target_pairs={{0,2},{1,3},{2,0},{3,1},{4,6},{5,7},{6,4},{7,5},{8,10},{9,11},{10,... | collective-permute-start | bytes 589832 | tf_op jit(solution)/shard_map/ppermute | solution.py:32
  11.8 0.5 %collective-permute-start.4 = (bf16[4,32,768]{2,1,0:T(8,128)(2,1)S(1)}, bf16[4,32,768]{2,1,0:T(8,128)(2,1)S(1)}, u32[]{:S(2)}, u32[]{:S(2)}) collective-permute-start(bf16[4,32,768]{2,1,0:T(8,128)(2,1)S(1)} %get-tuple-element.23), channel_id=1, source_target_pairs={{0,4},{4,0},{8,12},{12,8},{16,20},{20,16},{24,28},{28,24},{1,5},{5... | collective-permute-start | bytes 589832 | tf_op jit(solution)/shard_map/ppermute | solution.py:32
  12.4 1.3 %collective-permute-done.refs_1_ = bf16[2,32,768]{2,1,0:T(8,128)(2,1)S(1)} collective-permute-done((bf16[2,32,768]{2,1,0:T(8,128)(2,1)S(1)}, bf16[2,32,768]{2,1,0:T(8,128)(2,1)S(1)}, u32[]{:S(2)}, u32[]{:S(2)}) %collective-permute-start) | collective-permute-done | bytes 98336 | tf_op jit(solution)/shard_map/ppermute | solution.py:32
  13.7 1.6 %collective-permute-start.5 = (bf16[4,32,768]{2,1,0:T(8,128)(2,1)S(1)}, bf16[4,32,768]{2,1,0:T(8,128)(2,1)S(1)}, u32[]{:S(2)}, u32[]{:S(2)}) collective-permute-start(bf16[4,32,768]{2,1,0:T(8,128)(2,1)S(1)} %get-tuple-element.24), channel_id=1, source_target_pairs={{0,2},{1,3},{2,0},{3,1},{4,6},{5,7},{6,4},{7,5},{8,10},{9,11},{10,... | collective-permute-start | bytes 589832 | tf_op jit(solution)/shard_map/ppermute | solution.py:32
  15.3 0.0 collective-permute-done.3.refs_1_
  15.3 0.7 %collective-permute-start.2 = (bf16[2,2,32,768]{3,2,1,0:T(8,128)(2,1)S(1)}, bf16[2,2,32,768]{3,2,1,0:T(8,128)(2,1)S(1)}, u32[]{:S(2)}, u32[]{:S(2)}) collective-permute-start(bf16[2,2,32,768]{3,2,1,0:T(8,128)(2,1)S(1)} %widen.1.refs_4_), channel_id=1, source_target_pairs={{0,8},{4,12},{8,0},{12,4},{16,24},{20,28},{24,16},{28,20},{1,9},{5... | collective-permute-start | bytes 589832 | tf_op jit(solution)/shard_map/ppermute | solution.py:32
  16.1 0.6 %collective-permute-done.6.refs_2_ = bf16[1,4,32,768]{3,2,1,0:T(8,128)(2,1)S(1)} collective-permute-done((bf16[1,4,32,768]{3,2,1,0:T(8,128)(2,1)S(1)}, bf16[1,4,32,768]{3,2,1,0:T(8,128)(2,1)S(1)}, u32[]{:S(2)}, u32[]{:S(2)}) %collective-permute-start.6) | collective-permute-done | bytes 196640 | tf_op jit(solution)/shard_map/ppermute | solution.py:32
  16.6 0.7 %collective-permute-done.7.refs_3_ = bf16[4,32,768]{2,1,0:T(8,128)(2,1)S(1)} collective-permute-done((bf16[4,32,768]{2,1,0:T(8,128)(2,1)S(1)}, bf16[4,32,768]{2,1,0:T(8,128)(2,1)S(1)}, u32[]{:S(2)}, u32[]{:S(2)}) %collective-permute-start.7) | collective-permute-done | bytes 196640 | tf_op jit(solution)/shard_map/ppermute | solution.py:32
  17.4 0.1 stage2.1
  17.5 0.8 %collective-permute-start.18 = (bf16[4,32,768]{2,1,0:T(8,128)(2,1)S(1)}, bf16[4,32,768]{2,1,0:T(8,128)(2,1)S(1)}, u32[]{:S(2)}, u32[]{:S(2)}) collective-permute-start(bf16[4,32,768]{2,1,0:T(8,128)(2,1)S(1)} %get-tuple-element.26.refs_4_), channel_id=1, source_target_pairs={{0,4},{4,0},{8,12},{12,8},{16,20},{20,16},{24,28},{28,24},{1,5},{5... | collective-permute-start | bytes 589832 | tf_op jit(solution)/shard_map/ppermute | solution.py:32
  18.3 1.5 %collective-permute-start.19 = (bf16[4,32,768]{2,1,0:T(8,128)(2,1)S(1)}, bf16[4,32,768]{2,1,0:T(8,128)(2,1)S(1)}, u32[]{:S(2)}, u32[]{:S(2)}) collective-permute-start(bf16[4,32,768]{2,1,0:T(8,128)(2,1)S(1)} %get-tuple-element.31), channel_id=1, source_target_pairs={{0,2},{1,3},{2,0},{3,1},{4,6},{5,7},{6,4},{7,5},{8,10},{9,11},{10,... | collective-permute-start | bytes 589832 | tf_op jit(solution)/shard_map/ppermute | solution.py:32
  19.9 1.0 %collective-permute-done.4.refs_2_ = bf16[4,32,768]{2,1,0:T(8,128)(2,1)S(1)} collective-permute-done((bf16[4,32,768]{2,1,0:T(8,128)(2,1)S(1)}, bf16[4,32,768]{2,1,0:T(8,128)(2,1)S(1)}, u32[]{:S(2)}, u32[]{:S(2)}) %collective-permute-start.4) | collective-permute-done | bytes 196640 | tf_op jit(solution)/shard_map/ppermute | solution.py:32
  20.8 0.7 %collective-permute-done.5.refs_3_ = bf16[4,32,768]{2,1,0:T(8,128)(2,1)S(1)} collective-permute-done((bf16[4,32,768]{2,1,0:T(8,128)(2,1)S(1)}, bf16[4,32,768]{2,1,0:T(8,128)(2,1)S(1)}, u32[]{:S(2)}, u32[]{:S(2)}) %collective-permute-start.5) | collective-permute-done | bytes 196640 | tf_op jit(solution)/shard_map/ppermute | solution.py:32
  21.6 0.1 sides.1.refs_3_.refs_0_
  21.7 0.0 copy-start
  21.7 0.0 collective-permute-done.2.refs_2_
  21.8 1.2 %collective-permute-start.10 = (bf16[4,32,768]{2,1,0:T(8,128)(2,1)S(1)}, bf16[4,32,768]{2,1,0:T(8,128)(2,1)S(1)}, u32[]{:S(2)}, u32[]{:S(2)}) collective-permute-start(bf16[4,32,768]{2,1,0:T(8,128)(2,1)S(1)} %get-tuple-element.27.refs_0_.refs_3_), channel_id=1, source_target_pairs={{0,4},{4,0},{8,12},{12,8},{16,20},{20,16},{24,28},{28,24},{1,5},{5... | collective-permute-start | bytes 589832 | tf_op jit(solution)/shard_map/ppermute | solution.py:32
  22.9 1.8 %collective-permute-start.9 = (bf16[4,32,768]{2,1,0:T(8,128)(2,1)S(1)}, bf16[4,32,768]{2,1,0:T(8,128)(2,1)S(1)}, u32[]{:S(2)}, u32[]{:S(2)}) collective-permute-start(bf16[4,32,768]{2,1,0:T(8,128)(2,1)S(1)} %get-tuple-element.28.refs_1_), channel_id=1, source_target_pairs={{0,2},{1,3},{2,0},{3,1},{4,6},{5,7},{6,4},{7,5},{8,10},{9,11},{10,... | collective-permute-start | bytes 589832 | tf_op jit(solution)/shard_map/ppermute | solution.py:32
  24.8 1.4 %collective-permute-done.19.refs_2_ = bf16[4,32,768]{2,1,0:T(8,128)(2,1)S(1)} collective-permute-done((bf16[4,32,768]{2,1,0:T(8,128)(2,1)S(1)}, bf16[4,32,768]{2,1,0:T(8,128)(2,1)S(1)}, u32[]{:S(2)}, u32[]{:S(2)}) %collective-permute-start.19) | collective-permute-done | bytes 196640 | tf_op jit(solution)/shard_map/ppermute | solution.py:32
  26.2 1.6 %collective-permute-start.20 = (bf16[2,2,32,768]{3,2,1,0:T(8,128)(2,1)S(1)}, bf16[2,2,32,768]{3,2,1,0:T(8,128)(2,1)S(1)}, u32[]{:S(2)}, u32[]{:S(2)}) collective-permute-start(bf16[2,2,32,768]{3,2,1,0:T(8,128)(2,1)S(1)} %plane.2.refs_4_), channel_id=1, source_target_pairs={{0,8},{4,12},{8,0},{12,4},{16,24},{20,28},{24,16},{28,20},{1,9},{5... | collective-permute-start | bytes 589832 | tf_op jit(solution)/shard_map/ppermute | solution.py:32
  27.8 0.7 %collective-permute-start.11 = (bf16[4,32,768]{2,1,0:T(8,128)(2,1)S(1)}, bf16[4,32,768]{2,1,0:T(8,128)(2,1)S(1)}, u32[]{:S(2)}, u32[]{:S(2)}) collective-permute-start(bf16[4,32,768]{2,1,0:T(8,128)(2,1)S(1)} %get-tuple-element.28.refs_1_), channel_id=1, source_target_pairs={{0,4},{4,0},{8,12},{12,8},{16,20},{20,16},{24,28},{28,24},{1,5},{5... | collective-permute-start | bytes 589832 | tf_op jit(solution)/shard_map/ppermute | solution.py:32
  28.5 1.5 %collective-permute-start.8 = (bf16[4,32,768]{2,1,0:T(8,128)(2,1)S(1)}, bf16[4,32,768]{2,1,0:T(8,128)(2,1)S(1)}, u32[]{:S(2)}, u32[]{:S(2)}) collective-permute-start(bf16[4,32,768]{2,1,0:T(8,128)(2,1)S(1)} %get-tuple-element.27.refs_0_.refs_3_), channel_id=1, source_target_pairs={{0,2},{1,3},{2,0},{3,1},{4,6},{5,7},{6,4},{7,5},{8,10},{9,11},{10,... | collective-permute-start | bytes 589832 | tf_op jit(solution)/shard_map/ppermute | solution.py:32
  30.0 0.0 collective-permute-done.10.refs_4_
  30.0 0.5 %collective-permute-start.12 = (bf16[4,32,768]{2,1,0:T(8,128)(2,1)S(1)}, bf16[4,32,768]{2,1,0:T(8,128)(2,1)S(1)}, u32[]{:S(2)}, u32[]{:S(2)}) collective-permute-start(bf16[4,32,768]{2,1,0:T(8,128)(2,1)S(1)} %collective-permute-done.10.refs_4_), channel_id=1, source_target_pairs={{0,2},{1,3},{2,0},{3,1},{4,6},{5,7},{6,4},{7,5},{8,10},{9,11},{10,... | collective-permute-start | bytes 589832 | tf_op jit(solution)/shard_map/ppermute | solution.py:32
  30.5 0.0 collective-permute-done.9.refs_3_
  30.5 1.7 %collective-permute-start.13 = (bf16[4,32,768]{2,1,0:T(8,128)(2,1)S(1)}, bf16[4,32,768]{2,1,0:T(8,128)(2,1)S(1)}, u32[]{:S(2)}, u32[]{:S(2)}) collective-permute-start(bf16[4,32,768]{2,1,0:T(8,128)(2,1)S(1)} %collective-permute-done.9.refs_3_), channel_id=1, source_target_pairs={{0,4},{4,0},{8,12},{12,8},{16,20},{20,16},{24,28},{28,24},{1,5},{5... | collective-permute-start | bytes 589832 | tf_op jit(solution)/shard_map/ppermute | solution.py:32
  32.2 0.0 collective-permute-done.20.refs_3_
  32.3 1.4 %collective-permute-start.21 = (bf16[1,2,32,768]{3,2,1,0:T(8,128)(2,1)S(1)}, bf16[1,2,32,768]{3,2,1,0:T(8,128)(2,1)S(1)}, u32[]{:S(2)}, u32[]{:S(2)}) collective-permute-start(bf16[1,2,32,768]{3,2,1,0:T(8,128)(2,1)S(1)} %plane.3), channel_id=1, source_target_pairs={{0,16},{4,20},{8,24},{12,28},{16,0},{20,4},{24,8},{28,12},{1,17},{... | collective-permute-start | bytes 294920 | tf_op jit(solution)/shard_map/ppermute | solution.py:32
  33.6 1.1 %collective-permute-done.11.refs_5_ = bf16[4,32,768]{2,1,0:T(8,128)(2,1)S(1)} collective-permute-done((bf16[4,32,768]{2,1,0:T(8,128)(2,1)S(1)}, bf16[4,32,768]{2,1,0:T(8,128)(2,1)S(1)}, u32[]{:S(2)}, u32[]{:S(2)}) %collective-permute-start.11) | collective-permute-done | bytes 196640 | tf_op jit(solution)/shard_map/ppermute | solution.py:32
  34.7 0.9 %collective-permute-done.8.refs_2_ = bf16[4,32,768]{2,1,0:T(8,128)(2,1)S(1)} collective-permute-done((bf16[4,32,768]{2,1,0:T(8,128)(2,1)S(1)}, bf16[4,32,768]{2,1,0:T(8,128)(2,1)S(1)}, u32[]{:S(2)}, u32[]{:S(2)}) %collective-permute-start.8) | collective-permute-done | bytes 196640 | tf_op jit(solution)/shard_map/ppermute | solution.py:32
  35.6 0.1 most.1
  35.7 0.1 collective-permute-start.17
  35.8 0.5 %collective-permute-start.14 = (bf16[2,4,32,768]{3,2,1,0:T(8,128)(2,1)S(1)}, bf16[2,4,32,768]{3,2,1,0:T(8,128)(2,1)S(1)}, u32[]{:S(2)}, u32[]{:S(2)}) collective-permute-start(bf16[2,4,32,768]{3,2,1,0:T(8,128)(2,1)S(1)} %get-tuple-element.29.refs_0_), channel_id=1, source_target_pairs={{0,1},{1,0},{2,3},{3,2},{4,5},{5,4},{6,7},{7,6},{8,9},{9,8},{10,11... | collective-permute-start | bytes 1179656 | tf_op jit(solution)/shard_map/ppermute | solution.py:32
  36.3 1.4 %collective-permute-done.12.refs_1_ = bf16[4,32,768]{2,1,0:T(8,128)(2,1)S(1)} collective-permute-done((bf16[4,32,768]{2,1,0:T(8,128)(2,1)S(1)}, bf16[4,32,768]{2,1,0:T(8,128)(2,1)S(1)}, u32[]{:S(2)}, u32[]{:S(2)}) %collective-permute-start.12) | collective-permute-done | bytes 196640 | tf_op jit(solution)/shard_map/ppermute | solution.py:32
  37.7 0.0 collective-permute-start.15
  37.7 0.0 collective-permute-done.13.refs_2_
  37.7 0.5 %collective-permute-start.16 = (bf16[4,32,768]{2,1,0:T(8,128)(2,1)S(1)}, bf16[4,32,768]{2,1,0:T(8,128)(2,1)S(1)}, u32[]{:S(2)}, u32[]{:S(2)}) collective-permute-start(bf16[4,32,768]{2,1,0:T(8,128)(2,1)S(1)} %collective-permute-done.13.refs_2_), channel_id=1, source_target_pairs={{0,1},{1,0},{2,3},{3,2},{4,5},{5,4},{6,7},{7,6},{8,9},{9,8},{10,11... | collective-permute-start | bytes 589832 | tf_op jit(solution)/shard_map/ppermute | solution.py:32
  38.2 0.0 collective-permute-done.21.refs_4_
  38.2 0.7 %finish.1 = f32[32,1536]{1,0:T(8,128)} custom-call(f32[2,4,32,768]{3,2,1,0:T(8,128)S(1)} %sides.1.refs_3_.refs_0_, bf16[4,32,768]{2,1,0:T(8,128)(2,1)S(1)} %collective-permute-done.18.refs_1_, bf16[4,32,768]{2,1,0:T(8,128)(2,1)S(1)} %collective-permute-done.19.refs_2_, bf16[2,2,32,768]{3,2,1,0:T(8,128)(2,1)S(1)} %collective-permute-done.20.refs_3_, ...), custom_call_target="tpu_custom_call" | custom-call | flops 40000000000 | bytes 1 | tf_op jit(solution)/shard_map/finish/pallas_call | solution.py:174
  39.0 0.6 %project_near.1.refs_6_ = f32[128,128]{1,0:T(8,128)S(1)} custom-call(bf16[128,12288]{1,0:T(8,128)(2,1)S(1)} %copy-done, bf16[4,4,32,768]{3,2,1,0:T(8,128)(2,1)S(1)} %get-tuple-element.30.refs_0_, bf16[4,4,32,768]{3,2,1,0:T(8,128)(2,1)S(1)} %collective-permute-done.17.refs_1_), custom_call_target="tpu_custom_call" | custom-call | flops 201326592 | bytes 3145728 | tf_op jit(solution)/shard_map/project_near/pallas_call | solution.py:230
  39.6 1.4 %project_far.1 = bf16[128,128]{1,0:T(8,128)(2,1)} custom-call(bf16[128,12288]{1,0:T(8,128)(2,1)S(1)} %copy-done, bf16[2,4,32,768]{3,2,1,0:T(8,128)(2,1)S(1)} %get-tuple-element.29.refs_0_, bf16[4,32,768]{2,1,0:T(8,128)(2,1)S(1)} %collective-permute-done.12.refs_1_, bf16[4,32,768]{2,1,0:T(8,128)(2,1)S(1)} %collective-permute-done.13.refs_2_, ...), custom_call_target="tpu_custom_call" | custom-call | flops 201326592 | bytes 3145728 | tf_op jit(solution)/shard_map/project_far/pallas_call | solution.py:239
  (10 shorter events, 0.1 us)
Async XLA Ops:
  4.0 4.6 %collective-permute-start.1 = (bf16[4,4,32,768]{3,2,1,0:T(8,128)(2,1)S(1)}, bf16[4,4,32,768]{3,2,1,0:T(8,128)(2,1)S(1)}, u32[]{:S(2)}, u32[]{:S(2)}) collective-permute-start(bf16[4,4,32,768]{3,2,1,0:T(8,128)(2,1)S(1)} %get-tuple-element.19), channel_id=1, source_target_pairs={{0,1},{1,0},{2,3},{3,2},{4,5},{5,4},{6,7},{7,6},{8,9},{9,8},{10,11... | collective-permute-start | bytes 2359304 | tf_op jit(solution)/shard_map/ppermute | solution.py:32
  4.5 10.8 %collective-permute-start.3 = (bf16[4,4,32,768]{3,2,1,0:T(8,128)(2,1)S(1)}, bf16[4,4,32,768]{3,2,1,0:T(8,128)(2,1)S(1)}, u32[]{:S(2)}, u32[]{:S(2)}) collective-permute-start(bf16[4,4,32,768]{3,2,1,0:T(8,128)(2,1)S(1)} %get-tuple-element.22), channel_id=1, source_target_pairs={{0,1},{1,0},{2,3},{3,2},{4,5},{5,4},{6,7},{7,6},{8,9},{9,8},{10,11... | collective-permute-start | bytes 2359304 | tf_op jit(solution)/shard_map/ppermute | solution.py:32
  4.6 9.2 %collective-permute-start = (bf16[2,32,768]{2,1,0:T(8,128)(2,1)S(1)}, bf16[2,32,768]{2,1,0:T(8,128)(2,1)S(1)}, u32[]{:S(2)}, u32[]{:S(2)}) collective-permute-start(bf16[2,32,768]{2,1,0:T(8,128)(2,1)S(1)} %get-tuple-element.17.refs_0_), channel_id=1, source_target_pairs={{0,16},{4,20},{8,24},{12,28},{16,0},{20,4},{24,8},{28,12},{1,17},{... | collective-permute-start | bytes 294920 | tf_op jit(solution)/shard_map/ppermute | solution.py:32
  8.8 7.9 %collective-permute-start.6 = (bf16[1,4,32,768]{3,2,1,0:T(8,128)(2,1)S(1)}, bf16[1,4,32,768]{3,2,1,0:T(8,128)(2,1)S(1)}, u32[]{:S(2)}, u32[]{:S(2)}) collective-permute-start(bf16[1,4,32,768]{3,2,1,0:T(8,128)(2,1)S(1)} %get-tuple-element.20.refs_2_), channel_id=1, source_target_pairs={{0,4},{4,0},{8,12},{12,8},{16,20},{20,16},{24,28},{28,24},{1,5},{5... | collective-permute-start | bytes 589832 | tf_op jit(solution)/shard_map/ppermute | solution.py:32
  10.3 7.0 %collective-permute-start.7 = (bf16[4,32,768]{2,1,0:T(8,128)(2,1)S(1)}, bf16[4,32,768]{2,1,0:T(8,128)(2,1)S(1)}, u32[]{:S(2)}, u32[]{:S(2)}) collective-permute-start(bf16[4,32,768]{2,1,0:T(8,128)(2,1)S(1)} %get-tuple-element.25), channel_id=1, source_target_pairs={{0,2},{1,3},{2,0},{3,1},{4,6},{5,7},{6,4},{7,5},{8,10},{9,11},{10,... | collective-permute-start | bytes 589832 | tf_op jit(solution)/shard_map/ppermute | solution.py:32
  11.8 9.0 %collective-permute-start.4 = (bf16[4,32,768]{2,1,0:T(8,128)(2,1)S(1)}, bf16[4,32,768]{2,1,0:T(8,128)(2,1)S(1)}, u32[]{:S(2)}, u32[]{:S(2)}) collective-permute-start(bf16[4,32,768]{2,1,0:T(8,128)(2,1)S(1)} %get-tuple-element.23), channel_id=1, source_target_pairs={{0,4},{4,0},{8,12},{12,8},{16,20},{20,16},{24,28},{28,24},{1,5},{5... | collective-permute-start | bytes 589832 | tf_op jit(solution)/shard_map/ppermute | solution.py:32
  13.7 7.8 %collective-permute-start.5 = (bf16[4,32,768]{2,1,0:T(8,128)(2,1)S(1)}, bf16[4,32,768]{2,1,0:T(8,128)(2,1)S(1)}, u32[]{:S(2)}, u32[]{:S(2)}) collective-permute-start(bf16[4,32,768]{2,1,0:T(8,128)(2,1)S(1)} %get-tuple-element.24), channel_id=1, source_target_pairs={{0,2},{1,3},{2,0},{3,1},{4,6},{5,7},{6,4},{7,5},{8,10},{9,11},{10,... | collective-permute-start | bytes 589832 | tf_op jit(solution)/shard_map/ppermute | solution.py:32
  15.3 6.4 %collective-permute-start.2 = (bf16[2,2,32,768]{3,2,1,0:T(8,128)(2,1)S(1)}, bf16[2,2,32,768]{3,2,1,0:T(8,128)(2,1)S(1)}, u32[]{:S(2)}, u32[]{:S(2)}) collective-permute-start(bf16[2,2,32,768]{3,2,1,0:T(8,128)(2,1)S(1)} %widen.1.refs_4_), channel_id=1, source_target_pairs={{0,8},{4,12},{8,0},{12,4},{16,24},{20,28},{24,16},{28,20},{1,9},{5... | collective-permute-start | bytes 589832 | tf_op jit(solution)/shard_map/ppermute | solution.py:32
  17.5 7.3 %collective-permute-start.18 = (bf16[4,32,768]{2,1,0:T(8,128)(2,1)S(1)}, bf16[4,32,768]{2,1,0:T(8,128)(2,1)S(1)}, u32[]{:S(2)}, u32[]{:S(2)}) collective-permute-start(bf16[4,32,768]{2,1,0:T(8,128)(2,1)S(1)} %get-tuple-element.26.refs_4_), channel_id=1, source_target_pairs={{0,4},{4,0},{8,12},{12,8},{16,20},{20,16},{24,28},{28,24},{1,5},{5... | collective-permute-start | bytes 589832 | tf_op jit(solution)/shard_map/ppermute | solution.py:32
  18.3 7.8 %collective-permute-start.19 = (bf16[4,32,768]{2,1,0:T(8,128)(2,1)S(1)}, bf16[4,32,768]{2,1,0:T(8,128)(2,1)S(1)}, u32[]{:S(2)}, u32[]{:S(2)}) collective-permute-start(bf16[4,32,768]{2,1,0:T(8,128)(2,1)S(1)} %get-tuple-element.31), channel_id=1, source_target_pairs={{0,2},{1,3},{2,0},{3,1},{4,6},{5,7},{6,4},{7,5},{8,10},{9,11},{10,... | collective-permute-start | bytes 589832 | tf_op jit(solution)/shard_map/ppermute | solution.py:32
  21.7 16.5 %copy-start = (bf16[128,12288]{1,0:T(8,128)(2,1)S(1)}, bf16[128,12288]{1,0:T(8,128)(2,1)}, u32[]{:S(2)}) copy-start(bf16[128,12288]{1,0:T(8,128)(2,1)} %refs_5_.1) | copy-start | bytes 9437188
  21.8 8.3 %collective-permute-start.10 = (bf16[4,32,768]{2,1,0:T(8,128)(2,1)S(1)}, bf16[4,32,768]{2,1,0:T(8,128)(2,1)S(1)}, u32[]{:S(2)}, u32[]{:S(2)}) collective-permute-start(bf16[4,32,768]{2,1,0:T(8,128)(2,1)S(1)} %get-tuple-element.27.refs_0_.refs_3_), channel_id=1, source_target_pairs={{0,4},{4,0},{8,12},{12,8},{16,20},{20,16},{24,28},{28,24},{1,5},{5... | collective-permute-start | bytes 589832 | tf_op jit(solution)/shard_map/ppermute | solution.py:32
  22.9 7.6 %collective-permute-start.9 = (bf16[4,32,768]{2,1,0:T(8,128)(2,1)S(1)}, bf16[4,32,768]{2,1,0:T(8,128)(2,1)S(1)}, u32[]{:S(2)}, u32[]{:S(2)}) collective-permute-start(bf16[4,32,768]{2,1,0:T(8,128)(2,1)S(1)} %get-tuple-element.28.refs_1_), channel_id=1, source_target_pairs={{0,2},{1,3},{2,0},{3,1},{4,6},{5,7},{6,4},{7,5},{8,10},{9,11},{10,... | collective-permute-start | bytes 589832 | tf_op jit(solution)/shard_map/ppermute | solution.py:32
  26.2 6.0 %collective-permute-start.20 = (bf16[2,2,32,768]{3,2,1,0:T(8,128)(2,1)S(1)}, bf16[2,2,32,768]{3,2,1,0:T(8,128)(2,1)S(1)}, u32[]{:S(2)}, u32[]{:S(2)}) collective-permute-start(bf16[2,2,32,768]{3,2,1,0:T(8,128)(2,1)S(1)} %plane.2.refs_4_), channel_id=1, source_target_pairs={{0,8},{4,12},{8,0},{12,4},{16,24},{20,28},{24,16},{28,20},{1,9},{5... | collective-permute-start | bytes 589832 | tf_op jit(solution)/shard_map/ppermute | solution.py:32
  27.8 6.9 %collective-permute-start.11 = (bf16[4,32,768]{2,1,0:T(8,128)(2,1)S(1)}, bf16[4,32,768]{2,1,0:T(8,128)(2,1)S(1)}, u32[]{:S(2)}, u32[]{:S(2)}) collective-permute-start(bf16[4,32,768]{2,1,0:T(8,128)(2,1)S(1)} %get-tuple-element.28.refs_1_), channel_id=1, source_target_pairs={{0,4},{4,0},{8,12},{12,8},{16,20},{20,16},{24,28},{28,24},{1,5},{5... | collective-permute-start | bytes 589832 | tf_op jit(solution)/shard_map/ppermute | solution.py:32
  28.5 7.1 %collective-permute-start.8 = (bf16[4,32,768]{2,1,0:T(8,128)(2,1)S(1)}, bf16[4,32,768]{2,1,0:T(8,128)(2,1)S(1)}, u32[]{:S(2)}, u32[]{:S(2)}) collective-permute-start(bf16[4,32,768]{2,1,0:T(8,128)(2,1)S(1)} %get-tuple-element.27.refs_0_.refs_3_), channel_id=1, source_target_pairs={{0,2},{1,3},{2,0},{3,1},{4,6},{5,7},{6,4},{7,5},{8,10},{9,11},{10,... | collective-permute-start | bytes 589832 | tf_op jit(solution)/shard_map/ppermute | solution.py:32
  30.0 7.7 %collective-permute-start.12 = (bf16[4,32,768]{2,1,0:T(8,128)(2,1)S(1)}, bf16[4,32,768]{2,1,0:T(8,128)(2,1)S(1)}, u32[]{:S(2)}, u32[]{:S(2)}) collective-permute-start(bf16[4,32,768]{2,1,0:T(8,128)(2,1)S(1)} %collective-permute-done.10.refs_4_), channel_id=1, source_target_pairs={{0,2},{1,3},{2,0},{3,1},{4,6},{5,7},{6,4},{7,5},{8,10},{9,11},{10,... | collective-permute-start | bytes 589832 | tf_op jit(solution)/shard_map/ppermute | solution.py:32
  30.5 7.2 %collective-permute-start.13 = (bf16[4,32,768]{2,1,0:T(8,128)(2,1)S(1)}, bf16[4,32,768]{2,1,0:T(8,128)(2,1)S(1)}, u32[]{:S(2)}, u32[]{:S(2)}) collective-permute-start(bf16[4,32,768]{2,1,0:T(8,128)(2,1)S(1)} %collective-permute-done.9.refs_3_), channel_id=1, source_target_pairs={{0,4},{4,0},{8,12},{12,8},{16,20},{20,16},{24,28},{28,24},{1,5},{5... | collective-permute-start | bytes 589832 | tf_op jit(solution)/shard_map/ppermute | solution.py:32
  32.3 6.0 %collective-permute-start.21 = (bf16[1,2,32,768]{3,2,1,0:T(8,128)(2,1)S(1)}, bf16[1,2,32,768]{3,2,1,0:T(8,128)(2,1)S(1)}, u32[]{:S(2)}, u32[]{:S(2)}) collective-permute-start(bf16[1,2,32,768]{3,2,1,0:T(8,128)(2,1)S(1)} %plane.3), channel_id=1, source_target_pairs={{0,16},{4,20},{8,24},{12,28},{16,0},{20,4},{24,8},{28,12},{1,17},{... | collective-permute-start | bytes 294920 | tf_op jit(solution)/shard_map/ppermute | solution.py:32
  35.7 3.3 %collective-permute-start.17 = (bf16[4,4,32,768]{3,2,1,0:T(8,128)(2,1)S(1)}, bf16[4,4,32,768]{3,2,1,0:T(8,128)(2,1)S(1)}, u32[]{:S(2)}, u32[]{:S(2)}) collective-permute-start(bf16[4,4,32,768]{3,2,1,0:T(8,128)(2,1)S(1)} %get-tuple-element.30.refs_0_), channel_id=1, source_target_pairs={{0,1},{1,0},{2,3},{3,2},{4,5},{5,4},{6,7},{7,6},{8,9},{9,8},{10,11... | collective-permute-start | bytes 2359304 | tf_op jit(solution)/shard_map/ppermute | solution.py:32
  35.8 3.8 %collective-permute-start.14 = (bf16[2,4,32,768]{3,2,1,0:T(8,128)(2,1)S(1)}, bf16[2,4,32,768]{3,2,1,0:T(8,128)(2,1)S(1)}, u32[]{:S(2)}, u32[]{:S(2)}) collective-permute-start(bf16[2,4,32,768]{3,2,1,0:T(8,128)(2,1)S(1)} %get-tuple-element.29.refs_0_), channel_id=1, source_target_pairs={{0,1},{1,0},{2,3},{3,2},{4,5},{5,4},{6,7},{7,6},{8,9},{9,8},{10,11... | collective-permute-start | bytes 1179656 | tf_op jit(solution)/shard_map/ppermute | solution.py:32
  37.7 1.8 %collective-permute-start.15 = (bf16[4,32,768]{2,1,0:T(8,128)(2,1)S(1)}, bf16[4,32,768]{2,1,0:T(8,128)(2,1)S(1)}, u32[]{:S(2)}, u32[]{:S(2)}) collective-permute-start(bf16[4,32,768]{2,1,0:T(8,128)(2,1)S(1)} %collective-permute-done.12.refs_1_), channel_id=1, source_target_pairs={{0,1},{1,0},{2,3},{3,2},{4,5},{5,4},{6,7},{7,6},{8,9},{9,8},{10,11... | collective-permute-start | bytes 589832 | tf_op jit(solution)/shard_map/ppermute | solution.py:32
  37.7 1.8 %collective-permute-start.16 = (bf16[4,32,768]{2,1,0:T(8,128)(2,1)S(1)}, bf16[4,32,768]{2,1,0:T(8,128)(2,1)S(1)}, u32[]{:S(2)}, u32[]{:S(2)}) collective-permute-start(bf16[4,32,768]{2,1,0:T(8,128)(2,1)S(1)} %collective-permute-done.13.refs_2_), channel_id=1, source_target_pairs={{0,1},{1,0},{2,3},{3,2},{4,5},{5,4},{6,7},{7,6},{8,9},{9,8},{10,11... | collective-permute-start | bytes 589832 | tf_op jit(solution)/shard_map/ppermute | solution.py:32

commit v5 on v2

--- a/solution.py
+++ b/solution.py
@@ -187,8 +187,10 @@
         (*weights, out) = refs
         total = 0.0
     else:
-        (*weights, earlier, out, total_t) = refs
+        (*weights, earlier, grad, out, grad_out, total_t, sem) = refs
         total = earlier[...]
+        copy = pltpu.make_async_copy(grad, grad_out, sem)
+        copy.start()
     count = len(weights) // 2
     rows, half = weights[0].shape[2:]
     cols = 2 * half
@@ -200,7 +202,7 @@
                 held = weights[count * (n % 2) : count * (n % 2 + 1)]
                 y = n // 2
                 if x and y:
-                    picked.append(held[1 + 2 * (y - 1) + h][z])
+                    picked.append(held[1 + 2 * (y - 1) + 1 - h][z])
                 else:
                     picked.append(held[0][2 * y + h, z])
             left = jnp.concatenate(picked, axis=0)
@@ -213,9 +215,10 @@
     total_t[...] = total.reshape(total_t.shape)
     ordered = [total_t[lax.bitwise_xor(node, n)] for n in range(2 * ys)]
     out[...] = jnp.concatenate(ordered, axis=0).T.astype(BF16)
-
-
-def project(tokens, near, far, ys, zs):
+    copy.wait()
+
+
+def project(tokens, near, far, grad, ys, zs):
     rows = near[0].shape[2]
     count, width = tokens.shape[0], 2 * ys * rows
     cost = pl.CostEstimate(flops=tokens.size * width, bytes_accessed=2 * tokens.size, transcendentals=0)
@@ -230,17 +233,17 @@
     )(tokens, *near)
     return pl.pallas_call(
         functools.partial(project_kernel, ys, zs, 1),
-        out_shape=jax.ShapeDtypeStruct((count, width), BF16),
-        in_specs=[VMEM] * (2 + len(far)),
-        out_specs=VMEM,
-        scratch_shapes=[pltpu.VMEM((2 * ys, rows, count), F32)],
+        out_shape=(jax.ShapeDtypeStruct((count, width), BF16), jax.ShapeDtypeStruct(grad.shape, F32)),
+        in_specs=[VMEM] * (3 + len(far)),
+        out_specs=(VMEM, ANY),
+        scratch_shapes=[pltpu.VMEM((2 * ys, rows, count), F32), pltpu.SemaphoreType.DMA],
         compiler_params=PARAMS,
         cost_estimate=cost,
         name="project_far",
-    )(tokens, *far, earlier)
-
-
-def plain_project(tokens, near, far, ys, zs):
+    )(tokens, *far, earlier, grad)
+
+
+def plain_project(tokens, near, far, grad, ys, zs):
     rows, half = near[0].shape[2:]
     node, wide = lax.axis_index("node"), lax.axis_index("wide")
     pieces = tokens.reshape(tokens.shape[0], 2 * zs, 2, half)
@@ -248,7 +251,11 @@
     pieces = pieces.reshape(tokens.shape[0], zs, 2, 2, half)
     count = len(far) // 2
     weights = [
-        jnp.concatenate([near[c], far[count * c], jnp.stack(far[count * c + 1 : count * (c + 1)])]) for c in range(2)
+        jnp.concatenate(
+            [near[c], far[count * c]]
+            + [far[count * c + 1 + 2 * y + 1 - h][None] for y in range(ys - 1) for h in range(2)]
+        )
+        for c in range(2)
     ]
     total = []
     for n in range(2 * ys):
@@ -259,7 +266,7 @@
                 part = part + jnp.einsum("tzl,zrl->tr", pieces[:, :, x, h], held, preferred_element_type=F32)
         total.append(part)
     total = jnp.take(jnp.stack(total, axis=1), jnp.arange(2 * ys) ^ node, axis=1)
-    return total.reshape(tokens.shape[0], -1).astype(BF16)
+    return total.reshape(tokens.shape[0], -1).astype(BF16), grad
 
 
 def on_device(wides, nodes, tokens, codes, scales, cotangent):
@@ -361,10 +368,10 @@
     groups = [range(2 * ys), range(2 * ys, 2 * ys + 2)]
     outs = [((len(g), *one), [((i - g[0],), [(i, whole)]) for i in g]) for g in groups]
     near, side = add_up(outs, held, name="most")
-    ends = [d for ds in diag for d in ds]
+    ends = [d for ds in diag for d in ds[::-1]]
     near = [near, core_flip(near)]
     far = [side, *ends, core_flip(side), *[core_flip(e) for e in ends]]
-    projected = make_project(tokens, near, far, ys, zs)
+    projected, weight_grad = make_project(tokens, near, far, weight_grad, ys, zs)
     return projected, weight_grad.T
 
 

time: 41 us -> 41 us (level)
  Pallas kernels: 6.58 us -> 6.03 us
  starting transfers between devices: 24.3 us -> 24.8 us
    pallas_call x1, Pallas kernels: 0.72 us -> 0.04 us  [finish(): pl.pallas_call(kernel, out_shape=jax.ShapeDtypeStruct((rows, 2 * half), F...]
  transfers between devices with their start and end apart: 22 -> 22, of which waited for: 9 -> 10; matrix products, arithmetic and copies ran while one was open for 0% -> 0% of each run, Pallas kernels for 5% -> 3%
where the time goes in v5:
time: 41 us; the launch traced here: 40.9 us
  starting transfers between devices  24.8 us (60%)
  waiting for transfers between devices  9.33 us (23%)
  Pallas kernels  6.03 us (15%)
  between operations  0.75 us (2%)
    ppermute x22, starting transfers between devices, flip(): return lax.ppermute(entries, axis, [(i, i ^ offset) for i in range(size)])  24.8 us
    ppermute x22, waiting for transfers between devices, flip(): return lax.ppermute(entries, axis, [(i, i ^ offset) for i in range(size)])  9.33 us
    pallas_call x1, Pallas kernels, local_products(): pl.pallas_call(functools.partial(first_kernel, ys, zs), out_shape=(*block...  3.33 us
    pallas_call x1, Pallas kernels, project(): pl.pallas_call(functools.partial(project_kernel, ys, zs, 1), out_shape=(j...  1.44 us
  transfers between devices with their start and end apart: 22, of which 10 were waited for; matrix products, arithmetic and copies ran while one was open for 0% of the time, Pallas kernels for 3%

profile of v5, /device:TPU:0, one launch (start us, length us, event | category | flops | bytes accessed | tf_op | source)
XLA Modules:
  0.0 40.9 jit_solution(9131365095183062420)
XLA Ops:
  0.6 3.3 %first.1 = (bf16[4,4,32,768]{3,2,1,0:T(8,128)(2,1)S(1)}, bf16[4,4,32,768]{3,2,1,0:T(8,128)(2,1)S(1)}, bf16[4,4,32,768]{3,2,1,0:T(8,128)(2,1)S(1)}, bf16[4,4,32,7...) custom-call(bf16[128,12288]{1,0:T(8,128)(2,1)} %tokens.5, bf16[128,128]{1,0:T(8,128)(2,1)} %cot.1, bf16[32,1536]{1,0:T(8,128)(2,1)} %bitcast.3, ...), custom_call_target="tpu_custom_call" | custom-call | flops 402653184 | bytes 6291456 | tf_op jit(solution)/shard_map/first/pallas_call | solution.py:92
  4.0 0.5 %collective-permute-start.1 = (bf16[4,4,32,768]{3,2,1,0:T(8,128)(2,1)S(1)}, bf16[4,4,32,768]{3,2,1,0:T(8,128)(2,1)S(1)}, u32[]{:S(2)}, u32[]{:S(2)}) collective-permute-start(bf16[4,4,32,768]{3,2,1,0:T(8,128)(2,1)S(1)} %get-tuple-element.21), channel_id=1, source_target_pairs={{0,1},{1,0},{2,3},{3,2},{4,5},{5,4},{6,7},{7,6},{8,9},{9,8},{10,11... | collective-permute-start | bytes 2359304 | tf_op jit(solution)/shard_map/ppermute | solution.py:32
  4.5 0.1 collective-permute-start.3
  4.6 4.0 %collective-permute-start = (bf16[2,32,768]{2,1,0:T(8,128)(2,1)S(1)}, bf16[2,32,768]{2,1,0:T(8,128)(2,1)S(1)}, u32[]{:S(2)}, u32[]{:S(2)}) collective-permute-start(bf16[2,32,768]{2,1,0:T(8,128)(2,1)S(1)} %get-tuple-element.19.refs_0_), channel_id=1, source_target_pairs={{0,16},{4,20},{8,24},{12,28},{16,0},{20,4},{24,8},{28,12},{1,17},{... | collective-permute-start | bytes 294920 | tf_op jit(solution)/shard_map/ppermute | solution.py:32
  8.6 0.0 collective-permute-done.1.refs_1_
  8.6 0.2 stage1.1
  8.8 1.6 %collective-permute-start.6 = (bf16[1,4,32,768]{3,2,1,0:T(8,128)(2,1)S(1)}, bf16[1,4,32,768]{3,2,1,0:T(8,128)(2,1)S(1)}, u32[]{:S(2)}, u32[]{:S(2)}) collective-permute-start(bf16[1,4,32,768]{3,2,1,0:T(8,128)(2,1)S(1)} %get-tuple-element.22.refs_2_), channel_id=1, source_target_pairs={{0,4},{4,0},{8,12},{12,8},{16,20},{20,16},{24,28},{28,24},{1,5},{5... | collective-permute-start | bytes 589832 | tf_op jit(solution)/shard_map/ppermute | solution.py:32
  10.3 1.5 %collective-permute-start.7 = (bf16[4,32,768]{2,1,0:T(8,128)(2,1)S(1)}, bf16[4,32,768]{2,1,0:T(8,128)(2,1)S(1)}, u32[]{:S(2)}, u32[]{:S(2)}) collective-permute-start(bf16[4,32,768]{2,1,0:T(8,128)(2,1)S(1)} %get-tuple-element.27), channel_id=1, source_target_pairs={{0,2},{1,3},{2,0},{3,1},{4,6},{5,7},{6,4},{7,5},{8,10},{9,11},{10,... | collective-permute-start | bytes 589832 | tf_op jit(solution)/shard_map/ppermute | solution.py:32
  11.8 0.5 %collective-permute-start.4 = (bf16[4,32,768]{2,1,0:T(8,128)(2,1)S(1)}, bf16[4,32,768]{2,1,0:T(8,128)(2,1)S(1)}, u32[]{:S(2)}, u32[]{:S(2)}) collective-permute-start(bf16[4,32,768]{2,1,0:T(8,128)(2,1)S(1)} %get-tuple-element.25), channel_id=1, source_target_pairs={{0,4},{4,0},{8,12},{12,8},{16,20},{20,16},{24,28},{28,24},{1,5},{5... | collective-permute-start | bytes 589832 | tf_op jit(solution)/shard_map/ppermute | solution.py:32
  12.4 1.3 %collective-permute-done.refs_1_ = bf16[2,32,768]{2,1,0:T(8,128)(2,1)S(1)} collective-permute-done((bf16[2,32,768]{2,1,0:T(8,128)(2,1)S(1)}, bf16[2,32,768]{2,1,0:T(8,128)(2,1)S(1)}, u32[]{:S(2)}, u32[]{:S(2)}) %collective-permute-start) | collective-permute-done | bytes 98336 | tf_op jit(solution)/shard_map/ppermute | solution.py:32
  13.7 1.6 %collective-permute-start.5 = (bf16[4,32,768]{2,1,0:T(8,128)(2,1)S(1)}, bf16[4,32,768]{2,1,0:T(8,128)(2,1)S(1)}, u32[]{:S(2)}, u32[]{:S(2)}) collective-permute-start(bf16[4,32,768]{2,1,0:T(8,128)(2,1)S(1)} %get-tuple-element.26), channel_id=1, source_target_pairs={{0,2},{1,3},{2,0},{3,1},{4,6},{5,7},{6,4},{7,5},{8,10},{9,11},{10,... | collective-permute-start | bytes 589832 | tf_op jit(solution)/shard_map/ppermute | solution.py:32
  15.3 0.0 collective-permute-done.3.refs_1_
  15.3 0.7 %collective-permute-start.2 = (bf16[2,2,32,768]{3,2,1,0:T(8,128)(2,1)S(1)}, bf16[2,2,32,768]{3,2,1,0:T(8,128)(2,1)S(1)}, u32[]{:S(2)}, u32[]{:S(2)}) collective-permute-start(bf16[2,2,32,768]{3,2,1,0:T(8,128)(2,1)S(1)} %widen.1.refs_4_), channel_id=1, source_target_pairs={{0,8},{4,12},{8,0},{12,4},{16,24},{20,28},{24,16},{28,20},{1,9},{5... | collective-permute-start | bytes 589832 | tf_op jit(solution)/shard_map/ppermute | solution.py:32
  16.1 0.6 %collective-permute-done.6.refs_2_ = bf16[1,4,32,768]{3,2,1,0:T(8,128)(2,1)S(1)} collective-permute-done((bf16[1,4,32,768]{3,2,1,0:T(8,128)(2,1)S(1)}, bf16[1,4,32,768]{3,2,1,0:T(8,128)(2,1)S(1)}, u32[]{:S(2)}, u32[]{:S(2)}) %collective-permute-start.6) | collective-permute-done | bytes 196640 | tf_op jit(solution)/shard_map/ppermute | solution.py:32
  16.6 0.7 %collective-permute-done.7.refs_3_ = bf16[4,32,768]{2,1,0:T(8,128)(2,1)S(1)} collective-permute-done((bf16[4,32,768]{2,1,0:T(8,128)(2,1)S(1)}, bf16[4,32,768]{2,1,0:T(8,128)(2,1)S(1)}, u32[]{:S(2)}, u32[]{:S(2)}) %collective-permute-start.7) | collective-permute-done | bytes 196640 | tf_op jit(solution)/shard_map/ppermute | solution.py:32
  17.4 0.1 stage2.1
  17.5 0.8 %collective-permute-start.18 = (bf16[4,32,768]{2,1,0:T(8,128)(2,1)S(1)}, bf16[4,32,768]{2,1,0:T(8,128)(2,1)S(1)}, u32[]{:S(2)}, u32[]{:S(2)}) collective-permute-start(bf16[4,32,768]{2,1,0:T(8,128)(2,1)S(1)} %get-tuple-element.28.refs_4_), channel_id=1, source_target_pairs={{0,4},{4,0},{8,12},{12,8},{16,20},{20,16},{24,28},{28,24},{1,5},{5... | collective-permute-start | bytes 589832 | tf_op jit(solution)/shard_map/ppermute | solution.py:32
  18.3 1.5 %collective-permute-start.19 = (bf16[4,32,768]{2,1,0:T(8,128)(2,1)S(1)}, bf16[4,32,768]{2,1,0:T(8,128)(2,1)S(1)}, u32[]{:S(2)}, u32[]{:S(2)}) collective-permute-start(bf16[4,32,768]{2,1,0:T(8,128)(2,1)S(1)} %get-tuple-element.33), channel_id=1, source_target_pairs={{0,2},{1,3},{2,0},{3,1},{4,6},{5,7},{6,4},{7,5},{8,10},{9,11},{10,... | collective-permute-start | bytes 589832 | tf_op jit(solution)/shard_map/ppermute | solution.py:32
  19.9 1.0 %collective-permute-done.4.refs_2_ = bf16[4,32,768]{2,1,0:T(8,128)(2,1)S(1)} collective-permute-done((bf16[4,32,768]{2,1,0:T(8,128)(2,1)S(1)}, bf16[4,32,768]{2,1,0:T(8,128)(2,1)S(1)}, u32[]{:S(2)}, u32[]{:S(2)}) %collective-permute-start.4) | collective-permute-done | bytes 196640 | tf_op jit(solution)/shard_map/ppermute | solution.py:32
  20.8 0.7 %collective-permute-done.5.refs_3_ = bf16[4,32,768]{2,1,0:T(8,128)(2,1)S(1)} collective-permute-done((bf16[4,32,768]{2,1,0:T(8,128)(2,1)S(1)}, bf16[4,32,768]{2,1,0:T(8,128)(2,1)S(1)}, u32[]{:S(2)}, u32[]{:S(2)}) %collective-permute-start.5) | collective-permute-done | bytes 196640 | tf_op jit(solution)/shard_map/ppermute | solution.py:32
  21.6 0.1 sides.1.refs_3_.refs_0_
  21.7 0.0 copy-start
  21.7 0.0 collective-permute-done.2.refs_2_
  21.8 1.9 %collective-permute-start.9 = (bf16[4,32,768]{2,1,0:T(8,128)(2,1)S(1)}, bf16[4,32,768]{2,1,0:T(8,128)(2,1)S(1)}, u32[]{:S(2)}, u32[]{:S(2)}) collective-permute-start(bf16[4,32,768]{2,1,0:T(8,128)(2,1)S(1)} %get-tuple-element.30.refs_1_), channel_id=1, source_target_pairs={{0,2},{1,3},{2,0},{3,1},{4,6},{5,7},{6,4},{7,5},{8,10},{9,11},{10,... | collective-permute-start | bytes 589832 | tf_op jit(solution)/shard_map/ppermute | solution.py:32
  23.6 1.2 %collective-permute-start.10 = (bf16[4,32,768]{2,1,0:T(8,128)(2,1)S(1)}, bf16[4,32,768]{2,1,0:T(8,128)(2,1)S(1)}, u32[]{:S(2)}, u32[]{:S(2)}) collective-permute-start(bf16[4,32,768]{2,1,0:T(8,128)(2,1)S(1)} %get-tuple-element.29.refs_0_.refs_3_), channel_id=1, source_target_pairs={{0,4},{4,0},{8,12},{12,8},{16,20},{20,16},{24,28},{28,24},{1,5},{5... | collective-permute-start | bytes 589832 | tf_op jit(solution)/shard_map/ppermute | solution.py:32
  24.8 0.0 collective-permute-done.18.refs_1_
  24.8 1.4 %collective-permute-done.19.refs_2_ = bf16[4,32,768]{2,1,0:T(8,128)(2,1)S(1)} collective-permute-done((bf16[4,32,768]{2,1,0:T(8,128)(2,1)S(1)}, bf16[4,32,768]{2,1,0:T(8,128)(2,1)S(1)}, u32[]{:S(2)}, u32[]{:S(2)}) %collective-permute-start.19) | collective-permute-done | bytes 196640 | tf_op jit(solution)/shard_map/ppermute | solution.py:32
  26.2 1.6 %collective-permute-start.20 = (bf16[2,2,32,768]{3,2,1,0:T(8,128)(2,1)S(1)}, bf16[2,2,32,768]{3,2,1,0:T(8,128)(2,1)S(1)}, u32[]{:S(2)}, u32[]{:S(2)}) collective-permute-start(bf16[2,2,32,768]{3,2,1,0:T(8,128)(2,1)S(1)} %plane.2.refs_4_), channel_id=1, source_target_pairs={{0,8},{4,12},{8,0},{12,4},{16,24},{20,28},{24,16},{28,20},{1,9},{5... | collective-permute-start | bytes 589832 | tf_op jit(solution)/shard_map/ppermute | solution.py:32
  27.8 1.1 %collective-permute-start.11 = (bf16[4,32,768]{2,1,0:T(8,128)(2,1)S(1)}, bf16[4,32,768]{2,1,0:T(8,128)(2,1)S(1)}, u32[]{:S(2)}, u32[]{:S(2)}) collective-permute-start(bf16[4,32,768]{2,1,0:T(8,128)(2,1)S(1)} %get-tuple-element.30.refs_1_), channel_id=1, source_target_pairs={{0,4},{4,0},{8,12},{12,8},{16,20},{20,16},{24,28},{28,24},{1,5},{5... | collective-permute-start | bytes 589832 | tf_op jit(solution)/shard_map/ppermute | solution.py:32
  29.0 1.9 %collective-permute-start.8 = (bf16[4,32,768]{2,1,0:T(8,128)(2,1)S(1)}, bf16[4,32,768]{2,1,0:T(8,128)(2,1)S(1)}, u32[]{:S(2)}, u32[]{:S(2)}) collective-permute-start(bf16[4,32,768]{2,1,0:T(8,128)(2,1)S(1)} %get-tuple-element.29.refs_0_.refs_3_), channel_id=1, source_target_pairs={{0,2},{1,3},{2,0},{3,1},{4,6},{5,7},{6,4},{7,5},{8,10},{9,11},{10,... | collective-permute-start | bytes 589832 | tf_op jit(solution)/shard_map/ppermute | solution.py:32
  30.9 0.0 collective-permute-done.9.refs_3_
  30.9 0.5 %collective-permute-start.12 = (bf16[4,32,768]{2,1,0:T(8,128)(2,1)S(1)}, bf16[4,32,768]{2,1,0:T(8,128)(2,1)S(1)}, u32[]{:S(2)}, u32[]{:S(2)}) collective-permute-start(bf16[4,32,768]{2,1,0:T(8,128)(2,1)S(1)} %collective-permute-done.9.refs_3_), channel_id=1, source_target_pairs={{0,4},{4,0},{8,12},{12,8},{16,20},{20,16},{24,28},{28,24},{1,5},{5... | collective-permute-start | bytes 589832 | tf_op jit(solution)/shard_map/ppermute | solution.py:32
  31.4 0.5 %collective-permute-start.13 = (bf16[4,32,768]{2,1,0:T(8,128)(2,1)S(1)}, bf16[4,32,768]{2,1,0:T(8,128)(2,1)S(1)}, u32[]{:S(2)}, u32[]{:S(2)}) collective-permute-start(bf16[4,32,768]{2,1,0:T(8,128)(2,1)S(1)} %collective-permute-done.10.refs_4_), channel_id=1, source_target_pairs={{0,2},{1,3},{2,0},{3,1},{4,6},{5,7},{6,4},{7,5},{8,10},{9,11},{10,... | collective-permute-start | bytes 589832 | tf_op jit(solution)/shard_map/ppermute | solution.py:32
  31.9 0.0 collective-permute-done.20.refs_3_
  32.0 2.1 %collective-permute-start.21 = (bf16[1,2,32,768]{3,2,1,0:T(8,128)(2,1)S(1)}, bf16[1,2,32,768]{3,2,1,0:T(8,128)(2,1)S(1)}, u32[]{:S(2)}, u32[]{:S(2)}) collective-permute-start(bf16[1,2,32,768]{3,2,1,0:T(8,128)(2,1)S(1)} %plane.3), channel_id=1, source_target_pairs={{0,16},{4,20},{8,24},{12,28},{16,0},{20,4},{24,8},{28,12},{1,17},{... | collective-permute-start | bytes 294920 | tf_op jit(solution)/shard_map/ppermute | solution.py:32
  34.1 1.5 %collective-permute-done.11.refs_5_ = bf16[4,32,768]{2,1,0:T(8,128)(2,1)S(1)} collective-permute-done((bf16[4,32,768]{2,1,0:T(8,128)(2,1)S(1)}, bf16[4,32,768]{2,1,0:T(8,128)(2,1)S(1)}, u32[]{:S(2)}, u32[]{:S(2)}) %collective-permute-start.11) | collective-permute-done | bytes 196640 | tf_op jit(solution)/shard_map/ppermute | solution.py:32
  35.6 0.1 most.1
  35.7 0.1 collective-permute-start.17
  35.8 0.5 %collective-permute-start.14 = (bf16[2,4,32,768]{3,2,1,0:T(8,128)(2,1)S(1)}, bf16[2,4,32,768]{3,2,1,0:T(8,128)(2,1)S(1)}, u32[]{:S(2)}, u32[]{:S(2)}) collective-permute-start(bf16[2,4,32,768]{3,2,1,0:T(8,128)(2,1)S(1)} %get-tuple-element.31.refs_0_), channel_id=1, source_target_pairs={{0,1},{1,0},{2,3},{3,2},{4,5},{5,4},{6,7},{7,6},{8,9},{9,8},{10,11... | collective-permute-start | bytes 1179656 | tf_op jit(solution)/shard_map/ppermute | solution.py:32
  36.3 1.4 %collective-permute-done.12.refs_1_ = bf16[4,32,768]{2,1,0:T(8,128)(2,1)S(1)} collective-permute-done((bf16[4,32,768]{2,1,0:T(8,128)(2,1)S(1)}, bf16[4,32,768]{2,1,0:T(8,128)(2,1)S(1)}, u32[]{:S(2)}, u32[]{:S(2)}) %collective-permute-start.12) | collective-permute-done | bytes 196640 | tf_op jit(solution)/shard_map/ppermute | solution.py:32
  37.7 0.0 collective-permute-start.15
  37.7 0.5 %collective-permute-start.16 = (bf16[4,32,768]{2,1,0:T(8,128)(2,1)S(1)}, bf16[4,32,768]{2,1,0:T(8,128)(2,1)S(1)}, u32[]{:S(2)}, u32[]{:S(2)}) collective-permute-start(bf16[4,32,768]{2,1,0:T(8,128)(2,1)S(1)} %collective-permute-done.13.refs_2_), channel_id=1, source_target_pairs={{0,1},{1,0},{2,3},{3,2},{4,5},{5,4},{6,7},{7,6},{8,9},{9,8},{10,11... | collective-permute-start | bytes 589832 | tf_op jit(solution)/shard_map/ppermute | solution.py:32
  38.3 0.0 collective-permute-done.17.refs_1_
  38.3 0.6 %project_near.1.refs_6_ = f32[128,128]{1,0:T(8,128)S(1)} custom-call(bf16[128,12288]{1,0:T(8,128)(2,1)S(1)} %copy-done, bf16[4,4,32,768]{3,2,1,0:T(8,128)(2,1)S(1)} %get-tuple-element.32.refs_0_, bf16[4,4,32,768]{3,2,1,0:T(8,128)(2,1)S(1)} %collective-permute-done.17.refs_1_), custom_call_target="tpu_custom_call" | custom-call | flops 201326592 | bytes 3145728 | tf_op jit(solution)/shard_map/project_near/pallas_call | solution.py:225
  38.9 0.0 collective-permute-done.14.refs_3_
  38.9 0.3 collective-permute-done.15.refs_4_
  39.2 0.3 collective-permute-done.16.refs_5_
  39.4 1.4 %project_far.1 = (bf16[128,128]{1,0:T(8,128)(2,1)}, f32[32,1536]{1,0:T(8,128)}) custom-call(bf16[128,12288]{1,0:T(8,128)(2,1)S(1)} %copy-done, bf16[2,4,32,768]{3,2,1,0:T(8,128)(2,1)S(1)} %get-tuple-element.31.refs_0_, bf16[4,32,768]{2,1,0:T(8,128)(2,1)S(1)} %collective-permute-done.12.refs_1_, bf16[4,32,768]{2,1,0:T(8,128)(2,1)S(1)} %collective-permute-done.13.refs_2_, ...), custom_call_target="tpu_custom_call" | custom-call | flops 201326592 | bytes 3145728 | tf_op jit(solution)/shard_map/project_far/pallas_call | solution.py:234
  (10 shorter events, 0.2 us)
Async XLA Ops:
  4.0 4.6 %collective-permute-start.1 = (bf16[4,4,32,768]{3,2,1,0:T(8,128)(2,1)S(1)}, bf16[4,4,32,768]{3,2,1,0:T(8,128)(2,1)S(1)}, u32[]{:S(2)}, u32[]{:S(2)}) collective-permute-start(bf16[4,4,32,768]{3,2,1,0:T(8,128)(2,1)S(1)} %get-tuple-element.21), channel_id=1, source_target_pairs={{0,1},{1,0},{2,3},{3,2},{4,5},{5,4},{6,7},{7,6},{8,9},{9,8},{10,11... | collective-permute-start | bytes 2359304 | tf_op jit(solution)/shard_map/ppermute | solution.py:32
  4.5 10.8 %collective-permute-start.3 = (bf16[4,4,32,768]{3,2,1,0:T(8,128)(2,1)S(1)}, bf16[4,4,32,768]{3,2,1,0:T(8,128)(2,1)S(1)}, u32[]{:S(2)}, u32[]{:S(2)}) collective-permute-start(bf16[4,4,32,768]{3,2,1,0:T(8,128)(2,1)S(1)} %get-tuple-element.24), channel_id=1, source_target_pairs={{0,1},{1,0},{2,3},{3,2},{4,5},{5,4},{6,7},{7,6},{8,9},{9,8},{10,11... | collective-permute-start | bytes 2359304 | tf_op jit(solution)/shard_map/ppermute | solution.py:32
  4.6 9.2 %collective-permute-start = (bf16[2,32,768]{2,1,0:T(8,128)(2,1)S(1)}, bf16[2,32,768]{2,1,0:T(8,128)(2,1)S(1)}, u32[]{:S(2)}, u32[]{:S(2)}) collective-permute-start(bf16[2,32,768]{2,1,0:T(8,128)(2,1)S(1)} %get-tuple-element.19.refs_0_), channel_id=1, source_target_pairs={{0,16},{4,20},{8,24},{12,28},{16,0},{20,4},{24,8},{28,12},{1,17},{... | collective-permute-start | bytes 294920 | tf_op jit(solution)/shard_map/ppermute | solution.py:32
  8.8 7.9 %collective-permute-start.6 = (bf16[1,4,32,768]{3,2,1,0:T(8,128)(2,1)S(1)}, bf16[1,4,32,768]{3,2,1,0:T(8,128)(2,1)S(1)}, u32[]{:S(2)}, u32[]{:S(2)}) collective-permute-start(bf16[1,4,32,768]{3,2,1,0:T(8,128)(2,1)S(1)} %get-tuple-element.22.refs_2_), channel_id=1, source_target_pairs={{0,4},{4,0},{8,12},{12,8},{16,20},{20,16},{24,28},{28,24},{1,5},{5... | collective-permute-start | bytes 589832 | tf_op jit(solution)/shard_map/ppermute | solution.py:32
  10.3 7.0 %collective-permute-start.7 = (bf16[4,32,768]{2,1,0:T(8,128)(2,1)S(1)}, bf16[4,32,768]{2,1,0:T(8,128)(2,1)S(1)}, u32[]{:S(2)}, u32[]{:S(2)}) collective-permute-start(bf16[4,32,768]{2,1,0:T(8,128)(2,1)S(1)} %get-tuple-element.27), channel_id=1, source_target_pairs={{0,2},{1,3},{2,0},{3,1},{4,6},{5,7},{6,4},{7,5},{8,10},{9,11},{10,... | collective-permute-start | bytes 589832 | tf_op jit(solution)/shard_map/ppermute | solution.py:32
  11.8 9.0 %collective-permute-start.4 = (bf16[4,32,768]{2,1,0:T(8,128)(2,1)S(1)}, bf16[4,32,768]{2,1,0:T(8,128)(2,1)S(1)}, u32[]{:S(2)}, u32[]{:S(2)}) collective-permute-start(bf16[4,32,768]{2,1,0:T(8,128)(2,1)S(1)} %get-tuple-element.25), channel_id=1, source_target_pairs={{0,4},{4,0},{8,12},{12,8},{16,20},{20,16},{24,28},{28,24},{1,5},{5... | collective-permute-start | bytes 589832 | tf_op jit(solution)/shard_map/ppermute | solution.py:32
  13.7 7.8 %collective-permute-start.5 = (bf16[4,32,768]{2,1,0:T(8,128)(2,1)S(1)}, bf16[4,32,768]{2,1,0:T(8,128)(2,1)S(1)}, u32[]{:S(2)}, u32[]{:S(2)}) collective-permute-start(bf16[4,32,768]{2,1,0:T(8,128)(2,1)S(1)} %get-tuple-element.26), channel_id=1, source_target_pairs={{0,2},{1,3},{2,0},{3,1},{4,6},{5,7},{6,4},{7,5},{8,10},{9,11},{10,... | collective-permute-start | bytes 589832 | tf_op jit(solution)/shard_map/ppermute | solution.py:32
  15.3 6.4 %collective-permute-start.2 = (bf16[2,2,32,768]{3,2,1,0:T(8,128)(2,1)S(1)}, bf16[2,2,32,768]{3,2,1,0:T(8,128)(2,1)S(1)}, u32[]{:S(2)}, u32[]{:S(2)}) collective-permute-start(bf16[2,2,32,768]{3,2,1,0:T(8,128)(2,1)S(1)} %widen.1.refs_4_), channel_id=1, source_target_pairs={{0,8},{4,12},{8,0},{12,4},{16,24},{20,28},{24,16},{28,20},{1,9},{5... | collective-permute-start | bytes 589832 | tf_op jit(solution)/shard_map/ppermute | solution.py:32
  17.5 7.3 %collective-permute-start.18 = (bf16[4,32,768]{2,1,0:T(8,128)(2,1)S(1)}, bf16[4,32,768]{2,1,0:T(8,128)(2,1)S(1)}, u32[]{:S(2)}, u32[]{:S(2)}) collective-permute-start(bf16[4,32,768]{2,1,0:T(8,128)(2,1)S(1)} %get-tuple-element.28.refs_4_), channel_id=1, source_target_pairs={{0,4},{4,0},{8,12},{12,8},{16,20},{20,16},{24,28},{28,24},{1,5},{5... | collective-permute-start | bytes 589832 | tf_op jit(solution)/shard_map/ppermute | solution.py:32
  18.3 7.8 %collective-permute-start.19 = (bf16[4,32,768]{2,1,0:T(8,128)(2,1)S(1)}, bf16[4,32,768]{2,1,0:T(8,128)(2,1)S(1)}, u32[]{:S(2)}, u32[]{:S(2)}) collective-permute-start(bf16[4,32,768]{2,1,0:T(8,128)(2,1)S(1)} %get-tuple-element.33), channel_id=1, source_target_pairs={{0,2},{1,3},{2,0},{3,1},{4,6},{5,7},{6,4},{7,5},{8,10},{9,11},{10,... | collective-permute-start | bytes 589832 | tf_op jit(solution)/shard_map/ppermute | solution.py:32
  21.7 16.5 %copy-start = (bf16[128,12288]{1,0:T(8,128)(2,1)S(1)}, bf16[128,12288]{1,0:T(8,128)(2,1)}, u32[]{:S(2)}) copy-start(bf16[128,12288]{1,0:T(8,128)(2,1)} %tokens.5) | copy-start | bytes 9437188
  21.8 9.1 %collective-permute-start.9 = (bf16[4,32,768]{2,1,0:T(8,128)(2,1)S(1)}, bf16[4,32,768]{2,1,0:T(8,128)(2,1)S(1)}, u32[]{:S(2)}, u32[]{:S(2)}) collective-permute-start(bf16[4,32,768]{2,1,0:T(8,128)(2,1)S(1)} %get-tuple-element.30.refs_1_), channel_id=1, source_target_pairs={{0,2},{1,3},{2,0},{3,1},{4,6},{5,7},{6,4},{7,5},{8,10},{9,11},{10,... | collective-permute-start | bytes 589832 | tf_op jit(solution)/shard_map/ppermute | solution.py:32
  23.6 7.8 %collective-permute-start.10 = (bf16[4,32,768]{2,1,0:T(8,128)(2,1)S(1)}, bf16[4,32,768]{2,1,0:T(8,128)(2,1)S(1)}, u32[]{:S(2)}, u32[]{:S(2)}) collective-permute-start(bf16[4,32,768]{2,1,0:T(8,128)(2,1)S(1)} %get-tuple-element.29.refs_0_.refs_3_), channel_id=1, source_target_pairs={{0,4},{4,0},{8,12},{12,8},{16,20},{20,16},{24,28},{28,24},{1,5},{5... | collective-permute-start | bytes 589832 | tf_op jit(solution)/shard_map/ppermute | solution.py:32
  26.2 5.7 %collective-permute-start.20 = (bf16[2,2,32,768]{3,2,1,0:T(8,128)(2,1)S(1)}, bf16[2,2,32,768]{3,2,1,0:T(8,128)(2,1)S(1)}, u32[]{:S(2)}, u32[]{:S(2)}) collective-permute-start(bf16[2,2,32,768]{3,2,1,0:T(8,128)(2,1)S(1)} %plane.2.refs_4_), channel_id=1, source_target_pairs={{0,8},{4,12},{8,0},{12,4},{16,24},{20,28},{24,16},{28,20},{1,9},{5... | collective-permute-start | bytes 589832 | tf_op jit(solution)/shard_map/ppermute | solution.py:32
  27.8 7.8 %collective-permute-start.11 = (bf16[4,32,768]{2,1,0:T(8,128)(2,1)S(1)}, bf16[4,32,768]{2,1,0:T(8,128)(2,1)S(1)}, u32[]{:S(2)}, u32[]{:S(2)}) collective-permute-start(bf16[4,32,768]{2,1,0:T(8,128)(2,1)S(1)} %get-tuple-element.30.refs_1_), channel_id=1, source_target_pairs={{0,4},{4,0},{8,12},{12,8},{16,20},{20,16},{24,28},{28,24},{1,5},{5... | collective-permute-start | bytes 589832 | tf_op jit(solution)/shard_map/ppermute | solution.py:32
  29.0 6.7 %collective-permute-start.8 = (bf16[4,32,768]{2,1,0:T(8,128)(2,1)S(1)}, bf16[4,32,768]{2,1,0:T(8,128)(2,1)S(1)}, u32[]{:S(2)}, u32[]{:S(2)}) collective-permute-start(bf16[4,32,768]{2,1,0:T(8,128)(2,1)S(1)} %get-tuple-element.29.refs_0_.refs_3_), channel_id=1, source_target_pairs={{0,2},{1,3},{2,0},{3,1},{4,6},{5,7},{6,4},{7,5},{8,10},{9,11},{10,... | collective-permute-start | bytes 589832 | tf_op jit(solution)/shard_map/ppermute | solution.py:32
  30.9 6.9 %collective-permute-start.12 = (bf16[4,32,768]{2,1,0:T(8,128)(2,1)S(1)}, bf16[4,32,768]{2,1,0:T(8,128)(2,1)S(1)}, u32[]{:S(2)}, u32[]{:S(2)}) collective-permute-start(bf16[4,32,768]{2,1,0:T(8,128)(2,1)S(1)} %collective-permute-done.9.refs_3_), channel_id=1, source_target_pairs={{0,4},{4,0},{8,12},{12,8},{16,20},{20,16},{24,28},{28,24},{1,5},{5... | collective-permute-start | bytes 589832 | tf_op jit(solution)/shard_map/ppermute | solution.py:32
  31.4 6.3 %collective-permute-start.13 = (bf16[4,32,768]{2,1,0:T(8,128)(2,1)S(1)}, bf16[4,32,768]{2,1,0:T(8,128)(2,1)S(1)}, u32[]{:S(2)}, u32[]{:S(2)}) collective-permute-start(bf16[4,32,768]{2,1,0:T(8,128)(2,1)S(1)} %collective-permute-done.10.refs_4_), channel_id=1, source_target_pairs={{0,2},{1,3},{2,0},{3,1},{4,6},{5,7},{6,4},{7,5},{8,10},{9,11},{10,... | collective-permute-start | bytes 589832 | tf_op jit(solution)/shard_map/ppermute | solution.py:32
  32.0 6.2 %collective-permute-start.21 = (bf16[1,2,32,768]{3,2,1,0:T(8,128)(2,1)S(1)}, bf16[1,2,32,768]{3,2,1,0:T(8,128)(2,1)S(1)}, u32[]{:S(2)}, u32[]{:S(2)}) collective-permute-start(bf16[1,2,32,768]{3,2,1,0:T(8,128)(2,1)S(1)} %plane.3), channel_id=1, source_target_pairs={{0,16},{4,20},{8,24},{12,28},{16,0},{20,4},{24,8},{28,12},{1,17},{... | collective-permute-start | bytes 294920 | tf_op jit(solution)/shard_map/ppermute | solution.py:32
  35.7 2.6 %collective-permute-start.17 = (bf16[4,4,32,768]{3,2,1,0:T(8,128)(2,1)S(1)}, bf16[4,4,32,768]{3,2,1,0:T(8,128)(2,1)S(1)}, u32[]{:S(2)}, u32[]{:S(2)}) collective-permute-start(bf16[4,4,32,768]{3,2,1,0:T(8,128)(2,1)S(1)} %get-tuple-element.32.refs_0_), channel_id=1, source_target_pairs={{0,1},{1,0},{2,3},{3,2},{4,5},{5,4},{6,7},{7,6},{8,9},{9,8},{10,11... | collective-permute-start | bytes 2359304 | tf_op jit(solution)/shard_map/ppermute | solution.py:32
  35.8 3.1 %collective-permute-start.14 = (bf16[2,4,32,768]{3,2,1,0:T(8,128)(2,1)S(1)}, bf16[2,4,32,768]{3,2,1,0:T(8,128)(2,1)S(1)}, u32[]{:S(2)}, u32[]{:S(2)}) collective-permute-start(bf16[2,4,32,768]{3,2,1,0:T(8,128)(2,1)S(1)} %get-tuple-element.31.refs_0_), channel_id=1, source_target_pairs={{0,1},{1,0},{2,3},{3,2},{4,5},{5,4},{6,7},{7,6},{8,9},{9,8},{10,11... | collective-permute-start | bytes 1179656 | tf_op jit(solution)/shard_map/ppermute | solution.py:32
  37.7 1.4 %collective-permute-start.15 = (bf16[4,32,768]{2,1,0:T(8,128)(2,1)S(1)}, bf16[4,32,768]{2,1,0:T(8,128)(2,1)S(1)}, u32[]{:S(2)}, u32[]{:S(2)}) collective-permute-start(bf16[4,32,768]{2,1,0:T(8,128)(2,1)S(1)} %collective-permute-done.12.refs_1_), channel_id=1, source_target_pairs={{0,1},{1,0},{2,3},{3,2},{4,5},{5,4},{6,7},{7,6},{8,9},{9,8},{10,11... | collective-permute-start | bytes 589832 | tf_op jit(solution)/shard_map/ppermute | solution.py:32
  37.7 1.7 %collective-permute-start.16 = (bf16[4,32,768]{2,1,0:T(8,128)(2,1)S(1)}, bf16[4,32,768]{2,1,0:T(8,128)(2,1)S(1)}, u32[]{:S(2)}, u32[]{:S(2)}) collective-permute-start(bf16[4,32,768]{2,1,0:T(8,128)(2,1)S(1)} %collective-permute-done.13.refs_2_), channel_id=1, source_target_pairs={{0,1},{1,0},{2,3},{3,2},{4,5},{5,4},{6,7},{7,6},{8,9},{9,8},{10,11... | collective-permute-start | bytes 589832 | tf_op jit(solution)/shard_map/ppermute | solution.py:32

commit v6 on v5

--- a/solution.py
+++ b/solution.py
@@ -202,7 +202,7 @@
                 held = weights[count * (n % 2) : count * (n % 2 + 1)]
                 y = n // 2
                 if x and y:
-                    picked.append(held[1 + 2 * (y - 1) + 1 - h][z])
+                    picked.append(held[1 + 2 * (y - 1) + h][z])
                 else:
                     picked.append(held[0][2 * y + h, z])
             left = jnp.concatenate(picked, axis=0)
@@ -251,11 +251,7 @@
     pieces = pieces.reshape(tokens.shape[0], zs, 2, 2, half)
     count = len(far) // 2
     weights = [
-        jnp.concatenate(
-            [near[c], far[count * c]]
-            + [far[count * c + 1 + 2 * y + 1 - h][None] for y in range(ys - 1) for h in range(2)]
-        )
-        for c in range(2)
+        jnp.concatenate([near[c], far[count * c], jnp.stack(far[count * c + 1 : count * (c + 1)])]) for c in range(2)
     ]
     total = []
     for n in range(2 * ys):
@@ -368,7 +364,7 @@
     groups = [range(2 * ys), range(2 * ys, 2 * ys + 2)]
     outs = [((len(g), *one), [((i - g[0],), [(i, whole)]) for i in g]) for g in groups]
     near, side = add_up(outs, held, name="most")
-    ends = [d for ds in diag for d in ds[::-1]]
+    ends = [d for ds in diag for d in ds]
     near = [near, core_flip(near)]
     far = [side, *ends, core_flip(side), *[core_flip(e) for e in ends]]
     projected, weight_grad = make_project(tokens, near, far, weight_grad, ys, zs)

time: 41 us -> 41 us (level)
  starting transfers between devices: 24.8 us -> 24.3 us
  waiting for transfers between devices: 9.33 us -> 9.74 us
    ppermute x22, waiting for transfers between devices: 9.33 us -> 9.74 us  [flip(): return lax.ppermute(entries, axis, [(i, i ^ offset) for i in range(size)])]
  transfers between devices with their start and end apart: 22 -> 22, of which waited for: 10 -> 11; matrix products, arithmetic and copies ran while one was open for 0% -> 0% of each run, Pallas kernels for 3% -> 3%
where the time goes in v6:
time: 41 us; the launch traced here: 40.9 us
  starting transfers between devices  24.3 us (59%)
  waiting for transfers between devices  9.74 us (24%)
  Pallas kernels  6.04 us (15%)
  between operations  0.75 us (2%)
    ppermute x22, starting transfers between devices, flip(): return lax.ppermute(entries, axis, [(i, i ^ offset) for i in range(size)])  24.3 us
    ppermute x22, waiting for transfers between devices, flip(): return lax.ppermute(entries, axis, [(i, i ^ offset) for i in range(size)])  9.74 us
    pallas_call x1, Pallas kernels, local_products(): pl.pallas_call(functools.partial(first_kernel, ys, zs), out_shape=(*block...  3.33 us
    pallas_call x1, Pallas kernels, project(): pl.pallas_call(functools.partial(project_kernel, ys, zs, 1), out_shape=(j...  1.45 us
  transfers between devices with their start and end apart: 22, of which 11 were waited for; matrix products, arithmetic and copies ran while one was open for 0% of the time, Pallas kernels for 3%

profile of v6, /device:TPU:0, one launch (start us, length us, event | category | flops | bytes accessed | tf_op | source)
XLA Modules:
  0.0 40.9 jit_solution(17588335600137691066)
XLA Ops:
  0.6 3.3 %first.1 = (bf16[4,4,32,768]{3,2,1,0:T(8,128)(2,1)S(1)}, bf16[4,4,32,768]{3,2,1,0:T(8,128)(2,1)S(1)}, bf16[4,4,32,768]{3,2,1,0:T(8,128)(2,1)S(1)}, bf16[4,4,32,7...) custom-call(bf16[128,12288]{1,0:T(8,128)(2,1)} %tokens.5, bf16[128,128]{1,0:T(8,128)(2,1)} %cot.1, bf16[32,1536]{1,0:T(8,128)(2,1)} %bitcast.3, ...), custom_call_target="tpu_custom_call" | custom-call | flops 402653184 | bytes 6291456 | tf_op jit(solution)/shard_map/first/pallas_call | solution.py:92
  4.0 0.5 %collective-permute-start.1 = (bf16[4,4,32,768]{3,2,1,0:T(8,128)(2,1)S(1)}, bf16[4,4,32,768]{3,2,1,0:T(8,128)(2,1)S(1)}, u32[]{:S(2)}, u32[]{:S(2)}) collective-permute-start(bf16[4,4,32,768]{3,2,1,0:T(8,128)(2,1)S(1)} %get-tuple-element.21), channel_id=1, source_target_pairs={{0,1},{1,0},{2,3},{3,2},{4,5},{5,4},{6,7},{7,6},{8,9},{9,8},{10,11... | collective-permute-start | bytes 2359304 | tf_op jit(solution)/shard_map/ppermute | solution.py:32
  4.5 0.1 collective-permute-start.3
  4.6 4.0 %collective-permute-start = (bf16[2,32,768]{2,1,0:T(8,128)(2,1)S(1)}, bf16[2,32,768]{2,1,0:T(8,128)(2,1)S(1)}, u32[]{:S(2)}, u32[]{:S(2)}) collective-permute-start(bf16[2,32,768]{2,1,0:T(8,128)(2,1)S(1)} %get-tuple-element.19.refs_0_), channel_id=1, source_target_pairs={{0,16},{4,20},{8,24},{12,28},{16,0},{20,4},{24,8},{28,12},{1,17},{... | collective-permute-start | bytes 294920 | tf_op jit(solution)/shard_map/ppermute | solution.py:32
  8.6 0.0 collective-permute-done.1.refs_1_
  8.6 0.2 stage1.1
  8.8 1.6 %collective-permute-start.6 = (bf16[1,4,32,768]{3,2,1,0:T(8,128)(2,1)S(1)}, bf16[1,4,32,768]{3,2,1,0:T(8,128)(2,1)S(1)}, u32[]{:S(2)}, u32[]{:S(2)}) collective-permute-start(bf16[1,4,32,768]{3,2,1,0:T(8,128)(2,1)S(1)} %get-tuple-element.22.refs_2_), channel_id=1, source_target_pairs={{0,4},{4,0},{8,12},{12,8},{16,20},{20,16},{24,28},{28,24},{1,5},{5... | collective-permute-start | bytes 589832 | tf_op jit(solution)/shard_map/ppermute | solution.py:32
  10.3 1.5 %collective-permute-start.7 = (bf16[4,32,768]{2,1,0:T(8,128)(2,1)S(1)}, bf16[4,32,768]{2,1,0:T(8,128)(2,1)S(1)}, u32[]{:S(2)}, u32[]{:S(2)}) collective-permute-start(bf16[4,32,768]{2,1,0:T(8,128)(2,1)S(1)} %get-tuple-element.27), channel_id=1, source_target_pairs={{0,2},{1,3},{2,0},{3,1},{4,6},{5,7},{6,4},{7,5},{8,10},{9,11},{10,... | collective-permute-start | bytes 589832 | tf_op jit(solution)/shard_map/ppermute | solution.py:32
  11.8 0.5 %collective-permute-start.4 = (bf16[4,32,768]{2,1,0:T(8,128)(2,1)S(1)}, bf16[4,32,768]{2,1,0:T(8,128)(2,1)S(1)}, u32[]{:S(2)}, u32[]{:S(2)}) collective-permute-start(bf16[4,32,768]{2,1,0:T(8,128)(2,1)S(1)} %get-tuple-element.25), channel_id=1, source_target_pairs={{0,4},{4,0},{8,12},{12,8},{16,20},{20,16},{24,28},{28,24},{1,5},{5... | collective-permute-start | bytes 589832 | tf_op jit(solution)/shard_map/ppermute | solution.py:32
  12.4 1.3 %collective-permute-done.refs_1_ = bf16[2,32,768]{2,1,0:T(8,128)(2,1)S(1)} collective-permute-done((bf16[2,32,768]{2,1,0:T(8,128)(2,1)S(1)}, bf16[2,32,768]{2,1,0:T(8,128)(2,1)S(1)}, u32[]{:S(2)}, u32[]{:S(2)}) %collective-permute-start) | collective-permute-done | bytes 98336 | tf_op jit(solution)/shard_map/ppermute | solution.py:32
  13.7 1.6 %collective-permute-start.5 = (bf16[4,32,768]{2,1,0:T(8,128)(2,1)S(1)}, bf16[4,32,768]{2,1,0:T(8,128)(2,1)S(1)}, u32[]{:S(2)}, u32[]{:S(2)}) collective-permute-start(bf16[4,32,768]{2,1,0:T(8,128)(2,1)S(1)} %get-tuple-element.26), channel_id=1, source_target_pairs={{0,2},{1,3},{2,0},{3,1},{4,6},{5,7},{6,4},{7,5},{8,10},{9,11},{10,... | collective-permute-start | bytes 589832 | tf_op jit(solution)/shard_map/ppermute | solution.py:32
  15.3 0.0 collective-permute-done.3.refs_1_
  15.3 0.7 %collective-permute-start.2 = (bf16[2,2,32,768]{3,2,1,0:T(8,128)(2,1)S(1)}, bf16[2,2,32,768]{3,2,1,0:T(8,128)(2,1)S(1)}, u32[]{:S(2)}, u32[]{:S(2)}) collective-permute-start(bf16[2,2,32,768]{3,2,1,0:T(8,128)(2,1)S(1)} %widen.1.refs_4_), channel_id=1, source_target_pairs={{0,8},{4,12},{8,0},{12,4},{16,24},{20,28},{24,16},{28,20},{1,9},{5... | collective-permute-start | bytes 589832 | tf_op jit(solution)/shard_map/ppermute | solution.py:32
  16.1 0.6 %collective-permute-done.6.refs_2_ = bf16[1,4,32,768]{3,2,1,0:T(8,128)(2,1)S(1)} collective-permute-done((bf16[1,4,32,768]{3,2,1,0:T(8,128)(2,1)S(1)}, bf16[1,4,32,768]{3,2,1,0:T(8,128)(2,1)S(1)}, u32[]{:S(2)}, u32[]{:S(2)}) %collective-permute-start.6) | collective-permute-done | bytes 196640 | tf_op jit(solution)/shard_map/ppermute | solution.py:32
  16.6 0.7 %collective-permute-done.7.refs_3_ = bf16[4,32,768]{2,1,0:T(8,128)(2,1)S(1)} collective-permute-done((bf16[4,32,768]{2,1,0:T(8,128)(2,1)S(1)}, bf16[4,32,768]{2,1,0:T(8,128)(2,1)S(1)}, u32[]{:S(2)}, u32[]{:S(2)}) %collective-permute-start.7) | collective-permute-done | bytes 196640 | tf_op jit(solution)/shard_map/ppermute | solution.py:32
  17.4 0.1 stage2.1
  17.5 0.8 %collective-permute-start.18 = (bf16[4,32,768]{2,1,0:T(8,128)(2,1)S(1)}, bf16[4,32,768]{2,1,0:T(8,128)(2,1)S(1)}, u32[]{:S(2)}, u32[]{:S(2)}) collective-permute-start(bf16[4,32,768]{2,1,0:T(8,128)(2,1)S(1)} %get-tuple-element.28.refs_4_), channel_id=1, source_target_pairs={{0,4},{4,0},{8,12},{12,8},{16,20},{20,16},{24,28},{28,24},{1,5},{5... | collective-permute-start | bytes 589832 | tf_op jit(solution)/shard_map/ppermute | solution.py:32
  18.3 1.5 %collective-permute-start.19 = (bf16[4,32,768]{2,1,0:T(8,128)(2,1)S(1)}, bf16[4,32,768]{2,1,0:T(8,128)(2,1)S(1)}, u32[]{:S(2)}, u32[]{:S(2)}) collective-permute-start(bf16[4,32,768]{2,1,0:T(8,128)(2,1)S(1)} %get-tuple-element.33), channel_id=1, source_target_pairs={{0,2},{1,3},{2,0},{3,1},{4,6},{5,7},{6,4},{7,5},{8,10},{9,11},{10,... | collective-permute-start | bytes 589832 | tf_op jit(solution)/shard_map/ppermute | solution.py:32
  19.9 1.0 %collective-permute-done.4.refs_2_ = bf16[4,32,768]{2,1,0:T(8,128)(2,1)S(1)} collective-permute-done((bf16[4,32,768]{2,1,0:T(8,128)(2,1)S(1)}, bf16[4,32,768]{2,1,0:T(8,128)(2,1)S(1)}, u32[]{:S(2)}, u32[]{:S(2)}) %collective-permute-start.4) | collective-permute-done | bytes 196640 | tf_op jit(solution)/shard_map/ppermute | solution.py:32
  20.8 0.7 %collective-permute-done.5.refs_3_ = bf16[4,32,768]{2,1,0:T(8,128)(2,1)S(1)} collective-permute-done((bf16[4,32,768]{2,1,0:T(8,128)(2,1)S(1)}, bf16[4,32,768]{2,1,0:T(8,128)(2,1)S(1)}, u32[]{:S(2)}, u32[]{:S(2)}) %collective-permute-start.5) | collective-permute-done | bytes 196640 | tf_op jit(solution)/shard_map/ppermute | solution.py:32
  21.6 0.1 sides.1.refs_3_.refs_0_
  21.7 0.0 copy-start
  21.7 0.0 collective-permute-done.2.refs_2_
  21.8 1.2 %collective-permute-start.10 = (bf16[4,32,768]{2,1,0:T(8,128)(2,1)S(1)}, bf16[4,32,768]{2,1,0:T(8,128)(2,1)S(1)}, u32[]{:S(2)}, u32[]{:S(2)}) collective-permute-start(bf16[4,32,768]{2,1,0:T(8,128)(2,1)S(1)} %get-tuple-element.29.refs_0_.refs_3_), channel_id=1, source_target_pairs={{0,4},{4,0},{8,12},{12,8},{16,20},{20,16},{24,28},{28,24},{1,5},{5... | collective-permute-start | bytes 589832 | tf_op jit(solution)/shard_map/ppermute | solution.py:32
  22.9 1.8 %collective-permute-start.9 = (bf16[4,32,768]{2,1,0:T(8,128)(2,1)S(1)}, bf16[4,32,768]{2,1,0:T(8,128)(2,1)S(1)}, u32[]{:S(2)}, u32[]{:S(2)}) collective-permute-start(bf16[4,32,768]{2,1,0:T(8,128)(2,1)S(1)} %get-tuple-element.30.refs_1_), channel_id=1, source_target_pairs={{0,2},{1,3},{2,0},{3,1},{4,6},{5,7},{6,4},{7,5},{8,10},{9,11},{10,... | collective-permute-start | bytes 589832 | tf_op jit(solution)/shard_map/ppermute | solution.py:32
  24.8 0.0 collective-permute-done.18.refs_1_
  24.8 1.4 %collective-permute-done.19.refs_2_ = bf16[4,32,768]{2,1,0:T(8,128)(2,1)S(1)} collective-permute-done((bf16[4,32,768]{2,1,0:T(8,128)(2,1)S(1)}, bf16[4,32,768]{2,1,0:T(8,128)(2,1)S(1)}, u32[]{:S(2)}, u32[]{:S(2)}) %collective-permute-start.19) | collective-permute-done | bytes 196640 | tf_op jit(solution)/shard_map/ppermute | solution.py:32
  26.2 1.6 %collective-permute-start.20 = (bf16[2,2,32,768]{3,2,1,0:T(8,128)(2,1)S(1)}, bf16[2,2,32,768]{3,2,1,0:T(8,128)(2,1)S(1)}, u32[]{:S(2)}, u32[]{:S(2)}) collective-permute-start(bf16[2,2,32,768]{3,2,1,0:T(8,128)(2,1)S(1)} %plane.2.refs_4_), channel_id=1, source_target_pairs={{0,8},{4,12},{8,0},{12,4},{16,24},{20,28},{24,16},{28,20},{1,9},{5... | collective-permute-start | bytes 589832 | tf_op jit(solution)/shard_map/ppermute | solution.py:32
  27.8 0.7 %collective-permute-start.11 = (bf16[4,32,768]{2,1,0:T(8,128)(2,1)S(1)}, bf16[4,32,768]{2,1,0:T(8,128)(2,1)S(1)}, u32[]{:S(2)}, u32[]{:S(2)}) collective-permute-start(bf16[4,32,768]{2,1,0:T(8,128)(2,1)S(1)} %get-tuple-element.30.refs_1_), channel_id=1, source_target_pairs={{0,4},{4,0},{8,12},{12,8},{16,20},{20,16},{24,28},{28,24},{1,5},{5... | collective-permute-start | bytes 589832 | tf_op jit(solution)/shard_map/ppermute | solution.py:32
  28.5 1.5 %collective-permute-start.8 = (bf16[4,32,768]{2,1,0:T(8,128)(2,1)S(1)}, bf16[4,32,768]{2,1,0:T(8,128)(2,1)S(1)}, u32[]{:S(2)}, u32[]{:S(2)}) collective-permute-start(bf16[4,32,768]{2,1,0:T(8,128)(2,1)S(1)} %get-tuple-element.29.refs_0_.refs_3_), channel_id=1, source_target_pairs={{0,2},{1,3},{2,0},{3,1},{4,6},{5,7},{6,4},{7,5},{8,10},{9,11},{10,... | collective-permute-start | bytes 589832 | tf_op jit(solution)/shard_map/ppermute | solution.py:32
  30.0 0.5 %collective-permute-start.12 = (bf16[4,32,768]{2,1,0:T(8,128)(2,1)S(1)}, bf16[4,32,768]{2,1,0:T(8,128)(2,1)S(1)}, u32[]{:S(2)}, u32[]{:S(2)}) collective-permute-start(bf16[4,32,768]{2,1,0:T(8,128)(2,1)S(1)} %collective-permute-done.10.refs_4_), channel_id=1, source_target_pairs={{0,2},{1,3},{2,0},{3,1},{4,6},{5,7},{6,4},{7,5},{8,10},{9,11},{10,... | collective-permute-start | bytes 589832 | tf_op jit(solution)/shard_map/ppermute | solution.py:32
  30.5 1.7 %collective-permute-start.13 = (bf16[4,32,768]{2,1,0:T(8,128)(2,1)S(1)}, bf16[4,32,768]{2,1,0:T(8,128)(2,1)S(1)}, u32[]{:S(2)}, u32[]{:S(2)}) collective-permute-start(bf16[4,32,768]{2,1,0:T(8,128)(2,1)S(1)} %collective-permute-done.9.refs_3_), channel_id=1, source_target_pairs={{0,4},{4,0},{8,12},{12,8},{16,20},{20,16},{24,28},{28,24},{1,5},{5... | collective-permute-start | bytes 589832 | tf_op jit(solution)/shard_map/ppermute | solution.py:32
  32.3 1.4 %collective-permute-start.21 = (bf16[1,2,32,768]{3,2,1,0:T(8,128)(2,1)S(1)}, bf16[1,2,32,768]{3,2,1,0:T(8,128)(2,1)S(1)}, u32[]{:S(2)}, u32[]{:S(2)}) collective-permute-start(bf16[1,2,32,768]{3,2,1,0:T(8,128)(2,1)S(1)} %plane.3), channel_id=1, source_target_pairs={{0,16},{4,20},{8,24},{12,28},{16,0},{20,4},{24,8},{28,12},{1,17},{... | collective-permute-start | bytes 294920 | tf_op jit(solution)/shard_map/ppermute | solution.py:32
  33.6 1.1 %collective-permute-done.11.refs_5_ = bf16[4,32,768]{2,1,0:T(8,128)(2,1)S(1)} collective-permute-done((bf16[4,32,768]{2,1,0:T(8,128)(2,1)S(1)}, bf16[4,32,768]{2,1,0:T(8,128)(2,1)S(1)}, u32[]{:S(2)}, u32[]{:S(2)}) %collective-permute-start.11) | collective-permute-done | bytes 196640 | tf_op jit(solution)/shard_map/ppermute | solution.py:32
  34.7 0.9 %collective-permute-done.8.refs_2_ = bf16[4,32,768]{2,1,0:T(8,128)(2,1)S(1)} collective-permute-done((bf16[4,32,768]{2,1,0:T(8,128)(2,1)S(1)}, bf16[4,32,768]{2,1,0:T(8,128)(2,1)S(1)}, u32[]{:S(2)}, u32[]{:S(2)}) %collective-permute-start.8) | collective-permute-done | bytes 196640 | tf_op jit(solution)/shard_map/ppermute | solution.py:32
  35.6 0.1 most.1
  35.7 0.1 collective-permute-start.17
  35.8 0.5 %collective-permute-start.14 = (bf16[2,4,32,768]{3,2,1,0:T(8,128)(2,1)S(1)}, bf16[2,4,32,768]{3,2,1,0:T(8,128)(2,1)S(1)}, u32[]{:S(2)}, u32[]{:S(2)}) collective-permute-start(bf16[2,4,32,768]{3,2,1,0:T(8,128)(2,1)S(1)} %get-tuple-element.31.refs_0_), channel_id=1, source_target_pairs={{0,1},{1,0},{2,3},{3,2},{4,5},{5,4},{6,7},{7,6},{8,9},{9,8},{10,11... | collective-permute-start | bytes 1179656 | tf_op jit(solution)/shard_map/ppermute | solution.py:32
  36.3 1.4 %collective-permute-done.12.refs_1_ = bf16[4,32,768]{2,1,0:T(8,128)(2,1)S(1)} collective-permute-done((bf16[4,32,768]{2,1,0:T(8,128)(2,1)S(1)}, bf16[4,32,768]{2,1,0:T(8,128)(2,1)S(1)}, u32[]{:S(2)}, u32[]{:S(2)}) %collective-permute-start.12) | collective-permute-done | bytes 196640 | tf_op jit(solution)/shard_map/ppermute | solution.py:32
  37.7 0.0 collective-permute-done.13.refs_2_
  37.7 0.5 %collective-permute-start.16 = (bf16[4,32,768]{2,1,0:T(8,128)(2,1)S(1)}, bf16[4,32,768]{2,1,0:T(8,128)(2,1)S(1)}, u32[]{:S(2)}, u32[]{:S(2)}) collective-permute-start(bf16[4,32,768]{2,1,0:T(8,128)(2,1)S(1)} %collective-permute-done.13.refs_2_), channel_id=1, source_target_pairs={{0,1},{1,0},{2,3},{3,2},{4,5},{5,4},{6,7},{7,6},{8,9},{9,8},{10,11... | collective-permute-start | bytes 589832 | tf_op jit(solution)/shard_map/ppermute | solution.py:32
  38.2 0.0 collective-permute-done.21.refs_4_
  38.3 0.0 collective-permute-done.17.refs_1_
  38.3 0.6 %project_near.1.refs_6_ = f32[128,128]{1,0:T(8,128)S(1)} custom-call(bf16[128,12288]{1,0:T(8,128)(2,1)S(1)} %copy-done, bf16[4,4,32,768]{3,2,1,0:T(8,128)(2,1)S(1)} %get-tuple-element.32.refs_0_, bf16[4,4,32,768]{3,2,1,0:T(8,128)(2,1)S(1)} %collective-permute-done.17.refs_1_), custom_call_target="tpu_custom_call" | custom-call | flops 201326592 | bytes 3145728 | tf_op jit(solution)/shard_map/project_near/pallas_call | solution.py:225
  38.9 0.0 collective-permute-done.14.refs_3_
  38.9 0.3 collective-permute-done.15.refs_4_
  39.2 0.3 collective-permute-done.16.refs_5_
  39.4 1.4 %project_far.1 = (bf16[128,128]{1,0:T(8,128)(2,1)}, f32[32,1536]{1,0:T(8,128)}) custom-call(bf16[128,12288]{1,0:T(8,128)(2,1)S(1)} %copy-done, bf16[2,4,32,768]{3,2,1,0:T(8,128)(2,1)S(1)} %get-tuple-element.31.refs_0_, bf16[4,32,768]{2,1,0:T(8,128)(2,1)S(1)} %collective-permute-done.12.refs_1_, bf16[4,32,768]{2,1,0:T(8,128)(2,1)S(1)} %collective-permute-done.13.refs_2_, ...), custom_call_target="tpu_custom_call" | custom-call | flops 201326592 | bytes 3145728 | tf_op jit(solution)/shard_map/project_far/pallas_call | solution.py:234
  (10 shorter events, 0.2 us)
Async XLA Ops:
  4.0 4.6 %collective-permute-start.1 = (bf16[4,4,32,768]{3,2,1,0:T(8,128)(2,1)S(1)}, bf16[4,4,32,768]{3,2,1,0:T(8,128)(2,1)S(1)}, u32[]{:S(2)}, u32[]{:S(2)}) collective-permute-start(bf16[4,4,32,768]{3,2,1,0:T(8,128)(2,1)S(1)} %get-tuple-element.21), channel_id=1, source_target_pairs={{0,1},{1,0},{2,3},{3,2},{4,5},{5,4},{6,7},{7,6},{8,9},{9,8},{10,11... | collective-permute-start | bytes 2359304 | tf_op jit(solution)/shard_map/ppermute | solution.py:32
  4.5 10.8 %collective-permute-start.3 = (bf16[4,4,32,768]{3,2,1,0:T(8,128)(2,1)S(1)}, bf16[4,4,32,768]{3,2,1,0:T(8,128)(2,1)S(1)}, u32[]{:S(2)}, u32[]{:S(2)}) collective-permute-start(bf16[4,4,32,768]{3,2,1,0:T(8,128)(2,1)S(1)} %get-tuple-element.24), channel_id=1, source_target_pairs={{0,1},{1,0},{2,3},{3,2},{4,5},{5,4},{6,7},{7,6},{8,9},{9,8},{10,11... | collective-permute-start | bytes 2359304 | tf_op jit(solution)/shard_map/ppermute | solution.py:32
  4.6 9.2 %collective-permute-start = (bf16[2,32,768]{2,1,0:T(8,128)(2,1)S(1)}, bf16[2,32,768]{2,1,0:T(8,128)(2,1)S(1)}, u32[]{:S(2)}, u32[]{:S(2)}) collective-permute-start(bf16[2,32,768]{2,1,0:T(8,128)(2,1)S(1)} %get-tuple-element.19.refs_0_), channel_id=1, source_target_pairs={{0,16},{4,20},{8,24},{12,28},{16,0},{20,4},{24,8},{28,12},{1,17},{... | collective-permute-start | bytes 294920 | tf_op jit(solution)/shard_map/ppermute | solution.py:32
  8.8 7.9 %collective-permute-start.6 = (bf16[1,4,32,768]{3,2,1,0:T(8,128)(2,1)S(1)}, bf16[1,4,32,768]{3,2,1,0:T(8,128)(2,1)S(1)}, u32[]{:S(2)}, u32[]{:S(2)}) collective-permute-start(bf16[1,4,32,768]{3,2,1,0:T(8,128)(2,1)S(1)} %get-tuple-element.22.refs_2_), channel_id=1, source_target_pairs={{0,4},{4,0},{8,12},{12,8},{16,20},{20,16},{24,28},{28,24},{1,5},{5... | collective-permute-start | bytes 589832 | tf_op jit(solution)/shard_map/ppermute | solution.py:32
  10.3 7.0 %collective-permute-start.7 = (bf16[4,32,768]{2,1,0:T(8,128)(2,1)S(1)}, bf16[4,32,768]{2,1,0:T(8,128)(2,1)S(1)}, u32[]{:S(2)}, u32[]{:S(2)}) collective-permute-start(bf16[4,32,768]{2,1,0:T(8,128)(2,1)S(1)} %get-tuple-element.27), channel_id=1, source_target_pairs={{0,2},{1,3},{2,0},{3,1},{4,6},{5,7},{6,4},{7,5},{8,10},{9,11},{10,... | collective-permute-start | bytes 589832 | tf_op jit(solution)/shard_map/ppermute | solution.py:32
  11.8 9.0 %collective-permute-start.4 = (bf16[4,32,768]{2,1,0:T(8,128)(2,1)S(1)}, bf16[4,32,768]{2,1,0:T(8,128)(2,1)S(1)}, u32[]{:S(2)}, u32[]{:S(2)}) collective-permute-start(bf16[4,32,768]{2,1,0:T(8,128)(2,1)S(1)} %get-tuple-element.25), channel_id=1, source_target_pairs={{0,4},{4,0},{8,12},{12,8},{16,20},{20,16},{24,28},{28,24},{1,5},{5... | collective-permute-start | bytes 589832 | tf_op jit(solution)/shard_map/ppermute | solution.py:32
  13.7 7.8 %collective-permute-start.5 = (bf16[4,32,768]{2,1,0:T(8,128)(2,1)S(1)}, bf16[4,32,768]{2,1,0:T(8,128)(2,1)S(1)}, u32[]{:S(2)}, u32[]{:S(2)}) collective-permute-start(bf16[4,32,768]{2,1,0:T(8,128)(2,1)S(1)} %get-tuple-element.26), channel_id=1, source_target_pairs={{0,2},{1,3},{2,0},{3,1},{4,6},{5,7},{6,4},{7,5},{8,10},{9,11},{10,... | collective-permute-start | bytes 589832 | tf_op jit(solution)/shard_map/ppermute | solution.py:32
  15.3 6.4 %collective-permute-start.2 = (bf16[2,2,32,768]{3,2,1,0:T(8,128)(2,1)S(1)}, bf16[2,2,32,768]{3,2,1,0:T(8,128)(2,1)S(1)}, u32[]{:S(2)}, u32[]{:S(2)}) collective-permute-start(bf16[2,2,32,768]{3,2,1,0:T(8,128)(2,1)S(1)} %widen.1.refs_4_), channel_id=1, source_target_pairs={{0,8},{4,12},{8,0},{12,4},{16,24},{20,28},{24,16},{28,20},{1,9},{5... | collective-permute-start | bytes 589832 | tf_op jit(solution)/shard_map/ppermute | solution.py:32
  17.5 7.3 %collective-permute-start.18 = (bf16[4,32,768]{2,1,0:T(8,128)(2,1)S(1)}, bf16[4,32,768]{2,1,0:T(8,128)(2,1)S(1)}, u32[]{:S(2)}, u32[]{:S(2)}) collective-permute-start(bf16[4,32,768]{2,1,0:T(8,128)(2,1)S(1)} %get-tuple-element.28.refs_4_), channel_id=1, source_target_pairs={{0,4},{4,0},{8,12},{12,8},{16,20},{20,16},{24,28},{28,24},{1,5},{5... | collective-permute-start | bytes 589832 | tf_op jit(solution)/shard_map/ppermute | solution.py:32
  18.3 7.8 %collective-permute-start.19 = (bf16[4,32,768]{2,1,0:T(8,128)(2,1)S(1)}, bf16[4,32,768]{2,1,0:T(8,128)(2,1)S(1)}, u32[]{:S(2)}, u32[]{:S(2)}) collective-permute-start(bf16[4,32,768]{2,1,0:T(8,128)(2,1)S(1)} %get-tuple-element.33), channel_id=1, source_target_pairs={{0,2},{1,3},{2,0},{3,1},{4,6},{5,7},{6,4},{7,5},{8,10},{9,11},{10,... | collective-permute-start | bytes 589832 | tf_op jit(solution)/shard_map/ppermute | solution.py:32
  21.7 16.5 %copy-start = (bf16[128,12288]{1,0:T(8,128)(2,1)S(1)}, bf16[128,12288]{1,0:T(8,128)(2,1)}, u32[]{:S(2)}) copy-start(bf16[128,12288]{1,0:T(8,128)(2,1)} %tokens.5) | copy-start | bytes 9437188
  21.8 8.3 %collective-permute-start.10 = (bf16[4,32,768]{2,1,0:T(8,128)(2,1)S(1)}, bf16[4,32,768]{2,1,0:T(8,128)(2,1)S(1)}, u32[]{:S(2)}, u32[]{:S(2)}) collective-permute-start(bf16[4,32,768]{2,1,0:T(8,128)(2,1)S(1)} %get-tuple-element.29.refs_0_.refs_3_), channel_id=1, source_target_pairs={{0,4},{4,0},{8,12},{12,8},{16,20},{20,16},{24,28},{28,24},{1,5},{5... | collective-permute-start | bytes 589832 | tf_op jit(solution)/shard_map/ppermute | solution.py:32
  22.9 7.6 %collective-permute-start.9 = (bf16[4,32,768]{2,1,0:T(8,128)(2,1)S(1)}, bf16[4,32,768]{2,1,0:T(8,128)(2,1)S(1)}, u32[]{:S(2)}, u32[]{:S(2)}) collective-permute-start(bf16[4,32,768]{2,1,0:T(8,128)(2,1)S(1)} %get-tuple-element.30.refs_1_), channel_id=1, source_target_pairs={{0,2},{1,3},{2,0},{3,1},{4,6},{5,7},{6,4},{7,5},{8,10},{9,11},{10,... | collective-permute-start | bytes 589832 | tf_op jit(solution)/shard_map/ppermute | solution.py:32
  26.2 6.0 %collective-permute-start.20 = (bf16[2,2,32,768]{3,2,1,0:T(8,128)(2,1)S(1)}, bf16[2,2,32,768]{3,2,1,0:T(8,128)(2,1)S(1)}, u32[]{:S(2)}, u32[]{:S(2)}) collective-permute-start(bf16[2,2,32,768]{3,2,1,0:T(8,128)(2,1)S(1)} %plane.2.refs_4_), channel_id=1, source_target_pairs={{0,8},{4,12},{8,0},{12,4},{16,24},{20,28},{24,16},{28,20},{1,9},{5... | collective-permute-start | bytes 589832 | tf_op jit(solution)/shard_map/ppermute | solution.py:32
  27.8 6.9 %collective-permute-start.11 = (bf16[4,32,768]{2,1,0:T(8,128)(2,1)S(1)}, bf16[4,32,768]{2,1,0:T(8,128)(2,1)S(1)}, u32[]{:S(2)}, u32[]{:S(2)}) collective-permute-start(bf16[4,32,768]{2,1,0:T(8,128)(2,1)S(1)} %get-tuple-element.30.refs_1_), channel_id=1, source_target_pairs={{0,4},{4,0},{8,12},{12,8},{16,20},{20,16},{24,28},{28,24},{1,5},{5... | collective-permute-start | bytes 589832 | tf_op jit(solution)/shard_map/ppermute | solution.py:32
  28.5 7.1 %collective-permute-start.8 = (bf16[4,32,768]{2,1,0:T(8,128)(2,1)S(1)}, bf16[4,32,768]{2,1,0:T(8,128)(2,1)S(1)}, u32[]{:S(2)}, u32[]{:S(2)}) collective-permute-start(bf16[4,32,768]{2,1,0:T(8,128)(2,1)S(1)} %get-tuple-element.29.refs_0_.refs_3_), channel_id=1, source_target_pairs={{0,2},{1,3},{2,0},{3,1},{4,6},{5,7},{6,4},{7,5},{8,10},{9,11},{10,... | collective-permute-start | bytes 589832 | tf_op jit(solution)/shard_map/ppermute | solution.py:32
  30.0 7.7 %collective-permute-start.12 = (bf16[4,32,768]{2,1,0:T(8,128)(2,1)S(1)}, bf16[4,32,768]{2,1,0:T(8,128)(2,1)S(1)}, u32[]{:S(2)}, u32[]{:S(2)}) collective-permute-start(bf16[4,32,768]{2,1,0:T(8,128)(2,1)S(1)} %collective-permute-done.10.refs_4_), channel_id=1, source_target_pairs={{0,2},{1,3},{2,0},{3,1},{4,6},{5,7},{6,4},{7,5},{8,10},{9,11},{10,... | collective-permute-start | bytes 589832 | tf_op jit(solution)/shard_map/ppermute | solution.py:32
  30.5 7.2 %collective-permute-start.13 = (bf16[4,32,768]{2,1,0:T(8,128)(2,1)S(1)}, bf16[4,32,768]{2,1,0:T(8,128)(2,1)S(1)}, u32[]{:S(2)}, u32[]{:S(2)}) collective-permute-start(bf16[4,32,768]{2,1,0:T(8,128)(2,1)S(1)} %collective-permute-done.9.refs_3_), channel_id=1, source_target_pairs={{0,4},{4,0},{8,12},{12,8},{16,20},{20,16},{24,28},{28,24},{1,5},{5... | collective-permute-start | bytes 589832 | tf_op jit(solution)/shard_map/ppermute | solution.py:32
  32.3 6.0 %collective-permute-start.21 = (bf16[1,2,32,768]{3,2,1,0:T(8,128)(2,1)S(1)}, bf16[1,2,32,768]{3,2,1,0:T(8,128)(2,1)S(1)}, u32[]{:S(2)}, u32[]{:S(2)}) collective-permute-start(bf16[1,2,32,768]{3,2,1,0:T(8,128)(2,1)S(1)} %plane.3), channel_id=1, source_target_pairs={{0,16},{4,20},{8,24},{12,28},{16,0},{20,4},{24,8},{28,12},{1,17},{... | collective-permute-start | bytes 294920 | tf_op jit(solution)/shard_map/ppermute | solution.py:32
  35.7 2.6 %collective-permute-start.17 = (bf16[4,4,32,768]{3,2,1,0:T(8,128)(2,1)S(1)}, bf16[4,4,32,768]{3,2,1,0:T(8,128)(2,1)S(1)}, u32[]{:S(2)}, u32[]{:S(2)}) collective-permute-start(bf16[4,4,32,768]{3,2,1,0:T(8,128)(2,1)S(1)} %get-tuple-element.32.refs_0_), channel_id=1, source_target_pairs={{0,1},{1,0},{2,3},{3,2},{4,5},{5,4},{6,7},{7,6},{8,9},{9,8},{10,11... | collective-permute-start | bytes 2359304 | tf_op jit(solution)/shard_map/ppermute | solution.py:32
  35.8 3.1 %collective-permute-start.14 = (bf16[2,4,32,768]{3,2,1,0:T(8,128)(2,1)S(1)}, bf16[2,4,32,768]{3,2,1,0:T(8,128)(2,1)S(1)}, u32[]{:S(2)}, u32[]{:S(2)}) collective-permute-start(bf16[2,4,32,768]{3,2,1,0:T(8,128)(2,1)S(1)} %get-tuple-element.31.refs_0_), channel_id=1, source_target_pairs={{0,1},{1,0},{2,3},{3,2},{4,5},{5,4},{6,7},{7,6},{8,9},{9,8},{10,11... | collective-permute-start | bytes 1179656 | tf_op jit(solution)/shard_map/ppermute | solution.py:32
  37.7 1.4 %collective-permute-start.15 = (bf16[4,32,768]{2,1,0:T(8,128)(2,1)S(1)}, bf16[4,32,768]{2,1,0:T(8,128)(2,1)S(1)}, u32[]{:S(2)}, u32[]{:S(2)}) collective-permute-start(bf16[4,32,768]{2,1,0:T(8,128)(2,1)S(1)} %collective-permute-done.12.refs_1_), channel_id=1, source_target_pairs={{0,1},{1,0},{2,3},{3,2},{4,5},{5,4},{6,7},{7,6},{8,9},{9,8},{10,11... | collective-permute-start | bytes 589832 | tf_op jit(solution)/shard_map/ppermute | solution.py:32
  37.7 1.7 %collective-permute-start.16 = (bf16[4,32,768]{2,1,0:T(8,128)(2,1)S(1)}, bf16[4,32,768]{2,1,0:T(8,128)(2,1)S(1)}, u32[]{:S(2)}, u32[]{:S(2)}) collective-permute-start(bf16[4,32,768]{2,1,0:T(8,128)(2,1)S(1)} %collective-permute-done.13.refs_2_), channel_id=1, source_target_pairs={{0,1},{1,0},{2,3},{3,2},{4,5},{5,4},{6,7},{7,6},{8,9},{9,8},{10,11... | collective-permute-start | bytes 589832 | tf_op jit(solution)/shard_map/ppermute | solution.py:32

commit v7 on v6

--- a/solution.py
+++ b/solution.py
@@ -360,10 +360,9 @@
         step *= 2
     weight_grad = finish([sums[0, 0], sums[0, 1]], arrays, tokens)
 
-    held = own + [e for es in on_y for e in es] + on_x
-    groups = [range(2 * ys), range(2 * ys, 2 * ys + 2)]
-    outs = [((len(g), *one), [((i - g[0],), [(i, whole)]) for i in g]) for g in groups]
-    near, side = add_up(outs, held, name="most")
+    held = own + [e for es in on_y for e in es]
+    (near,) = add_up([((2 * ys, *one), [((i,), [(i, whole)]) for i in range(2 * ys)])], held, name="near")
+    (side,) = add_up([((2, *one), [((h,), [(h, whole)]) for h in range(2)])], on_x, [near], name="side")
     ends = [d for ds in diag for d in ds]
     near = [near, core_flip(near)]
     far = [side, *ends, core_flip(side), *[core_flip(e) for e in ends]]

time: 41 us -> 41 us (level)
  transfers between devices with their start and end apart: 22 -> 22, of which waited for: 11 -> 10; matrix products, arithmetic and copies ran while one was open for 0% -> 0% of each run, Pallas kernels for 3% -> 3%
where the time goes in v7:
time: 41 us; the launch traced here: 40.9 us
  starting transfers between devices  24.4 us (60%)
  waiting for transfers between devices  9.72 us (24%)
  Pallas kernels  6.04 us (15%)
  between operations  0.76 us (2%)
    ppermute x22, starting transfers between devices, flip(): return lax.ppermute(entries, axis, [(i, i ^ offset) for i in range(size)])  24.4 us
    ppermute x22, waiting for transfers between devices, flip(): return lax.ppermute(entries, axis, [(i, i ^ offset) for i in range(size)])  9.72 us
    pallas_call x1, Pallas kernels, local_products(): pl.pallas_call(functools.partial(first_kernel, ys, zs), out_shape=(*block...  3.33 us
    pallas_call x1, Pallas kernels, project(): pl.pallas_call(functools.partial(project_kernel, ys, zs, 1), out_shape=(j...  1.45 us
  transfers between devices with their start and end apart: 22, of which 10 were waited for; matrix products, arithmetic and copies ran while one was open for 0% of the time, Pallas kernels for 3%

profile of v7, /device:TPU:0, one launch (start us, length us, event | category | flops | bytes accessed | tf_op | source)
XLA Modules:
  0.0 40.9 jit_solution(10418382501642819821)
XLA Ops:
  0.6 3.3 %first.1 = (bf16[4,4,32,768]{3,2,1,0:T(8,128)(2,1)S(1)}, bf16[4,4,32,768]{3,2,1,0:T(8,128)(2,1)S(1)}, bf16[4,4,32,768]{3,2,1,0:T(8,128)(2,1)S(1)}, bf16[4,4,32,7...) custom-call(bf16[128,12288]{1,0:T(8,128)(2,1)} %tokens.5, bf16[128,128]{1,0:T(8,128)(2,1)} %cot.1, bf16[32,1536]{1,0:T(8,128)(2,1)} %bitcast.3, ...), custom_call_target="tpu_custom_call" | custom-call | flops 402653184 | bytes 6291456 | tf_op jit(solution)/shard_map/first/pallas_call | solution.py:92
  4.0 0.5 %collective-permute-start.1 = (bf16[4,4,32,768]{3,2,1,0:T(8,128)(2,1)S(1)}, bf16[4,4,32,768]{3,2,1,0:T(8,128)(2,1)S(1)}, u32[]{:S(2)}, u32[]{:S(2)}) collective-permute-start(bf16[4,4,32,768]{3,2,1,0:T(8,128)(2,1)S(1)} %get-tuple-element.19), channel_id=1, source_target_pairs={{0,1},{1,0},{2,3},{3,2},{4,5},{5,4},{6,7},{7,6},{8,9},{9,8},{10,11... | collective-permute-start | bytes 2359304 | tf_op jit(solution)/shard_map/ppermute | solution.py:32
  4.5 0.1 collective-permute-start.3
  4.6 4.0 %collective-permute-start = (bf16[2,32,768]{2,1,0:T(8,128)(2,1)S(1)}, bf16[2,32,768]{2,1,0:T(8,128)(2,1)S(1)}, u32[]{:S(2)}, u32[]{:S(2)}) collective-permute-start(bf16[2,32,768]{2,1,0:T(8,128)(2,1)S(1)} %get-tuple-element.17.refs_0_), channel_id=1, source_target_pairs={{0,16},{4,20},{8,24},{12,28},{16,0},{20,4},{24,8},{28,12},{1,17},{... | collective-permute-start | bytes 294920 | tf_op jit(solution)/shard_map/ppermute | solution.py:32
  8.6 0.0 collective-permute-done.1.refs_1_
  8.6 0.2 stage1.1
  8.8 1.6 %collective-permute-start.6 = (bf16[1,4,32,768]{3,2,1,0:T(8,128)(2,1)S(1)}, bf16[1,4,32,768]{3,2,1,0:T(8,128)(2,1)S(1)}, u32[]{:S(2)}, u32[]{:S(2)}) collective-permute-start(bf16[1,4,32,768]{3,2,1,0:T(8,128)(2,1)S(1)} %get-tuple-element.20.refs_2_), channel_id=1, source_target_pairs={{0,4},{4,0},{8,12},{12,8},{16,20},{20,16},{24,28},{28,24},{1,5},{5... | collective-permute-start | bytes 589832 | tf_op jit(solution)/shard_map/ppermute | solution.py:32
  10.3 1.5 %collective-permute-start.7 = (bf16[4,32,768]{2,1,0:T(8,128)(2,1)S(1)}, bf16[4,32,768]{2,1,0:T(8,128)(2,1)S(1)}, u32[]{:S(2)}, u32[]{:S(2)}) collective-permute-start(bf16[4,32,768]{2,1,0:T(8,128)(2,1)S(1)} %get-tuple-element.25), channel_id=1, source_target_pairs={{0,2},{1,3},{2,0},{3,1},{4,6},{5,7},{6,4},{7,5},{8,10},{9,11},{10,... | collective-permute-start | bytes 589832 | tf_op jit(solution)/shard_map/ppermute | solution.py:32
  11.8 0.5 %collective-permute-start.4 = (bf16[4,32,768]{2,1,0:T(8,128)(2,1)S(1)}, bf16[4,32,768]{2,1,0:T(8,128)(2,1)S(1)}, u32[]{:S(2)}, u32[]{:S(2)}) collective-permute-start(bf16[4,32,768]{2,1,0:T(8,128)(2,1)S(1)} %get-tuple-element.23), channel_id=1, source_target_pairs={{0,4},{4,0},{8,12},{12,8},{16,20},{20,16},{24,28},{28,24},{1,5},{5... | collective-permute-start | bytes 589832 | tf_op jit(solution)/shard_map/ppermute | solution.py:32
  12.4 1.3 %collective-permute-done.refs_1_ = bf16[2,32,768]{2,1,0:T(8,128)(2,1)S(1)} collective-permute-done((bf16[2,32,768]{2,1,0:T(8,128)(2,1)S(1)}, bf16[2,32,768]{2,1,0:T(8,128)(2,1)S(1)}, u32[]{:S(2)}, u32[]{:S(2)}) %collective-permute-start) | collective-permute-done | bytes 98336 | tf_op jit(solution)/shard_map/ppermute | solution.py:32
  13.7 1.6 %collective-permute-start.5 = (bf16[4,32,768]{2,1,0:T(8,128)(2,1)S(1)}, bf16[4,32,768]{2,1,0:T(8,128)(2,1)S(1)}, u32[]{:S(2)}, u32[]{:S(2)}) collective-permute-start(bf16[4,32,768]{2,1,0:T(8,128)(2,1)S(1)} %get-tuple-element.24), channel_id=1, source_target_pairs={{0,2},{1,3},{2,0},{3,1},{4,6},{5,7},{6,4},{7,5},{8,10},{9,11},{10,... | collective-permute-start | bytes 589832 | tf_op jit(solution)/shard_map/ppermute | solution.py:32
  15.3 0.0 collective-permute-done.3.refs_1_
  15.3 0.7 %collective-permute-start.2 = (bf16[2,2,32,768]{3,2,1,0:T(8,128)(2,1)S(1)}, bf16[2,2,32,768]{3,2,1,0:T(8,128)(2,1)S(1)}, u32[]{:S(2)}, u32[]{:S(2)}) collective-permute-start(bf16[2,2,32,768]{3,2,1,0:T(8,128)(2,1)S(1)} %widen.1.refs_4_), channel_id=1, source_target_pairs={{0,8},{4,12},{8,0},{12,4},{16,24},{20,28},{24,16},{28,20},{1,9},{5... | collective-permute-start | bytes 589832 | tf_op jit(solution)/shard_map/ppermute | solution.py:32
  16.1 0.6 %collective-permute-done.6.refs_2_ = bf16[1,4,32,768]{3,2,1,0:T(8,128)(2,1)S(1)} collective-permute-done((bf16[1,4,32,768]{3,2,1,0:T(8,128)(2,1)S(1)}, bf16[1,4,32,768]{3,2,1,0:T(8,128)(2,1)S(1)}, u32[]{:S(2)}, u32[]{:S(2)}) %collective-permute-start.6) | collective-permute-done | bytes 196640 | tf_op jit(solution)/shard_map/ppermute | solution.py:32
  16.6 0.7 %collective-permute-done.7.refs_3_ = bf16[4,32,768]{2,1,0:T(8,128)(2,1)S(1)} collective-permute-done((bf16[4,32,768]{2,1,0:T(8,128)(2,1)S(1)}, bf16[4,32,768]{2,1,0:T(8,128)(2,1)S(1)}, u32[]{:S(2)}, u32[]{:S(2)}) %collective-permute-start.7) | collective-permute-done | bytes 196640 | tf_op jit(solution)/shard_map/ppermute | solution.py:32
  17.4 0.1 stage2.1
  17.5 0.8 %collective-permute-start.18 = (bf16[4,32,768]{2,1,0:T(8,128)(2,1)S(1)}, bf16[4,32,768]{2,1,0:T(8,128)(2,1)S(1)}, u32[]{:S(2)}, u32[]{:S(2)}) collective-permute-start(bf16[4,32,768]{2,1,0:T(8,128)(2,1)S(1)} %get-tuple-element.26.refs_4_), channel_id=1, source_target_pairs={{0,4},{4,0},{8,12},{12,8},{16,20},{20,16},{24,28},{28,24},{1,5},{5... | collective-permute-start | bytes 589832 | tf_op jit(solution)/shard_map/ppermute | solution.py:32
  18.3 1.5 %collective-permute-start.19 = (bf16[4,32,768]{2,1,0:T(8,128)(2,1)S(1)}, bf16[4,32,768]{2,1,0:T(8,128)(2,1)S(1)}, u32[]{:S(2)}, u32[]{:S(2)}) collective-permute-start(bf16[4,32,768]{2,1,0:T(8,128)(2,1)S(1)} %get-tuple-element.29), channel_id=1, source_target_pairs={{0,2},{1,3},{2,0},{3,1},{4,6},{5,7},{6,4},{7,5},{8,10},{9,11},{10,... | collective-permute-start | bytes 589832 | tf_op jit(solution)/shard_map/ppermute | solution.py:32
  19.9 1.0 %collective-permute-done.4.refs_2_ = bf16[4,32,768]{2,1,0:T(8,128)(2,1)S(1)} collective-permute-done((bf16[4,32,768]{2,1,0:T(8,128)(2,1)S(1)}, bf16[4,32,768]{2,1,0:T(8,128)(2,1)S(1)}, u32[]{:S(2)}, u32[]{:S(2)}) %collective-permute-start.4) | collective-permute-done | bytes 196640 | tf_op jit(solution)/shard_map/ppermute | solution.py:32
  20.8 0.7 %collective-permute-done.5.refs_3_ = bf16[4,32,768]{2,1,0:T(8,128)(2,1)S(1)} collective-permute-done((bf16[4,32,768]{2,1,0:T(8,128)(2,1)S(1)}, bf16[4,32,768]{2,1,0:T(8,128)(2,1)S(1)}, u32[]{:S(2)}, u32[]{:S(2)}) %collective-permute-start.5) | collective-permute-done | bytes 196640 | tf_op jit(solution)/shard_map/ppermute | solution.py:32
  21.6 0.1 sides.1.refs_3_.refs_0_
  21.7 0.0 collective-permute-done.2.refs_2_
  21.8 1.2 %collective-permute-start.8 = (bf16[4,32,768]{2,1,0:T(8,128)(2,1)S(1)}, bf16[4,32,768]{2,1,0:T(8,128)(2,1)S(1)}, u32[]{:S(2)}, u32[]{:S(2)}) collective-permute-start(bf16[4,32,768]{2,1,0:T(8,128)(2,1)S(1)} %get-tuple-element.27.refs_0_.refs_3_), channel_id=1, source_target_pairs={{0,4},{4,0},{8,12},{12,8},{16,20},{20,16},{24,28},{28,24},{1,5},{5... | collective-permute-start | bytes 589832 | tf_op jit(solution)/shard_map/ppermute | solution.py:32
  22.9 1.8 %collective-permute-start.11 = (bf16[4,32,768]{2,1,0:T(8,128)(2,1)S(1)}, bf16[4,32,768]{2,1,0:T(8,128)(2,1)S(1)}, u32[]{:S(2)}, u32[]{:S(2)}) collective-permute-start(bf16[4,32,768]{2,1,0:T(8,128)(2,1)S(1)} %get-tuple-element.28.refs_1_), channel_id=1, source_target_pairs={{0,2},{1,3},{2,0},{3,1},{4,6},{5,7},{6,4},{7,5},{8,10},{9,11},{10,... | collective-permute-start | bytes 589832 | tf_op jit(solution)/shard_map/ppermute | solution.py:32
  24.8 1.4 %collective-permute-done.19.refs_2_ = bf16[4,32,768]{2,1,0:T(8,128)(2,1)S(1)} collective-permute-done((bf16[4,32,768]{2,1,0:T(8,128)(2,1)S(1)}, bf16[4,32,768]{2,1,0:T(8,128)(2,1)S(1)}, u32[]{:S(2)}, u32[]{:S(2)}) %collective-permute-start.19) | collective-permute-done | bytes 196640 | tf_op jit(solution)/shard_map/ppermute | solution.py:32
  26.2 1.6 %collective-permute-start.20 = (bf16[2,2,32,768]{3,2,1,0:T(8,128)(2,1)S(1)}, bf16[2,2,32,768]{3,2,1,0:T(8,128)(2,1)S(1)}, u32[]{:S(2)}, u32[]{:S(2)}) collective-permute-start(bf16[2,2,32,768]{3,2,1,0:T(8,128)(2,1)S(1)} %plane.2.refs_4_), channel_id=1, source_target_pairs={{0,8},{4,12},{8,0},{12,4},{16,24},{20,28},{24,16},{28,20},{1,9},{5... | collective-permute-start | bytes 589832 | tf_op jit(solution)/shard_map/ppermute | solution.py:32
  27.8 1.5 %collective-permute-start.10 = (bf16[4,32,768]{2,1,0:T(8,128)(2,1)S(1)}, bf16[4,32,768]{2,1,0:T(8,128)(2,1)S(1)}, u32[]{:S(2)}, u32[]{:S(2)}) collective-permute-start(bf16[4,32,768]{2,1,0:T(8,128)(2,1)S(1)} %get-tuple-element.27.refs_0_.refs_3_), channel_id=1, source_target_pairs={{0,2},{1,3},{2,0},{3,1},{4,6},{5,7},{6,4},{7,5},{8,10},{9,11},{10,... | collective-permute-start | bytes 589832 | tf_op jit(solution)/shard_map/ppermute | solution.py:32
  29.4 0.7 %collective-permute-start.9 = (bf16[4,32,768]{2,1,0:T(8,128)(2,1)S(1)}, bf16[4,32,768]{2,1,0:T(8,128)(2,1)S(1)}, u32[]{:S(2)}, u32[]{:S(2)}) collective-permute-start(bf16[4,32,768]{2,1,0:T(8,128)(2,1)S(1)} %get-tuple-element.28.refs_1_), channel_id=1, source_target_pairs={{0,4},{4,0},{8,12},{12,8},{16,20},{20,16},{24,28},{28,24},{1,5},{5... | collective-permute-start | bytes 589832 | tf_op jit(solution)/shard_map/ppermute | solution.py:32
  30.0 0.0 collective-permute-done.8.refs_0_
  30.0 0.5 %collective-permute-start.12 = (bf16[4,32,768]{2,1,0:T(8,128)(2,1)S(1)}, bf16[4,32,768]{2,1,0:T(8,128)(2,1)S(1)}, u32[]{:S(2)}, u32[]{:S(2)}) collective-permute-start(bf16[4,32,768]{2,1,0:T(8,128)(2,1)S(1)} %collective-permute-done.8.refs_0_), channel_id=1, source_target_pairs={{0,2},{1,3},{2,0},{3,1},{4,6},{5,7},{6,4},{7,5},{8,10},{9,11},{10,... | collective-permute-start | bytes 589832 | tf_op jit(solution)/shard_map/ppermute | solution.py:32
  30.5 0.0 collective-permute-done.11.refs_3_
  30.5 1.4 %collective-permute-start.13 = (bf16[4,32,768]{2,1,0:T(8,128)(2,1)S(1)}, bf16[4,32,768]{2,1,0:T(8,128)(2,1)S(1)}, u32[]{:S(2)}, u32[]{:S(2)}) collective-permute-start(bf16[4,32,768]{2,1,0:T(8,128)(2,1)S(1)} %collective-permute-done.11.refs_3_), channel_id=1, source_target_pairs={{0,4},{4,0},{8,12},{12,8},{16,20},{20,16},{24,28},{28,24},{1,5},{5... | collective-permute-start | bytes 589832 | tf_op jit(solution)/shard_map/ppermute | solution.py:32
  32.0 1.6 %collective-permute-start.21 = (bf16[1,2,32,768]{3,2,1,0:T(8,128)(2,1)S(1)}, bf16[1,2,32,768]{3,2,1,0:T(8,128)(2,1)S(1)}, u32[]{:S(2)}, u32[]{:S(2)}) collective-permute-start(bf16[1,2,32,768]{3,2,1,0:T(8,128)(2,1)S(1)} %plane.3), channel_id=1, source_target_pairs={{0,16},{4,20},{8,24},{12,28},{16,0},{20,4},{24,8},{28,12},{1,17},{... | collective-permute-start | bytes 294920 | tf_op jit(solution)/shard_map/ppermute | solution.py:32
  33.6 2.0 %collective-permute-done.10.refs_2_ = bf16[4,32,768]{2,1,0:T(8,128)(2,1)S(1)} collective-permute-done((bf16[4,32,768]{2,1,0:T(8,128)(2,1)S(1)}, bf16[4,32,768]{2,1,0:T(8,128)(2,1)S(1)}, u32[]{:S(2)}, u32[]{:S(2)}) %collective-permute-start.10) | collective-permute-done | bytes 196640 | tf_op jit(solution)/shard_map/ppermute | solution.py:32
  35.6 0.1 near.1.refs_2_.refs_0_
  35.7 0.1 collective-permute-start.17
  35.7 0.0 collective-permute-done.9.refs_1_
  35.8 0.5 %collective-permute-start.14 = (bf16[2,4,32,768]{3,2,1,0:T(8,128)(2,1)S(1)}, bf16[2,4,32,768]{3,2,1,0:T(8,128)(2,1)S(1)}, u32[]{:S(2)}, u32[]{:S(2)}) collective-permute-start(bf16[2,4,32,768]{3,2,1,0:T(8,128)(2,1)S(1)} %side.1.refs_0_), channel_id=1, source_target_pairs={{0,1},{1,0},{2,3},{3,2},{4,5},{5,4},{6,7},{7,6},{8,9},{9,8},{10,11... | collective-permute-start | bytes 1179656 | tf_op jit(solution)/shard_map/ppermute | solution.py:32
  36.3 1.4 %collective-permute-done.12.refs_1_ = bf16[4,32,768]{2,1,0:T(8,128)(2,1)S(1)} collective-permute-done((bf16[4,32,768]{2,1,0:T(8,128)(2,1)S(1)}, bf16[4,32,768]{2,1,0:T(8,128)(2,1)S(1)}, u32[]{:S(2)}, u32[]{:S(2)}) %collective-permute-start.12) | collective-permute-done | bytes 196640 | tf_op jit(solution)/shard_map/ppermute | solution.py:32
  37.7 0.0 collective-permute-done.13.refs_2_
  37.8 0.5 %collective-permute-start.16 = (bf16[4,32,768]{2,1,0:T(8,128)(2,1)S(1)}, bf16[4,32,768]{2,1,0:T(8,128)(2,1)S(1)}, u32[]{:S(2)}, u32[]{:S(2)}) collective-permute-start(bf16[4,32,768]{2,1,0:T(8,128)(2,1)S(1)} %collective-permute-done.13.refs_2_), channel_id=1, source_target_pairs={{0,1},{1,0},{2,3},{3,2},{4,5},{5,4},{6,7},{7,6},{8,9},{9,8},{10,11... | collective-permute-start | bytes 589832 | tf_op jit(solution)/shard_map/ppermute | solution.py:32
  38.2 0.0 collective-permute-done.21.refs_4_
  38.3 0.0 collective-permute-done.17.refs_1_
  38.3 0.6 %project_near.1.refs_6_ = f32[128,128]{1,0:T(8,128)S(1)} custom-call(bf16[128,12288]{1,0:T(8,128)(2,1)S(1)} %copy-done, bf16[4,4,32,768]{3,2,1,0:T(8,128)(2,1)S(1)} %near.1.refs_2_.refs_0_, bf16[4,4,32,768]{3,2,1,0:T(8,128)(2,1)S(1)} %collective-permute-done.17.refs_1_), custom_call_target="tpu_custom_call" | custom-call | flops 201326592 | bytes 3145728 | tf_op jit(solution)/shard_map/project_near/pallas_call | solution.py:225
  38.9 0.0 collective-permute-done.14.refs_3_
  38.9 0.3 collective-permute-done.15.refs_4_
  39.2 0.3 collective-permute-done.16.refs_5_
  39.4 1.4 %project_far.1 = (bf16[128,128]{1,0:T(8,128)(2,1)}, f32[32,1536]{1,0:T(8,128)}) custom-call(bf16[128,12288]{1,0:T(8,128)(2,1)S(1)} %copy-done, bf16[2,4,32,768]{3,2,1,0:T(8,128)(2,1)S(1)} %side.1.refs_0_, bf16[4,32,768]{2,1,0:T(8,128)(2,1)S(1)} %collective-permute-done.12.refs_1_, bf16[4,32,768]{2,1,0:T(8,128)(2,1)S(1)} %collective-permute-done.13.refs_2_, ...), custom_call_target="tpu_custom_call" | custom-call | flops 201326592 | bytes 3145728 | tf_op jit(solution)/shard_map/project_far/pallas_call | solution.py:234
  (11 shorter events, 0.2 us)
Async XLA Ops:
  4.0 4.6 %collective-permute-start.1 = (bf16[4,4,32,768]{3,2,1,0:T(8,128)(2,1)S(1)}, bf16[4,4,32,768]{3,2,1,0:T(8,128)(2,1)S(1)}, u32[]{:S(2)}, u32[]{:S(2)}) collective-permute-start(bf16[4,4,32,768]{3,2,1,0:T(8,128)(2,1)S(1)} %get-tuple-element.19), channel_id=1, source_target_pairs={{0,1},{1,0},{2,3},{3,2},{4,5},{5,4},{6,7},{7,6},{8,9},{9,8},{10,11... | collective-permute-start | bytes 2359304 | tf_op jit(solution)/shard_map/ppermute | solution.py:32
  4.5 10.8 %collective-permute-start.3 = (bf16[4,4,32,768]{3,2,1,0:T(8,128)(2,1)S(1)}, bf16[4,4,32,768]{3,2,1,0:T(8,128)(2,1)S(1)}, u32[]{:S(2)}, u32[]{:S(2)}) collective-permute-start(bf16[4,4,32,768]{3,2,1,0:T(8,128)(2,1)S(1)} %get-tuple-element.22), channel_id=1, source_target_pairs={{0,1},{1,0},{2,3},{3,2},{4,5},{5,4},{6,7},{7,6},{8,9},{9,8},{10,11... | collective-permute-start | bytes 2359304 | tf_op jit(solution)/shard_map/ppermute | solution.py:32
  4.6 9.2 %collective-permute-start = (bf16[2,32,768]{2,1,0:T(8,128)(2,1)S(1)}, bf16[2,32,768]{2,1,0:T(8,128)(2,1)S(1)}, u32[]{:S(2)}, u32[]{:S(2)}) collective-permute-start(bf16[2,32,768]{2,1,0:T(8,128)(2,1)S(1)} %get-tuple-element.17.refs_0_), channel_id=1, source_target_pairs={{0,16},{4,20},{8,24},{12,28},{16,0},{20,4},{24,8},{28,12},{1,17},{... | collective-permute-start | bytes 294920 | tf_op jit(solution)/shard_map/ppermute | solution.py:32
  8.8 7.9 %collective-permute-start.6 = (bf16[1,4,32,768]{3,2,1,0:T(8,128)(2,1)S(1)}, bf16[1,4,32,768]{3,2,1,0:T(8,128)(2,1)S(1)}, u32[]{:S(2)}, u32[]{:S(2)}) collective-permute-start(bf16[1,4,32,768]{3,2,1,0:T(8,128)(2,1)S(1)} %get-tuple-element.20.refs_2_), channel_id=1, source_target_pairs={{0,4},{4,0},{8,12},{12,8},{16,20},{20,16},{24,28},{28,24},{1,5},{5... | collective-permute-start | bytes 589832 | tf_op jit(solution)/shard_map/ppermute | solution.py:32
  10.3 7.0 %collective-permute-start.7 = (bf16[4,32,768]{2,1,0:T(8,128)(2,1)S(1)}, bf16[4,32,768]{2,1,0:T(8,128)(2,1)S(1)}, u32[]{:S(2)}, u32[]{:S(2)}) collective-permute-start(bf16[4,32,768]{2,1,0:T(8,128)(2,1)S(1)} %get-tuple-element.25), channel_id=1, source_target_pairs={{0,2},{1,3},{2,0},{3,1},{4,6},{5,7},{6,4},{7,5},{8,10},{9,11},{10,... | collective-permute-start | bytes 589832 | tf_op jit(solution)/shard_map/ppermute | solution.py:32
  11.8 9.0 %collective-permute-start.4 = (bf16[4,32,768]{2,1,0:T(8,128)(2,1)S(1)}, bf16[4,32,768]{2,1,0:T(8,128)(2,1)S(1)}, u32[]{:S(2)}, u32[]{:S(2)}) collective-permute-start(bf16[4,32,768]{2,1,0:T(8,128)(2,1)S(1)} %get-tuple-element.23), channel_id=1, source_target_pairs={{0,4},{4,0},{8,12},{12,8},{16,20},{20,16},{24,28},{28,24},{1,5},{5... | collective-permute-start | bytes 589832 | tf_op jit(solution)/shard_map/ppermute | solution.py:32
  13.7 7.8 %collective-permute-start.5 = (bf16[4,32,768]{2,1,0:T(8,128)(2,1)S(1)}, bf16[4,32,768]{2,1,0:T(8,128)(2,1)S(1)}, u32[]{:S(2)}, u32[]{:S(2)}) collective-permute-start(bf16[4,32,768]{2,1,0:T(8,128)(2,1)S(1)} %get-tuple-element.24), channel_id=1, source_target_pairs={{0,2},{1,3},{2,0},{3,1},{4,6},{5,7},{6,4},{7,5},{8,10},{9,11},{10,... | collective-permute-start | bytes 589832 | tf_op jit(solution)/shard_map/ppermute | solution.py:32
  15.3 6.4 %collective-permute-start.2 = (bf16[2,2,32,768]{3,2,1,0:T(8,128)(2,1)S(1)}, bf16[2,2,32,768]{3,2,1,0:T(8,128)(2,1)S(1)}, u32[]{:S(2)}, u32[]{:S(2)}) collective-permute-start(bf16[2,2,32,768]{3,2,1,0:T(8,128)(2,1)S(1)} %widen.1.refs_4_), channel_id=1, source_target_pairs={{0,8},{4,12},{8,0},{12,4},{16,24},{20,28},{24,16},{28,20},{1,9},{5... | collective-permute-start | bytes 589832 | tf_op jit(solution)/shard_map/ppermute | solution.py:32
  17.5 7.3 %collective-permute-start.18 = (bf16[4,32,768]{2,1,0:T(8,128)(2,1)S(1)}, bf16[4,32,768]{2,1,0:T(8,128)(2,1)S(1)}, u32[]{:S(2)}, u32[]{:S(2)}) collective-permute-start(bf16[4,32,768]{2,1,0:T(8,128)(2,1)S(1)} %get-tuple-element.26.refs_4_), channel_id=1, source_target_pairs={{0,4},{4,0},{8,12},{12,8},{16,20},{20,16},{24,28},{28,24},{1,5},{5... | collective-permute-start | bytes 589832 | tf_op jit(solution)/shard_map/ppermute | solution.py:32
  18.3 7.8 %collective-permute-start.19 = (bf16[4,32,768]{2,1,0:T(8,128)(2,1)S(1)}, bf16[4,32,768]{2,1,0:T(8,128)(2,1)S(1)}, u32[]{:S(2)}, u32[]{:S(2)}) collective-permute-start(bf16[4,32,768]{2,1,0:T(8,128)(2,1)S(1)} %get-tuple-element.29), channel_id=1, source_target_pairs={{0,2},{1,3},{2,0},{3,1},{4,6},{5,7},{6,4},{7,5},{8,10},{9,11},{10,... | collective-permute-start | bytes 589832 | tf_op jit(solution)/shard_map/ppermute | solution.py:32
  21.8 8.3 %collective-permute-start.8 = (bf16[4,32,768]{2,1,0:T(8,128)(2,1)S(1)}, bf16[4,32,768]{2,1,0:T(8,128)(2,1)S(1)}, u32[]{:S(2)}, u32[]{:S(2)}) collective-permute-start(bf16[4,32,768]{2,1,0:T(8,128)(2,1)S(1)} %get-tuple-element.27.refs_0_.refs_3_), channel_id=1, source_target_pairs={{0,4},{4,0},{8,12},{12,8},{16,20},{20,16},{24,28},{28,24},{1,5},{5... | collective-permute-start | bytes 589832 | tf_op jit(solution)/shard_map/ppermute | solution.py:32
  22.9 15.3 %copy-start = (bf16[128,12288]{1,0:T(8,128)(2,1)S(1)}, bf16[128,12288]{1,0:T(8,128)(2,1)}, u32[]{:S(2)}) copy-start(bf16[128,12288]{1,0:T(8,128)(2,1)} %tokens.5) | copy-start | bytes 9437188
  22.9 7.6 %collective-permute-start.11 = (bf16[4,32,768]{2,1,0:T(8,128)(2,1)S(1)}, bf16[4,32,768]{2,1,0:T(8,128)(2,1)S(1)}, u32[]{:S(2)}, u32[]{:S(2)}) collective-permute-start(bf16[4,32,768]{2,1,0:T(8,128)(2,1)S(1)} %get-tuple-element.28.refs_1_), channel_id=1, source_target_pairs={{0,2},{1,3},{2,0},{3,1},{4,6},{5,7},{6,4},{7,5},{8,10},{9,11},{10,... | collective-permute-start | bytes 589832 | tf_op jit(solution)/shard_map/ppermute | solution.py:32
  26.2 5.8 %collective-permute-start.20 = (bf16[2,2,32,768]{3,2,1,0:T(8,128)(2,1)S(1)}, bf16[2,2,32,768]{3,2,1,0:T(8,128)(2,1)S(1)}, u32[]{:S(2)}, u32[]{:S(2)}) collective-permute-start(bf16[2,2,32,768]{3,2,1,0:T(8,128)(2,1)S(1)} %plane.2.refs_4_), channel_id=1, source_target_pairs={{0,8},{4,12},{8,0},{12,4},{16,24},{20,28},{24,16},{28,20},{1,9},{5... | collective-permute-start | bytes 589832 | tf_op jit(solution)/shard_map/ppermute | solution.py:32
  27.8 7.8 %collective-permute-start.10 = (bf16[4,32,768]{2,1,0:T(8,128)(2,1)S(1)}, bf16[4,32,768]{2,1,0:T(8,128)(2,1)S(1)}, u32[]{:S(2)}, u32[]{:S(2)}) collective-permute-start(bf16[4,32,768]{2,1,0:T(8,128)(2,1)S(1)} %get-tuple-element.27.refs_0_.refs_3_), channel_id=1, source_target_pairs={{0,2},{1,3},{2,0},{3,1},{4,6},{5,7},{6,4},{7,5},{8,10},{9,11},{10,... | collective-permute-start | bytes 589832 | tf_op jit(solution)/shard_map/ppermute | solution.py:32
  29.4 6.4 %collective-permute-start.9 = (bf16[4,32,768]{2,1,0:T(8,128)(2,1)S(1)}, bf16[4,32,768]{2,1,0:T(8,128)(2,1)S(1)}, u32[]{:S(2)}, u32[]{:S(2)}) collective-permute-start(bf16[4,32,768]{2,1,0:T(8,128)(2,1)S(1)} %get-tuple-element.28.refs_1_), channel_id=1, source_target_pairs={{0,4},{4,0},{8,12},{12,8},{16,20},{20,16},{24,28},{28,24},{1,5},{5... | collective-permute-start | bytes 589832 | tf_op jit(solution)/shard_map/ppermute | solution.py:32
  30.0 7.7 %collective-permute-start.12 = (bf16[4,32,768]{2,1,0:T(8,128)(2,1)S(1)}, bf16[4,32,768]{2,1,0:T(8,128)(2,1)S(1)}, u32[]{:S(2)}, u32[]{:S(2)}) collective-permute-start(bf16[4,32,768]{2,1,0:T(8,128)(2,1)S(1)} %collective-permute-done.8.refs_0_), channel_id=1, source_target_pairs={{0,2},{1,3},{2,0},{3,1},{4,6},{5,7},{6,4},{7,5},{8,10},{9,11},{10,... | collective-permute-start | bytes 589832 | tf_op jit(solution)/shard_map/ppermute | solution.py:32
  30.5 7.2 %collective-permute-start.13 = (bf16[4,32,768]{2,1,0:T(8,128)(2,1)S(1)}, bf16[4,32,768]{2,1,0:T(8,128)(2,1)S(1)}, u32[]{:S(2)}, u32[]{:S(2)}) collective-permute-start(bf16[4,32,768]{2,1,0:T(8,128)(2,1)S(1)} %collective-permute-done.11.refs_3_), channel_id=1, source_target_pairs={{0,4},{4,0},{8,12},{12,8},{16,20},{20,16},{24,28},{28,24},{1,5},{5... | collective-permute-start | bytes 589832 | tf_op jit(solution)/shard_map/ppermute | solution.py:32
  32.0 6.2 %collective-permute-start.21 = (bf16[1,2,32,768]{3,2,1,0:T(8,128)(2,1)S(1)}, bf16[1,2,32,768]{3,2,1,0:T(8,128)(2,1)S(1)}, u32[]{:S(2)}, u32[]{:S(2)}) collective-permute-start(bf16[1,2,32,768]{3,2,1,0:T(8,128)(2,1)S(1)} %plane.3), channel_id=1, source_target_pairs={{0,16},{4,20},{8,24},{12,28},{16,0},{20,4},{24,8},{28,12},{1,17},{... | collective-permute-start | bytes 294920 | tf_op jit(solution)/shard_map/ppermute | solution.py:32
  35.7 2.6 %collective-permute-start.17 = (bf16[4,4,32,768]{3,2,1,0:T(8,128)(2,1)S(1)}, bf16[4,4,32,768]{3,2,1,0:T(8,128)(2,1)S(1)}, u32[]{:S(2)}, u32[]{:S(2)}) collective-permute-start(bf16[4,4,32,768]{3,2,1,0:T(8,128)(2,1)S(1)} %near.1.refs_2_.refs_0_), channel_id=1, source_target_pairs={{0,1},{1,0},{2,3},{3,2},{4,5},{5,4},{6,7},{7,6},{8,9},{9,8},{10,11... | collective-permute-start | bytes 2359304 | tf_op jit(solution)/shard_map/ppermute | solution.py:32
  35.8 3.1 %collective-permute-start.14 = (bf16[2,4,32,768]{3,2,1,0:T(8,128)(2,1)S(1)}, bf16[2,4,32,768]{3,2,1,0:T(8,128)(2,1)S(1)}, u32[]{:S(2)}, u32[]{:S(2)}) collective-permute-start(bf16[2,4,32,768]{3,2,1,0:T(8,128)(2,1)S(1)} %side.1.refs_0_), channel_id=1, source_target_pairs={{0,1},{1,0},{2,3},{3,2},{4,5},{5,4},{6,7},{7,6},{8,9},{9,8},{10,11... | collective-permute-start | bytes 1179656 | tf_op jit(solution)/shard_map/ppermute | solution.py:32
  37.7 1.4 %collective-permute-start.15 = (bf16[4,32,768]{2,1,0:T(8,128)(2,1)S(1)}, bf16[4,32,768]{2,1,0:T(8,128)(2,1)S(1)}, u32[]{:S(2)}, u32[]{:S(2)}) collective-permute-start(bf16[4,32,768]{2,1,0:T(8,128)(2,1)S(1)} %collective-permute-done.12.refs_1_), channel_id=1, source_target_pairs={{0,1},{1,0},{2,3},{3,2},{4,5},{5,4},{6,7},{7,6},{8,9},{9,8},{10,11... | collective-permute-start | bytes 589832 | tf_op jit(solution)/shard_map/ppermute | solution.py:32
  37.8 1.7 %collective-permute-start.16 = (bf16[4,32,768]{2,1,0:T(8,128)(2,1)S(1)}, bf16[4,32,768]{2,1,0:T(8,128)(2,1)S(1)}, u32[]{:S(2)}, u32[]{:S(2)}) collective-permute-start(bf16[4,32,768]{2,1,0:T(8,128)(2,1)S(1)} %collective-permute-done.13.refs_2_), channel_id=1, source_target_pairs={{0,1},{1,0},{2,3},{3,2},{4,5},{5,4},{6,7},{7,6},{8,9},{9,8},{10,11... | collective-permute-start | bytes 589832 | tf_op jit(solution)/shard_map/ppermute | solution.py:32

commit v8 on v3

--- a/solution.py
+++ b/solution.py
@@ -212,8 +212,10 @@
         (*weights, out) = refs
         total = 0.0
     else:
-        (earlier, *weights, out, total_t) = refs
+        (earlier, grad, *weights, out, grad_out, total_t, sem) = refs
         total = earlier[...]
+        copy = pltpu.make_async_copy(grad, grad_out, sem)
+        copy.start()
     count = len(weights) // 2
     rows, half = weights[0].shape[2:]
     cols = 2 * half
@@ -238,9 +240,10 @@
     total_t[...] = total.reshape(total_t.shape)
     ordered = [total_t[lax.bitwise_xor(node, n)] for n in range(2 * ys)]
     out[...] = jnp.concatenate(ordered, axis=0).T.astype(BF16)
-
-
-def project(tokens, near, far, ys, zs):
+    copy.wait()
+
+
+def project(tokens, near, far, grad, ys, zs):
     rows = near[0].shape[2]
     count, width = tokens.shape[0], 2 * ys * rows
     cost = pl.CostEstimate(flops=tokens.size * width, bytes_accessed=2 * tokens.size, transcendentals=0)
@@ -255,17 +258,17 @@
     )(tokens, *near)
     return pl.pallas_call(
         functools.partial(project_kernel, ys, zs, 1),
-        out_shape=jax.ShapeDtypeStruct((count, width), BF16),
-        in_specs=[VMEM] * (2 + len(far)),
-        out_specs=VMEM,
-        scratch_shapes=[pltpu.VMEM((2 * ys, rows, count), F32)],
+        out_shape=(jax.ShapeDtypeStruct((count, width), BF16), jax.ShapeDtypeStruct(grad.shape, F32)),
+        in_specs=[VMEM] * (3 + len(far)),
+        out_specs=(VMEM, ANY),
+        scratch_shapes=[pltpu.VMEM((2 * ys, rows, count), F32), pltpu.SemaphoreType.DMA],
         compiler_params=PARAMS,
         cost_estimate=cost,
         name="project_far",
-    )(tokens, earlier, *far)
-
-
-def plain_project(tokens, near, far, ys, zs):
+    )(tokens, earlier, grad, *far)
+
+
+def plain_project(tokens, near, far, grad, ys, zs):
     rows, half = near[0].shape[2:]
     node, wide = lax.axis_index("node"), lax.axis_index("wide")
     pieces = tokens.reshape(tokens.shape[0], 2 * zs, 2, half)
@@ -284,7 +287,7 @@
                 part = part + jnp.einsum("tzl,zrl->tr", pieces[:, :, x, h], held, preferred_element_type=F32)
         total.append(part)
     total = jnp.take(jnp.stack(total, axis=1), jnp.arange(2 * ys) ^ node, axis=1)
-    return total.reshape(tokens.shape[0], -1).astype(BF16)
+    return total.reshape(tokens.shape[0], -1).astype(BF16), grad
 
 
 def on_device(wides, nodes, tokens, codes, scales, cotangent):
@@ -388,7 +391,7 @@
     ends = [d for ds in diag for d in ds]
     near = [near, core_flip(near)]
     far = [side, *ends, core_flip(side), *[core_flip(e) for e in ends]]
-    projected = make_project(tokens, near, far, ys, zs)
+    projected, weight_grad = make_project(tokens, near, far, weight_grad, ys, zs)
     return projected, weight_grad.T
 
 

time: 41.2 us -> 41.2 us (level)
  Pallas kernels: 6.63 us -> 6.07 us
  waiting for transfers between devices: 9.88 us -> 10.4 us
    pallas_call x1, Pallas kernels: 0.72 us -> 0.04 us  [finish(): pl.pallas_call(kernel, out_shape=jax.ShapeDtypeStruct((rows, 2 * half), F...]
    ppermute x22, waiting for transfers between devices: 9.88 us -> 10.4 us  [flip(): return lax.ppermute(entries, axis, [(i, i ^ offset) for i in range(size)])]
  transfers between devices with their start and end apart: 22 -> 22, of which waited for: 9 -> 11; matrix products, arithmetic and copies ran while one was open for 0% -> 0% of each run, Pallas kernels for 7% -> 5%
where the time goes in v8:
time: 41.2 us; the launch traced here: 41 us
  starting transfers between devices  23.8 us (58%)
  waiting for transfers between devices  10.4 us (25%)
  Pallas kernels  6.07 us (15%)
  between operations  0.77 us (2%)
    ppermute x22, starting transfers between devices, flip(): return lax.ppermute(entries, axis, [(i, i ^ offset) for i in range(size)])  23.8 us
    ppermute x22, waiting for transfers between devices, flip(): return lax.ppermute(entries, axis, [(i, i ^ offset) for i in range(size)])  10.4 us
    pallas_call x1, Pallas kernels, local_products(): pl.pallas_call(functools.partial(first_kernel, ys, zs), out_shape=(blocks...  2.6 us
    pallas_call x1, Pallas kernels, project(): pl.pallas_call(functools.partial(project_kernel, ys, zs, 1), out_shape=(j...  1.44 us
  transfers between devices with their start and end apart: 22, of which 11 were waited for; matrix products, arithmetic and copies ran while one was open for 0% of the time, Pallas kernels for 5%

profile of v8, /device:TPU:0, one launch (start us, length us, event | category | flops | bytes accessed | tf_op | source)
XLA Modules:
  0.0 41.0 jit_solution(9411816461854859133)
XLA Ops:
  0.7 2.6 %first.1 = (bf16[4,4,32,768]{3,2,1,0:T(8,128)(2,1)S(1)}, bf16[128,128]{1,0:T(8,128)(2,1)S(1)}, bf16[128,12288]{1,0:T(8,128)(2,1)S(1)}) custom-call(bf16[128,12288]{1,0:T(8,128)(2,1)} %tokens.5, bf16[128,128]{1,0:T(8,128)(2,1)} %cot.1), custom_call_target="tpu_custom_call" | custom-call | flops 201326592 | bytes 4718592 | tf_op jit(solution)/shard_map/first/pallas_call | solution.py:106
  3.3 0.5 %collective-permute-start.1 = (bf16[4,4,32,768]{3,2,1,0:T(8,128)(2,1)S(1)}, bf16[4,4,32,768]{3,2,1,0:T(8,128)(2,1)S(1)}, u32[]{:S(2)}, u32[]{:S(2)}) collective-permute-start(bf16[4,4,32,768]{3,2,1,0:T(8,128)(2,1)S(1)} %get-tuple-element.23), channel_id=1, source_target_pairs={{0,1},{1,0},{2,3},{3,2},{4,5},{5,4},{6,7},{7,6},{8,9},{9,8},{10,11... | collective-permute-start | bytes 2359304 | tf_op jit(solution)/shard_map/ppermute | solution.py:32
  3.8 0.8 %second.1 = (bf16[4,4,32,768]{3,2,1,0:T(8,128)(2,1)S(1)}, bf16[4,4,32,768]{3,2,1,0:T(8,128)(2,1)S(1)}, bf16[4,4,32,768]{3,2,1,0:T(8,128)(2,1)S(1)}, bf16[2,32,768]{2,1,0:T(8,128)(2,1)S(1)}) custom-call(bf16[128,12288]{1,0:T(8,128)(2,1)S(1)} %get-tuple-element.19.held, bf16[128,128]{1,0:T(8,128)(2,1)S(1)} %get-tuple-element.20.left, ...), custom_call_target="tpu_custom_call" | custom-call | flops 201326592 | bytes 4718592 | tf_op jit(solution)/shard_map/second/pallas_call | solution.py:120
  4.6 0.1 collective-permute-start.3
  4.7 4.0 %collective-permute-start = (bf16[2,32,768]{2,1,0:T(8,128)(2,1)S(1)}, bf16[2,32,768]{2,1,0:T(8,128)(2,1)S(1)}, u32[]{:S(2)}, u32[]{:S(2)}) collective-permute-start(bf16[2,32,768]{2,1,0:T(8,128)(2,1)S(1)} %get-tuple-element.21.refs_0_), channel_id=1, source_target_pairs={{0,16},{4,20},{8,24},{12,28},{16,0},{20,4},{24,8},{28,12},{1,17},{... | collective-permute-start | bytes 294920 | tf_op jit(solution)/shard_map/ppermute | solution.py:32
  8.7 0.2 stage1.1
  8.9 1.6 %collective-permute-start.7 = (bf16[4,32,768]{2,1,0:T(8,128)(2,1)S(1)}, bf16[4,32,768]{2,1,0:T(8,128)(2,1)S(1)}, u32[]{:S(2)}, u32[]{:S(2)}) collective-permute-start(bf16[4,32,768]{2,1,0:T(8,128)(2,1)S(1)} %get-tuple-element.29), channel_id=1, source_target_pairs={{0,2},{1,3},{2,0},{3,1},{4,6},{5,7},{6,4},{7,5},{8,10},{9,11},{10,... | collective-permute-start | bytes 589832 | tf_op jit(solution)/shard_map/ppermute | solution.py:32
  10.5 1.5 %collective-permute-start.6 = (bf16[1,4,32,768]{3,2,1,0:T(8,128)(2,1)S(1)}, bf16[1,4,32,768]{3,2,1,0:T(8,128)(2,1)S(1)}, u32[]{:S(2)}, u32[]{:S(2)}) collective-permute-start(bf16[1,4,32,768]{3,2,1,0:T(8,128)(2,1)S(1)} %get-tuple-element.24.refs_2_), channel_id=1, source_target_pairs={{0,4},{4,0},{8,12},{12,8},{16,20},{20,16},{24,28},{28,24},{1,5},{5... | collective-permute-start | bytes 589832 | tf_op jit(solution)/shard_map/ppermute | solution.py:32
  12.0 0.5 %collective-permute-start.4 = (bf16[4,32,768]{2,1,0:T(8,128)(2,1)S(1)}, bf16[4,32,768]{2,1,0:T(8,128)(2,1)S(1)}, u32[]{:S(2)}, u32[]{:S(2)}) collective-permute-start(bf16[4,32,768]{2,1,0:T(8,128)(2,1)S(1)} %get-tuple-element.27), channel_id=1, source_target_pairs={{0,2},{1,3},{2,0},{3,1},{4,6},{5,7},{6,4},{7,5},{8,10},{9,11},{10,... | collective-permute-start | bytes 589832 | tf_op jit(solution)/shard_map/ppermute | solution.py:32
  12.5 1.4 %collective-permute-done.refs_1_ = bf16[2,32,768]{2,1,0:T(8,128)(2,1)S(1)} collective-permute-done((bf16[2,32,768]{2,1,0:T(8,128)(2,1)S(1)}, bf16[2,32,768]{2,1,0:T(8,128)(2,1)S(1)}, u32[]{:S(2)}, u32[]{:S(2)}) %collective-permute-start) | collective-permute-done | bytes 98336 | tf_op jit(solution)/shard_map/ppermute | solution.py:32
  13.9 1.5 %collective-permute-start.5 = (bf16[4,32,768]{2,1,0:T(8,128)(2,1)S(1)}, bf16[4,32,768]{2,1,0:T(8,128)(2,1)S(1)}, u32[]{:S(2)}, u32[]{:S(2)}) collective-permute-start(bf16[4,32,768]{2,1,0:T(8,128)(2,1)S(1)} %get-tuple-element.28), channel_id=1, source_target_pairs={{0,4},{4,0},{8,12},{12,8},{16,20},{20,16},{24,28},{28,24},{1,5},{5... | collective-permute-start | bytes 589832 | tf_op jit(solution)/shard_map/ppermute | solution.py:32
  15.4 0.0 collective-permute-done.3.refs_1_
  15.4 0.7 %collective-permute-start.2 = (bf16[2,2,32,768]{3,2,1,0:T(8,128)(2,1)S(1)}, bf16[2,2,32,768]{3,2,1,0:T(8,128)(2,1)S(1)}, u32[]{:S(2)}, u32[]{:S(2)}) collective-permute-start(bf16[2,2,32,768]{3,2,1,0:T(8,128)(2,1)S(1)} %widen.1.refs_4_), channel_id=1, source_target_pairs={{0,8},{4,12},{8,0},{12,4},{16,24},{20,28},{24,16},{28,20},{1,9},{5... | collective-permute-start | bytes 589832 | tf_op jit(solution)/shard_map/ppermute | solution.py:32
  16.2 0.6 %collective-permute-done.7.refs_3_ = bf16[4,32,768]{2,1,0:T(8,128)(2,1)S(1)} collective-permute-done((bf16[4,32,768]{2,1,0:T(8,128)(2,1)S(1)}, bf16[4,32,768]{2,1,0:T(8,128)(2,1)S(1)}, u32[]{:S(2)}, u32[]{:S(2)}) %collective-permute-start.7) | collective-permute-done | bytes 196640 | tf_op jit(solution)/shard_map/ppermute | solution.py:32
  16.8 0.8 %collective-permute-done.6.refs_2_ = bf16[1,4,32,768]{3,2,1,0:T(8,128)(2,1)S(1)} collective-permute-done((bf16[1,4,32,768]{3,2,1,0:T(8,128)(2,1)S(1)}, bf16[1,4,32,768]{3,2,1,0:T(8,128)(2,1)S(1)}, u32[]{:S(2)}, u32[]{:S(2)}) %collective-permute-start.6) | collective-permute-done | bytes 196640 | tf_op jit(solution)/shard_map/ppermute | solution.py:32
  17.5 0.1 stage2.1
  17.7 0.8 %collective-permute-start.12 = (bf16[4,32,768]{2,1,0:T(8,128)(2,1)S(1)}, bf16[4,32,768]{2,1,0:T(8,128)(2,1)S(1)}, u32[]{:S(2)}, u32[]{:S(2)}) collective-permute-start(bf16[4,32,768]{2,1,0:T(8,128)(2,1)S(1)} %get-tuple-element.33), channel_id=1, source_target_pairs={{0,2},{1,3},{2,0},{3,1},{4,6},{5,7},{6,4},{7,5},{8,10},{9,11},{10,... | collective-permute-start | bytes 589832 | tf_op jit(solution)/shard_map/ppermute | solution.py:32
  18.5 1.5 %collective-permute-start.11 = (bf16[4,32,768]{2,1,0:T(8,128)(2,1)S(1)}, bf16[4,32,768]{2,1,0:T(8,128)(2,1)S(1)}, u32[]{:S(2)}, u32[]{:S(2)}) collective-permute-start(bf16[4,32,768]{2,1,0:T(8,128)(2,1)S(1)} %get-tuple-element.30.refs_4_), channel_id=1, source_target_pairs={{0,4},{4,0},{8,12},{12,8},{16,20},{20,16},{24,28},{28,24},{1,5},{5... | collective-permute-start | bytes 589832 | tf_op jit(solution)/shard_map/ppermute | solution.py:32
  20.0 1.0 %collective-permute-done.4.refs_2_ = bf16[4,32,768]{2,1,0:T(8,128)(2,1)S(1)} collective-permute-done((bf16[4,32,768]{2,1,0:T(8,128)(2,1)S(1)}, bf16[4,32,768]{2,1,0:T(8,128)(2,1)S(1)}, u32[]{:S(2)}, u32[]{:S(2)}) %collective-permute-start.4) | collective-permute-done | bytes 196640 | tf_op jit(solution)/shard_map/ppermute | solution.py:32
  21.0 0.8 %collective-permute-done.5.refs_3_ = bf16[4,32,768]{2,1,0:T(8,128)(2,1)S(1)} collective-permute-done((bf16[4,32,768]{2,1,0:T(8,128)(2,1)S(1)}, bf16[4,32,768]{2,1,0:T(8,128)(2,1)S(1)}, u32[]{:S(2)}, u32[]{:S(2)}) %collective-permute-start.5) | collective-permute-done | bytes 196640 | tf_op jit(solution)/shard_map/ppermute | solution.py:32
  21.8 0.1 sides.1.refs_3_.refs_0_
  21.9 0.0 collective-permute-done.2.refs_2_
  21.9 1.1 %collective-permute-start.9 = (bf16[4,32,768]{2,1,0:T(8,128)(2,1)S(1)}, bf16[4,32,768]{2,1,0:T(8,128)(2,1)S(1)}, u32[]{:S(2)}, u32[]{:S(2)}) collective-permute-start(bf16[4,32,768]{2,1,0:T(8,128)(2,1)S(1)} %get-tuple-element.32.refs_1_), channel_id=1, source_target_pairs={{0,2},{1,3},{2,0},{3,1},{4,6},{5,7},{6,4},{7,5},{8,10},{9,11},{10,... | collective-permute-start | bytes 589832 | tf_op jit(solution)/shard_map/ppermute | solution.py:32
  23.1 1.8 %collective-permute-start.15 = (bf16[4,32,768]{2,1,0:T(8,128)(2,1)S(1)}, bf16[4,32,768]{2,1,0:T(8,128)(2,1)S(1)}, u32[]{:S(2)}, u32[]{:S(2)}) collective-permute-start(bf16[4,32,768]{2,1,0:T(8,128)(2,1)S(1)} %get-tuple-element.31.refs_0_.refs_3_), channel_id=1, source_target_pairs={{0,4},{4,0},{8,12},{12,8},{16,20},{20,16},{24,28},{28,24},{1,5},{5... | collective-permute-start | bytes 589832 | tf_op jit(solution)/shard_map/ppermute | solution.py:32
  24.9 0.0 collective-permute-done.12.refs_2_
  24.9 1.5 %collective-permute-done.11.refs_1_ = bf16[4,32,768]{2,1,0:T(8,128)(2,1)S(1)} collective-permute-done((bf16[4,32,768]{2,1,0:T(8,128)(2,1)S(1)}, bf16[4,32,768]{2,1,0:T(8,128)(2,1)S(1)}, u32[]{:S(2)}, u32[]{:S(2)}) %collective-permute-start.11) | collective-permute-done | bytes 196640 | tf_op jit(solution)/shard_map/ppermute | solution.py:32
  26.4 1.7 %collective-permute-start.13 = (bf16[2,2,32,768]{3,2,1,0:T(8,128)(2,1)S(1)}, bf16[2,2,32,768]{3,2,1,0:T(8,128)(2,1)S(1)}, u32[]{:S(2)}, u32[]{:S(2)}) collective-permute-start(bf16[2,2,32,768]{3,2,1,0:T(8,128)(2,1)S(1)} %plane.2.refs_4_), channel_id=1, source_target_pairs={{0,8},{4,12},{8,0},{12,4},{16,24},{20,28},{24,16},{28,20},{1,9},{5... | collective-permute-start | bytes 589832 | tf_op jit(solution)/shard_map/ppermute | solution.py:32
  28.0 0.7 %collective-permute-start.8 = (bf16[4,32,768]{2,1,0:T(8,128)(2,1)S(1)}, bf16[4,32,768]{2,1,0:T(8,128)(2,1)S(1)}, u32[]{:S(2)}, u32[]{:S(2)}) collective-permute-start(bf16[4,32,768]{2,1,0:T(8,128)(2,1)S(1)} %get-tuple-element.31.refs_0_.refs_3_), channel_id=1, source_target_pairs={{0,2},{1,3},{2,0},{3,1},{4,6},{5,7},{6,4},{7,5},{8,10},{9,11},{10,... | collective-permute-start | bytes 589832 | tf_op jit(solution)/shard_map/ppermute | solution.py:32
  28.8 1.5 %collective-permute-start.16 = (bf16[4,32,768]{2,1,0:T(8,128)(2,1)S(1)}, bf16[4,32,768]{2,1,0:T(8,128)(2,1)S(1)}, u32[]{:S(2)}, u32[]{:S(2)}) collective-permute-start(bf16[4,32,768]{2,1,0:T(8,128)(2,1)S(1)} %get-tuple-element.32.refs_1_), channel_id=1, source_target_pairs={{0,4},{4,0},{8,12},{12,8},{16,20},{20,16},{24,28},{28,24},{1,5},{5... | collective-permute-start | bytes 589832 | tf_op jit(solution)/shard_map/ppermute | solution.py:32
  30.3 0.5 %collective-permute-start.18 = (bf16[4,32,768]{2,1,0:T(8,128)(2,1)S(1)}, bf16[4,32,768]{2,1,0:T(8,128)(2,1)S(1)}, u32[]{:S(2)}, u32[]{:S(2)}) collective-permute-start(bf16[4,32,768]{2,1,0:T(8,128)(2,1)S(1)} %collective-permute-done.9.refs_3_), channel_id=1, source_target_pairs={{0,4},{4,0},{8,12},{12,8},{16,20},{20,16},{24,28},{28,24},{1,5},{5... | collective-permute-start | bytes 589832 | tf_op jit(solution)/shard_map/ppermute | solution.py:32
  30.8 0.0 collective-permute-done.15.refs_0_
  30.8 1.6 %collective-permute-start.17 = (bf16[4,32,768]{2,1,0:T(8,128)(2,1)S(1)}, bf16[4,32,768]{2,1,0:T(8,128)(2,1)S(1)}, u32[]{:S(2)}, u32[]{:S(2)}) collective-permute-start(bf16[4,32,768]{2,1,0:T(8,128)(2,1)S(1)} %collective-permute-done.15.refs_0_), channel_id=1, source_target_pairs={{0,2},{1,3},{2,0},{3,1},{4,6},{5,7},{6,4},{7,5},{8,10},{9,11},{10,... | collective-permute-start | bytes 589832 | tf_op jit(solution)/shard_map/ppermute | solution.py:32
  32.4 0.0 collective-permute-done.13.refs_3_
  32.4 1.3 %collective-permute-start.14 = (bf16[1,2,32,768]{3,2,1,0:T(8,128)(2,1)S(1)}, bf16[1,2,32,768]{3,2,1,0:T(8,128)(2,1)S(1)}, u32[]{:S(2)}, u32[]{:S(2)}) collective-permute-start(bf16[1,2,32,768]{3,2,1,0:T(8,128)(2,1)S(1)} %plane.3), channel_id=1, source_target_pairs={{0,16},{4,20},{8,24},{12,28},{16,0},{20,4},{24,8},{28,12},{1,17},{... | collective-permute-start | bytes 294920 | tf_op jit(solution)/shard_map/ppermute | solution.py:32
  33.7 1.2 %collective-permute-done.8.refs_2_ = bf16[4,32,768]{2,1,0:T(8,128)(2,1)S(1)} collective-permute-done((bf16[4,32,768]{2,1,0:T(8,128)(2,1)S(1)}, bf16[4,32,768]{2,1,0:T(8,128)(2,1)S(1)}, u32[]{:S(2)}, u32[]{:S(2)}) %collective-permute-start.8) | collective-permute-done | bytes 196640 | tf_op jit(solution)/shard_map/ppermute | solution.py:32
  34.9 0.1 near.1.refs_0_.refs_2_
  35.0 0.1 collective-permute-start.10
  35.0 0.7 %collective-permute-done.16.refs_1_ = bf16[4,32,768]{2,1,0:T(8,128)(2,1)S(1)} collective-permute-done((bf16[4,32,768]{2,1,0:T(8,128)(2,1)S(1)}, bf16[4,32,768]{2,1,0:T(8,128)(2,1)S(1)}, u32[]{:S(2)}, u32[]{:S(2)}) %collective-permute-start.16) | collective-permute-done | bytes 196640 | tf_op jit(solution)/shard_map/ppermute | solution.py:32
  35.8 0.1 collective-permute-start.19
  35.9 2.0 %collective-permute-done.18.refs_4_ = bf16[4,32,768]{2,1,0:T(8,128)(2,1)S(1)} collective-permute-done((bf16[4,32,768]{2,1,0:T(8,128)(2,1)S(1)}, bf16[4,32,768]{2,1,0:T(8,128)(2,1)S(1)}, u32[]{:S(2)}, u32[]{:S(2)}) %collective-permute-start.18) | collective-permute-done | bytes 196640 | tf_op jit(solution)/shard_map/ppermute | solution.py:32
  37.9 0.0 collective-permute-start.21
  37.9 0.0 collective-permute-done.17.refs_3_
  37.9 0.5 %collective-permute-start.20 = (bf16[4,32,768]{2,1,0:T(8,128)(2,1)S(1)}, bf16[4,32,768]{2,1,0:T(8,128)(2,1)S(1)}, u32[]{:S(2)}, u32[]{:S(2)}) collective-permute-start(bf16[4,32,768]{2,1,0:T(8,128)(2,1)S(1)} %collective-permute-done.17.refs_3_), channel_id=1, source_target_pairs={{0,1},{1,0},{2,3},{3,2},{4,5},{5,4},{6,7},{7,6},{8,9},{9,8},{10,11... | collective-permute-start | bytes 589832 | tf_op jit(solution)/shard_map/ppermute | solution.py:32
  38.4 0.0 collective-permute-done.14.refs_4_
  38.5 0.6 %project_near.1.refs_0_ = f32[128,128]{1,0:T(8,128)S(1)} custom-call(bf16[128,12288]{1,0:T(8,128)(2,1)S(1)} %copy-done, bf16[4,4,32,768]{3,2,1,0:T(8,128)(2,1)S(1)} %near.1.refs_0_.refs_2_, bf16[4,4,32,768]{3,2,1,0:T(8,128)(2,1)S(1)} %collective-permute-done.10.refs_1_), custom_call_target="tpu_custom_call" | custom-call | flops 201326592 | bytes 3145728 | tf_op jit(solution)/shard_map/project_near/pallas_call | solution.py:250
  39.0 0.3 collective-permute-done.21.refs_7_
  39.3 0.3 collective-permute-done.20.refs_6_
  39.6 1.4 %project_far.1 = (bf16[128,128]{1,0:T(8,128)(2,1)}, f32[32,1536]{1,0:T(8,128)}) custom-call(bf16[128,12288]{1,0:T(8,128)(2,1)S(1)} %copy-done, f32[128,128]{1,0:T(8,128)S(1)} %project_near.1.refs_0_, f32[32,1536]{1,0:T(8,128)S(1)} %finish.1.refs_1_, bf16[2,4,32,768]{3,2,1,0:T(8,128)(2,1)S(1)} %side.1.refs_2_, ...), custom_call_target="tpu_custom_call" | custom-call | flops 201326592 | bytes 3145728 | tf_op jit(solution)/shard_map/project_far/pallas_call | solution.py:259
  (16 shorter events, 0.2 us)
Async XLA Ops:
  0.6 3.1 %copy-start.2 = (bf16[96,32]{0,1:T(8,128)(2,1)S(1)}, bf16[96,32]{0,1:T(8,128)(2,1)}, u32[]{:S(2)}) copy-start(bf16[96,32]{0,1:T(8,128)(2,1)} %param.6) | copy-start | bytes 18436
  0.6 3.1 %copy-start.1 = (bf16[1536,32]{0,1:T(8,128)(2,1)S(1)}, bf16[1536,32]{0,1:T(8,128)(2,1)}, u32[]{:S(2)}) copy-start(bf16[1536,32]{0,1:T(8,128)(2,1)} %param.5) | copy-start | bytes 294916
  3.3 5.5 %collective-permute-start.1 = (bf16[4,4,32,768]{3,2,1,0:T(8,128)(2,1)S(1)}, bf16[4,4,32,768]{3,2,1,0:T(8,128)(2,1)S(1)}, u32[]{:S(2)}, u32[]{:S(2)}) collective-permute-start(bf16[4,4,32,768]{3,2,1,0:T(8,128)(2,1)S(1)} %get-tuple-element.23), channel_id=1, source_target_pairs={{0,1},{1,0},{2,3},{3,2},{4,5},{5,4},{6,7},{7,6},{8,9},{9,8},{10,11... | collective-permute-start | bytes 2359304 | tf_op jit(solution)/shard_map/ppermute | solution.py:32
  4.6 10.9 %collective-permute-start.3 = (bf16[4,4,32,768]{3,2,1,0:T(8,128)(2,1)S(1)}, bf16[4,4,32,768]{3,2,1,0:T(8,128)(2,1)S(1)}, u32[]{:S(2)}, u32[]{:S(2)}) collective-permute-start(bf16[4,4,32,768]{3,2,1,0:T(8,128)(2,1)S(1)} %get-tuple-element.26), channel_id=1, source_target_pairs={{0,1},{1,0},{2,3},{3,2},{4,5},{5,4},{6,7},{7,6},{8,9},{9,8},{10,11... | collective-permute-start | bytes 2359304 | tf_op jit(solution)/shard_map/ppermute | solution.py:32
  4.7 9.2 %collective-permute-start = (bf16[2,32,768]{2,1,0:T(8,128)(2,1)S(1)}, bf16[2,32,768]{2,1,0:T(8,128)(2,1)S(1)}, u32[]{:S(2)}, u32[]{:S(2)}) collective-permute-start(bf16[2,32,768]{2,1,0:T(8,128)(2,1)S(1)} %get-tuple-element.21.refs_0_), channel_id=1, source_target_pairs={{0,16},{4,20},{8,24},{12,28},{16,0},{20,4},{24,8},{28,12},{1,17},{... | collective-permute-start | bytes 294920 | tf_op jit(solution)/shard_map/ppermute | solution.py:32
  8.9 7.9 %collective-permute-start.7 = (bf16[4,32,768]{2,1,0:T(8,128)(2,1)S(1)}, bf16[4,32,768]{2,1,0:T(8,128)(2,1)S(1)}, u32[]{:S(2)}, u32[]{:S(2)}) collective-permute-start(bf16[4,32,768]{2,1,0:T(8,128)(2,1)S(1)} %get-tuple-element.29), channel_id=1, source_target_pairs={{0,2},{1,3},{2,0},{3,1},{4,6},{5,7},{6,4},{7,5},{8,10},{9,11},{10,... | collective-permute-start | bytes 589832 | tf_op jit(solution)/shard_map/ppermute | solution.py:32
  10.5 7.1 %collective-permute-start.6 = (bf16[1,4,32,768]{3,2,1,0:T(8,128)(2,1)S(1)}, bf16[1,4,32,768]{3,2,1,0:T(8,128)(2,1)S(1)}, u32[]{:S(2)}, u32[]{:S(2)}) collective-permute-start(bf16[1,4,32,768]{3,2,1,0:T(8,128)(2,1)S(1)} %get-tuple-element.24.refs_2_), channel_id=1, source_target_pairs={{0,4},{4,0},{8,12},{12,8},{16,20},{20,16},{24,28},{28,24},{1,5},{5... | collective-permute-start | bytes 589832 | tf_op jit(solution)/shard_map/ppermute | solution.py:32
  12.0 9.0 %collective-permute-start.4 = (bf16[4,32,768]{2,1,0:T(8,128)(2,1)S(1)}, bf16[4,32,768]{2,1,0:T(8,128)(2,1)S(1)}, u32[]{:S(2)}, u32[]{:S(2)}) collective-permute-start(bf16[4,32,768]{2,1,0:T(8,128)(2,1)S(1)} %get-tuple-element.27), channel_id=1, source_target_pairs={{0,2},{1,3},{2,0},{3,1},{4,6},{5,7},{6,4},{7,5},{8,10},{9,11},{10,... | collective-permute-start | bytes 589832 | tf_op jit(solution)/shard_map/ppermute | solution.py:32
  13.9 7.9 %collective-permute-start.5 = (bf16[4,32,768]{2,1,0:T(8,128)(2,1)S(1)}, bf16[4,32,768]{2,1,0:T(8,128)(2,1)S(1)}, u32[]{:S(2)}, u32[]{:S(2)}) collective-permute-start(bf16[4,32,768]{2,1,0:T(8,128)(2,1)S(1)} %get-tuple-element.28), channel_id=1, source_target_pairs={{0,4},{4,0},{8,12},{12,8},{16,20},{20,16},{24,28},{28,24},{1,5},{5... | collective-permute-start | bytes 589832 | tf_op jit(solution)/shard_map/ppermute | solution.py:32
  15.4 6.5 %collective-permute-start.2 = (bf16[2,2,32,768]{3,2,1,0:T(8,128)(2,1)S(1)}, bf16[2,2,32,768]{3,2,1,0:T(8,128)(2,1)S(1)}, u32[]{:S(2)}, u32[]{:S(2)}) collective-permute-start(bf16[2,2,32,768]{3,2,1,0:T(8,128)(2,1)S(1)} %widen.1.refs_4_), channel_id=1, source_target_pairs={{0,8},{4,12},{8,0},{12,4},{16,24},{20,28},{24,16},{28,20},{1,9},{5... | collective-permute-start | bytes 589832 | tf_op jit(solution)/shard_map/ppermute | solution.py:32
  17.7 7.2 %collective-permute-start.12 = (bf16[4,32,768]{2,1,0:T(8,128)(2,1)S(1)}, bf16[4,32,768]{2,1,0:T(8,128)(2,1)S(1)}, u32[]{:S(2)}, u32[]{:S(2)}) collective-permute-start(bf16[4,32,768]{2,1,0:T(8,128)(2,1)S(1)} %get-tuple-element.33), channel_id=1, source_target_pairs={{0,2},{1,3},{2,0},{3,1},{4,6},{5,7},{6,4},{7,5},{8,10},{9,11},{10,... | collective-permute-start | bytes 589832 | tf_op jit(solution)/shard_map/ppermute | solution.py:32
  18.5 7.8 %collective-permute-start.11 = (bf16[4,32,768]{2,1,0:T(8,128)(2,1)S(1)}, bf16[4,32,768]{2,1,0:T(8,128)(2,1)S(1)}, u32[]{:S(2)}, u32[]{:S(2)}) collective-permute-start(bf16[4,32,768]{2,1,0:T(8,128)(2,1)S(1)} %get-tuple-element.30.refs_4_), channel_id=1, source_target_pairs={{0,4},{4,0},{8,12},{12,8},{16,20},{20,16},{24,28},{28,24},{1,5},{5... | collective-permute-start | bytes 589832 | tf_op jit(solution)/shard_map/ppermute | solution.py:32
  21.9 8.3 %collective-permute-start.9 = (bf16[4,32,768]{2,1,0:T(8,128)(2,1)S(1)}, bf16[4,32,768]{2,1,0:T(8,128)(2,1)S(1)}, u32[]{:S(2)}, u32[]{:S(2)}) collective-permute-start(bf16[4,32,768]{2,1,0:T(8,128)(2,1)S(1)} %get-tuple-element.32.refs_1_), channel_id=1, source_target_pairs={{0,2},{1,3},{2,0},{3,1},{4,6},{5,7},{6,4},{7,5},{8,10},{9,11},{10,... | collective-permute-start | bytes 589832 | tf_op jit(solution)/shard_map/ppermute | solution.py:32
  23.1 15.3 %copy-start = (bf16[128,12288]{1,0:T(8,128)(2,1)S(1)}, bf16[128,12288]{1,0:T(8,128)(2,1)}, u32[]{:S(2)}) copy-start(bf16[128,12288]{1,0:T(8,128)(2,1)} %tokens.5) | copy-start | bytes 9437188
  23.1 7.7 %collective-permute-start.15 = (bf16[4,32,768]{2,1,0:T(8,128)(2,1)S(1)}, bf16[4,32,768]{2,1,0:T(8,128)(2,1)S(1)}, u32[]{:S(2)}, u32[]{:S(2)}) collective-permute-start(bf16[4,32,768]{2,1,0:T(8,128)(2,1)S(1)} %get-tuple-element.31.refs_0_.refs_3_), channel_id=1, source_target_pairs={{0,4},{4,0},{8,12},{12,8},{16,20},{20,16},{24,28},{28,24},{1,5},{5... | collective-permute-start | bytes 589832 | tf_op jit(solution)/shard_map/ppermute | solution.py:32
  26.4 6.0 %collective-permute-start.13 = (bf16[2,2,32,768]{3,2,1,0:T(8,128)(2,1)S(1)}, bf16[2,2,32,768]{3,2,1,0:T(8,128)(2,1)S(1)}, u32[]{:S(2)}, u32[]{:S(2)}) collective-permute-start(bf16[2,2,32,768]{3,2,1,0:T(8,128)(2,1)S(1)} %plane.2.refs_4_), channel_id=1, source_target_pairs={{0,8},{4,12},{8,0},{12,4},{16,24},{20,28},{24,16},{28,20},{1,9},{5... | collective-permute-start | bytes 589832 | tf_op jit(solution)/shard_map/ppermute | solution.py:32
  28.0 6.9 %collective-permute-start.8 = (bf16[4,32,768]{2,1,0:T(8,128)(2,1)S(1)}, bf16[4,32,768]{2,1,0:T(8,128)(2,1)S(1)}, u32[]{:S(2)}, u32[]{:S(2)}) collective-permute-start(bf16[4,32,768]{2,1,0:T(8,128)(2,1)S(1)} %get-tuple-element.31.refs_0_.refs_3_), channel_id=1, source_target_pairs={{0,2},{1,3},{2,0},{3,1},{4,6},{5,7},{6,4},{7,5},{8,10},{9,11},{10,... | collective-permute-start | bytes 589832 | tf_op jit(solution)/shard_map/ppermute | solution.py:32
  28.8 7.0 %collective-permute-start.16 = (bf16[4,32,768]{2,1,0:T(8,128)(2,1)S(1)}, bf16[4,32,768]{2,1,0:T(8,128)(2,1)S(1)}, u32[]{:S(2)}, u32[]{:S(2)}) collective-permute-start(bf16[4,32,768]{2,1,0:T(8,128)(2,1)S(1)} %get-tuple-element.32.refs_1_), channel_id=1, source_target_pairs={{0,4},{4,0},{8,12},{12,8},{16,20},{20,16},{24,28},{28,24},{1,5},{5... | collective-permute-start | bytes 589832 | tf_op jit(solution)/shard_map/ppermute | solution.py:32
  30.3 7.6 %collective-permute-start.18 = (bf16[4,32,768]{2,1,0:T(8,128)(2,1)S(1)}, bf16[4,32,768]{2,1,0:T(8,128)(2,1)S(1)}, u32[]{:S(2)}, u32[]{:S(2)}) collective-permute-start(bf16[4,32,768]{2,1,0:T(8,128)(2,1)S(1)} %collective-permute-done.9.refs_3_), channel_id=1, source_target_pairs={{0,4},{4,0},{8,12},{12,8},{16,20},{20,16},{24,28},{28,24},{1,5},{5... | collective-permute-start | bytes 589832 | tf_op jit(solution)/shard_map/ppermute | solution.py:32
  30.8 7.1 %collective-permute-start.17 = (bf16[4,32,768]{2,1,0:T(8,128)(2,1)S(1)}, bf16[4,32,768]{2,1,0:T(8,128)(2,1)S(1)}, u32[]{:S(2)}, u32[]{:S(2)}) collective-permute-start(bf16[4,32,768]{2,1,0:T(8,128)(2,1)S(1)} %collective-permute-done.15.refs_0_), channel_id=1, source_target_pairs={{0,2},{1,3},{2,0},{3,1},{4,6},{5,7},{6,4},{7,5},{8,10},{9,11},{10,... | collective-permute-start | bytes 589832 | tf_op jit(solution)/shard_map/ppermute | solution.py:32
  32.4 6.0 %collective-permute-start.14 = (bf16[1,2,32,768]{3,2,1,0:T(8,128)(2,1)S(1)}, bf16[1,2,32,768]{3,2,1,0:T(8,128)(2,1)S(1)}, u32[]{:S(2)}, u32[]{:S(2)}) collective-permute-start(bf16[1,2,32,768]{3,2,1,0:T(8,128)(2,1)S(1)} %plane.3), channel_id=1, source_target_pairs={{0,16},{4,20},{8,24},{12,28},{16,0},{20,4},{24,8},{28,12},{1,17},{... | collective-permute-start | bytes 294920 | tf_op jit(solution)/shard_map/ppermute | solution.py:32
  35.0 3.5 %collective-permute-start.10 = (bf16[4,4,32,768]{3,2,1,0:T(8,128)(2,1)S(1)}, bf16[4,4,32,768]{3,2,1,0:T(8,128)(2,1)S(1)}, u32[]{:S(2)}, u32[]{:S(2)}) collective-permute-start(bf16[4,4,32,768]{3,2,1,0:T(8,128)(2,1)S(1)} %near.1.refs_0_.refs_2_), channel_id=1, source_target_pairs={{0,1},{1,0},{2,3},{3,2},{4,5},{5,4},{6,7},{7,6},{8,9},{9,8},{10,11... | collective-permute-start | bytes 2359304 | tf_op jit(solution)/shard_map/ppermute | solution.py:32
  35.8 3.8 %collective-permute-start.19 = (bf16[2,4,32,768]{3,2,1,0:T(8,128)(2,1)S(1)}, bf16[2,4,32,768]{3,2,1,0:T(8,128)(2,1)S(1)}, u32[]{:S(2)}, u32[]{:S(2)}) collective-permute-start(bf16[2,4,32,768]{3,2,1,0:T(8,128)(2,1)S(1)} %side.1.refs_2_), channel_id=1, source_target_pairs={{0,1},{1,0},{2,3},{3,2},{4,5},{5,4},{6,7},{7,6},{8,9},{9,8},{10,11... | collective-permute-start | bytes 1179656 | tf_op jit(solution)/shard_map/ppermute | solution.py:32
  37.9 1.4 %collective-permute-start.21 = (bf16[4,32,768]{2,1,0:T(8,128)(2,1)S(1)}, bf16[4,32,768]{2,1,0:T(8,128)(2,1)S(1)}, u32[]{:S(2)}, u32[]{:S(2)}) collective-permute-start(bf16[4,32,768]{2,1,0:T(8,128)(2,1)S(1)} %collective-permute-done.18.refs_4_), channel_id=1, source_target_pairs={{0,1},{1,0},{2,3},{3,2},{4,5},{5,4},{6,7},{7,6},{8,9},{9,8},{10,11... | collective-permute-start | bytes 589832 | tf_op jit(solution)/shard_map/ppermute | solution.py:32
  37.9 1.7 %collective-permute-start.20 = (bf16[4,32,768]{2,1,0:T(8,128)(2,1)S(1)}, bf16[4,32,768]{2,1,0:T(8,128)(2,1)S(1)}, u32[]{:S(2)}, u32[]{:S(2)}) collective-permute-start(bf16[4,32,768]{2,1,0:T(8,128)(2,1)S(1)} %collective-permute-done.17.refs_3_), channel_id=1, source_target_pairs={{0,1},{1,0},{2,3},{3,2},{4,5},{5,4},{6,7},{7,6},{8,9},{9,8},{10,11... | collective-permute-start | bytes 589832 | tf_op jit(solution)/shard_map/ppermute | solution.py:32
